TPU v7x, 32 devices: a whole 2x2x4 slice. The times are simulated.
32 devices in a mesh: groups: 2 (over y), expert: 4 (over z), seq: 2 (over x), replica: 2 (over core).
Axes of the slice: x: 2, y: 2, z: 4, core: 2. Of those that a mesh axis runs over, the one named last changes fastest.
Arguments:
- tokens: bfloat16 [1024, 1024], P(('groups', 'expert', 'seq', 'replica')), parts along dimension 0, may hold values from -6 to 6
- cotangent: bfloat16 [1024, 1024], P(('groups', 'expert', 'seq', 'replica')), parts along dimension 0, may hold values from -6 to 6
- expert_ids: int32 [1024, 8], P(('groups', 'expert', 'seq', 'replica')), parts along dimension 0, may hold values from 0 to 7, as said below
- combine_int: int32 [1024, 8], P(('groups', 'expert', 'seq', 'replica')), parts along dimension 0, may hold values from 1 to 1023
- w_gate: bfloat16 [8, 1024, 384], P(('expert', 'seq')), may hold values from -0.1875 to 0.1875
- w_up: bfloat16 [8, 1024, 384], P(('expert', 'seq')), may hold values from -0.1875 to 0.1875
- w_down: bfloat16 [8, 384, 1024], P(('expert', 'seq')), may hold values from -0.3125 to 0.3125
Outputs:
- token_grad: bfloat16 [1024, 1024], P(('groups', 'expert', 'seq', 'replica')), parts along dimension 0
- combine_grad: float32 [1024, 8], P(('groups', 'expert', 'seq', 'replica')), parts along dimension 0
- grad_gate: float32 [16, 1024, 384], P(('groups', 'expert', 'seq'), 'replica'), parts along dimension 0
- grad_up: float32 [16, 1024, 384], P(('groups', 'expert', 'seq'), 'replica'), parts along dimension 0
There are 2 independent parts, one for each index of `groups`. A program takes and returns all parts, laid end to end along the dimension named above; an argument that names none is the same for every part. Nothing has to cross between parts.
Inputs may be any that keep to these rules, and one draw needn't show every extreme that they name: `expert_ids`: each row names 8 different experts. The rows of one device name each expert at most 32 times, and some experts are named exactly 32 times by the rows of every device.
All inputs are finite; a program needn't handle non-finite values.
Results may differ from a plain program's by a relative error of at most 0.0065.
Values may be sent and summed in bfloat16 or wider, within the bound.
No kernel may reach another device: no remote copies, remote signals or barrier semaphores. Data moves between devices by JAX's collectives and lax.ppermute only.
A program may use at most 64 MiB of HBM per device.

v0:
```python
import jax
import jax.numpy as jnp
from jax import lax
from jax.sharding import PartitionSpec as P


def from_partner(block, axis, distance):
    count = lax.axis_size(axis)
    route = []
    for low in range(count):
        high = low | 1 << distance
        if high != low and high < count:
            route += [(low, high), (high, low)]
    return lax.ppermute(block, axis, route)


def expert_pass(x_rows, y_rows, mix_rows, gate_w, up_w, down_w):
    pre_gate = jnp.dot(x_rows, gate_w, preferred_element_type=jnp.float32)
    pre_up = jnp.dot(x_rows, up_w, preferred_element_type=jnp.float32)
    back_hidden = lax.dot_general(
        y_rows, down_w, (((1,), (1,)), ((), ())), preferred_element_type=jnp.float32
    )
    sigmoid_gate = jax.nn.sigmoid(pre_gate)
    activated = pre_gate * sigmoid_gate
    hidden = activated * pre_up
    pair_comb = jnp.sum(back_hidden * hidden, axis=1).astype(jnp.bfloat16)
    scaled = mix_rows.astype(jnp.float32)[:, None] * back_hidden
    d_gate = (scaled * pre_up * sigmoid_gate * (1.0 + pre_gate * (1.0 - sigmoid_gate))).astype(
        jnp.bfloat16
    )
    d_up = (scaled * activated).astype(jnp.bfloat16)
    token_part = lax.dot_general(
        d_gate, gate_w, (((1,), (1,)), ((), ())), preferred_element_type=jnp.float32
    )
    token_part = token_part + lax.dot_general(
        d_up, up_w, (((1,), (1,)), ((), ())), preferred_element_type=jnp.float32
    )
    return (d_gate, d_up, token_part.astype(jnp.bfloat16), pair_comb)


def body(tokens, cotangent, expert_ids, combine_int, w_gate, w_up, w_down):
    peer_count = lax.axis_size(("expert", "seq"))
    count_tok, feature_dim = tokens.shape
    top_k = expert_ids.shape[1]
    hidden_w = w_gate.shape[2]
    capacity = min(count_tok, max(top_k, 4 * count_tok * top_k // peer_count))
    slots_all = peer_count * capacity
    weights_f = combine_int.astype(jnp.float32)
    mix_weights = (weights_f / jnp.sum(weights_f, axis=1, keepdims=True)).astype(jnp.bfloat16)
    member = (
        expert_ids[:, :, None] == jnp.arange(peer_count, dtype=jnp.int32)[None, None, :]
    ).astype(jnp.int32)
    per_token = jnp.sum(member, axis=1)
    earlier = jnp.cumsum(per_token, axis=0) - per_token
    rank_in = jnp.sum(earlier[:, None, :] * member, axis=2)
    slot_ids = expert_ids * capacity + rank_in
    routing = (
        slot_ids[:, :, None] == jnp.arange(slots_all, dtype=jnp.int32)[None, None, :]
    ).astype(jnp.float32)
    placing = jnp.sum(routing, axis=1).astype(jnp.bfloat16)
    sent_x = lax.dot_general(
        placing, tokens, (((0,), (0,)), ((), ())), preferred_element_type=jnp.float32
    )
    sent_x = sent_x.astype(jnp.bfloat16).reshape(peer_count, capacity, feature_dim)
    sent_y = lax.dot_general(
        placing, cotangent, (((0,), (0,)), ((), ())), preferred_element_type=jnp.float32
    )
    sent_y = sent_y.astype(jnp.bfloat16).reshape(peer_count, capacity, feature_dim)
    sent_g = jnp.einsum("tks,tk->s", routing, mix_weights.astype(jnp.float32))
    sent_g = sent_g.astype(jnp.bfloat16).reshape(peer_count, capacity)
    got_x, got_y, got_g = (
        lax.all_to_all(sent_x, ("expert", "seq"), split_axis=0, concat_axis=0, tiled=True),
        lax.all_to_all(sent_y, ("expert", "seq"), split_axis=0, concat_axis=0, tiled=True),
        lax.all_to_all(sent_g, ("expert", "seq"), split_axis=0, concat_axis=0, tiled=True),
    )
    x_rows = got_x.reshape(slots_all, feature_dim)
    y_rows = got_y.reshape(slots_all, feature_dim)
    mix_rows = got_g.reshape(slots_all)
    d_gate, d_up, token_part, pair_comb = expert_pass(
        x_rows, y_rows, mix_rows, w_gate[0], w_up[0], w_down[0]
    )
    ret_x, ret_c = (
        lax.all_to_all(
            token_part.reshape(peer_count, capacity, feature_dim),
            ("expert", "seq"),
            split_axis=0,
            concat_axis=0,
            tiled=True,
        ),
        lax.all_to_all(
            pair_comb.reshape(peer_count, capacity),
            ("expert", "seq"),
            split_axis=0,
            concat_axis=0,
            tiled=True,
        ),
    )
    d_both = jnp.concatenate([d_gate, d_up], axis=1)
    half_rows = feature_dim // lax.axis_size("replica")
    other_x, other_d = from_partner((x_rows, d_both), "replica", 0)
    first_row = lax.axis_index("replica") * half_rows
    own_cols = lax.dynamic_slice_in_dim(x_rows, first_row, half_rows, 1)
    other_cols = lax.dynamic_slice_in_dim(other_x, first_row, half_rows, 1)
    grad_rows = lax.dot_general(
        own_cols, d_both, (((0,), (0,)), ((), ())), preferred_element_type=jnp.float32
    )
    grad_rows = grad_rows + lax.dot_general(
        other_cols, other_d, (((0,), (0,)), ((), ())), preferred_element_type=jnp.float32
    )
    grad_gate = grad_rows[:, :hidden_w][None]
    grad_up = grad_rows[:, hidden_w:][None]
    token_grad = jnp.dot(
        placing, ret_x.reshape(slots_all, feature_dim), preferred_element_type=jnp.float32
    )
    combine_grad = jnp.einsum("tks,s->tk", routing, ret_c.reshape(slots_all).astype(jnp.float32))
    return (token_grad.astype(jnp.bfloat16), combine_grad, grad_gate, grad_up)


def solution(mesh):
    in_specs = (
        P(("groups", "expert", "seq", "replica"), None),
        P(("groups", "expert", "seq", "replica"), None),
        P(("groups", "expert", "seq", "replica"), None),
        P(("groups", "expert", "seq", "replica"), None),
        P(("expert", "seq"), None, None),
        P(("expert", "seq"), None, None),
        P(("expert", "seq"), None, None),
    )
    out_specs = (
        P(("groups", "expert", "seq", "replica"), None),
        P(("groups", "expert", "seq", "replica"), None),
        P(("groups", "expert", "seq"), "replica", None),
        P(("groups", "expert", "seq"), "replica", None),
    )
    return jax.shard_map(body, mesh=mesh, in_specs=in_specs, out_specs=out_specs, check_vma=False)
```

profile of v0, /device:TPU:0, one launch (start us, length us, event | category | flops | bytes accessed | tf_op | source)
XLA Modules:
  0.0 85.6 jit_solution(2114080563941359245)
XLA Ops:
  0.7 0.8 convert_reduce_fusion.1
  1.7 0.7 select_reduce_fusion
  2.4 0.7 multiply_add_fusion
  3.1 0.7 convert_reduce_fusion.3
  3.9 0.7 fusion.18
  4.9 0.7 all_to_all.25
  5.6 7.3 %all-to-all-start = ((bf16[8,1,32]{2,1,0:T(2,128)(2,1)}), bf16[8,1,32]{2,1,0:T(2,128)(2,1)S(1)}, u32[]{:S(2)}, u32[]{:S(2)}) async-start(bf16[8,1,32]{2,1,0:T(2,128)(2,1)} %all_to_all.25), calls=%async_computation | async-start | bytes 8192 | tf_op jit(solution)/shard_map/all_to_all | solution.py:74
  13.0 2.0 %convolution_convert_fusion = bf16[256,1024]{1,0:T(8,128)(2,1)} fusion(bf16[32,1024]{1,0:T(8,128)(2,1)} %param.7, bf16[32,256]{1,0:T(8,128)(2,1)S(1)} %convert_reduce_fusion), kind=kOutput, calls=%fused_computation.3 | convolution fusion | flops 17039360 | bytes 606208 | tf_op jit(solution)/shard_map/dot_general | solution.py:61
  15.0 4.2 %all-to-all-done = bf16[8,1,32]{2,1,0:T(2,128)(2,1)S(1)} async-done(((bf16[8,1,32]{2,1,0:T(2,128)(2,1)}), bf16[8,1,32]{2,1,0:T(2,128)(2,1)S(1)}, u32[]{:S(2)}, u32[]{:S(2)}) %all-to-all-start) | async-done | bytes 544 | tf_op jit(solution)/shard_map/all_to_all | solution.py:74
  19.2 3.5 %all-to-all-start.2 = ((bf16[8,32,1024]{2,1,0:T(8,128)(2,1)}), bf16[8,32,1024]{2,1,0:T(8,128)(2,1)S(1)}, u32[]{:S(2)}, u32[]{:S(2)}) async-start(bf16[8,32,1024]{2,1,0:T(8,128)(2,1)} %bitcast.5), calls=%async_computation.2 | async-start | bytes 1048576 | tf_op jit(solution)/shard_map/all_to_all | solution.py:72
  22.7 1.1 %convolution_convert_fusion.1 = bf16[256,1024]{1,0:T(8,128)(2,1)} fusion(bf16[32,1024]{1,0:T(8,128)(2,1)S(1)} %copy-done.4, bf16[32,256]{1,0:T(8,128)(2,1)S(1)} %convert_reduce_fusion), kind=kOutput, calls=%fused_computation.4 | convolution fusion | flops 17039360 | bytes 606208 | tf_op jit(solution)/shard_map/dot_general | solution.py:65
  23.8 12.1 %all-to-all-done.2 = bf16[8,32,1024]{2,1,0:T(8,128)(2,1)S(1)} async-done(((bf16[8,32,1024]{2,1,0:T(8,128)(2,1)}), bf16[8,32,1024]{2,1,0:T(8,128)(2,1)S(1)}, u32[]{:S(2)}, u32[]{:S(2)}) %all-to-all-start.2) | async-done | bytes 524320 | tf_op jit(solution)/shard_map/all_to_all | solution.py:72
  36.0 3.7 %all-to-all-start.1 = ((bf16[8,32,1024]{2,1,0:T(8,128)(2,1)}), bf16[8,32,1024]{2,1,0:T(8,128)(2,1)S(1)}, u32[]{:S(2)}, u32[]{:S(2)}) async-start(bf16[8,32,1024]{2,1,0:T(8,128)(2,1)} %bitcast.2), calls=%async_computation.1 | async-start | bytes 1048576 | tf_op jit(solution)/shard_map/all_to_all | solution.py:73
  39.8 0.4 fusion.6
  40.2 1.2 %fusion.3 = f32[256,384]{1,0:T(8,128)} fusion(bf16[256,1024]{1,0:T(8,128)(2,1)S(1)} %bitcast.45, bf16[1,1024,384]{2,1,0:T(8,128)(2,1)S(1)} %copy-done), kind=kOutput, calls=%fused_computation.10 | convolution fusion | flops 201326592 | bytes 1703936 | tf_op jit(solution)/shard_map/dot_general | solution.py:18
  41.4 12.1 %all-to-all-done.1 = bf16[8,32,1024]{2,1,0:T(8,128)(2,1)S(1)} async-done(((bf16[8,32,1024]{2,1,0:T(8,128)(2,1)}), bf16[8,32,1024]{2,1,0:T(8,128)(2,1)S(1)}, u32[]{:S(2)}, u32[]{:S(2)}) %all-to-all-start.1) | async-done | bytes 524320 | tf_op jit(solution)/shard_map/all_to_all | solution.py:73
  53.5 2.5 %multiply_reduce_fusion = (bf16[256]{0:T(256)(128)(2,1)}, bf16[256,384]{1,0:T(8,128)(2,1)S(1)}, bf16[256,384]{1,0:T(8,128)(2,1)S(1)}) fusion(f32[256,384]{1,0:T(8,128)S(1)} %fusion.6, f32[256,384]{1,0:T(8,128)} %fusion.3, f32[256]{0:T(256)S(1)} %reshape.77, bf16[256,1024]{1,0:T(8,128)(2,1)S(1)} %bitcast.49, bf16[1,384,1024]{2,1,0:T(8,128)(2,1)} %param.13), kind=kOutput, calls=%fused_computation.18 | convolution fusion | flops 202997504 | bytes 2491904 | tf_op jit(solution)/shard_map/dot_general | solution.py:20
  55.9 0.5 fusion.1
  56.4 1.4 %convert_element_type.79 = bf16[8,1,32]{2,1,0:T(2,128)(2,1)} reshape(bf16[256]{0:T(256)(128)(2,1)} %get-tuple-element.6) | data formatting | bytes 1024 | tf_op jit(solution)/shard_map/convert_element_type | solution.py:26
  57.8 3.8 %all-to-all-start.4 = ((bf16[8,1,32]{2,1,0:T(2,128)(2,1)}), bf16[8,1,32]{2,1,0:T(2,128)(2,1)}, u32[]{:S(2)}, u32[]{:S(2)}) async-start(bf16[8,1,32]{2,1,0:T(2,128)(2,1)} %convert_element_type.79), calls=%async_computation.4 | async-start | bytes 8192 | tf_op jit(solution)/shard_map/all_to_all | solution.py:90
  61.6 0.8 pad_maximum_fusion
  62.4 1.3 %fusion = bf16[256,1024]{1,0:T(8,128)(2,1)} fusion(f32[256,1024]{1,0:T(8,128)S(1)} %fusion.1, bf16[256,384]{1,0:T(8,128)(2,1)S(1)} %get-tuple-element.8, bf16[1,1024,384]{2,1,0:T(8,128)(2,1)S(1)} %copy-done.1), kind=kOutput, calls=%fused_computation.2 | convolution fusion | flops 201850880 | bytes 2555904 | tf_op jit(solution)/shard_map/dot_general | solution.py:35
  63.7 4.2 %all-to-all-done.4 = bf16[8,1,32]{2,1,0:T(2,128)(2,1)} async-done(((bf16[8,1,32]{2,1,0:T(2,128)(2,1)}), bf16[8,1,32]{2,1,0:T(2,128)(2,1)}, u32[]{:S(2)}, u32[]{:S(2)}) %all-to-all-start.4) | async-done | bytes 544 | tf_op jit(solution)/shard_map/all_to_all | solution.py:90
  67.8 3.6 %all-to-all-start.3 = ((bf16[8,32,1024]{2,1,0:T(8,128)(2,1)}), bf16[8,32,1024]{2,1,0:T(8,128)(2,1)S(1)}, u32[]{:S(2)}, u32[]{:S(2)}) async-start(bf16[8,32,1024]{2,1,0:T(8,128)(2,1)} %bitcast.47), calls=%async_computation.3 | async-start | bytes 1048576 | tf_op jit(solution)/shard_map/all_to_all | solution.py:83
  71.5 1.4 %fusion.12 = f32[512,768]{1,0:T(8,128)S(1)} fusion(bf16[256,1024]{1,0:T(8,128)(2,1)S(1)} %bitcast.46, s32[]{:T(128)S(6)} %select_n.4, bf16[256,384]{1,0:T(8,128)(2,1)} %copy-done.2, bf16[256,384]{1,0:T(8,128)(2,1)} %copy-done.3), kind=kOutput, calls=%fused_computation.24 | convolution fusion | flops 202113024 | bytes 2228228 | tf_op jit(solution)/shard_map/dot_general | solution.py:104
  72.9 0.7 reduce.1
  73.7 0.5 fusion.14
  74.2 0.7 copy.26
  74.9 1.5 %convolution_add_fusion = f32[512,768]{1,0:T(8,128)S(1)} fusion(f32[512,768]{1,0:T(8,128)S(1)} %fusion.12, bf16[256,768]{1,0:T(8,128)(2,1)} %collective-permute-done.1, bf16[256,1024]{1,0:T(8,128)(2,1)} %collective-permute-done, s32[]{:T(128)S(6)} %select_n.4), kind=kOutput, calls=%fused_computation | convolution fusion | flops 201719808 | bytes 3801092 | tf_op jit(solution)/shard_map/dot_general | solution.py:107
  76.3 1.2 %slice_bitcast_fusion = (f32[1,512,384]{2,1,0:T(8,128)}, f32[1,512,384]{2,1,0:T(8,128)}) fusion(f32[512,768]{1,0:T(8,128)S(1)} %convolution_add_fusion), kind=kLoop, calls=%fused_computation.6 | loop fusion | bytes 3145728 | tf_op jit(solution)/shard_map/broadcast_in_dim | solution.py:111
  77.6 7.2 %all-to-all-done.3 = bf16[8,32,1024]{2,1,0:T(8,128)(2,1)S(1)} async-done(((bf16[8,32,1024]{2,1,0:T(8,128)(2,1)}), bf16[8,32,1024]{2,1,0:T(8,128)(2,1)S(1)}, u32[]{:S(2)}, u32[]{:S(2)}) %all-to-all-start.3) | async-done | bytes 524320 | tf_op jit(solution)/shard_map/all_to_all | solution.py:83
  84.8 0.8 convolution_convert_fusion.2
  (30 shorter events, 1.0 us)
Async XLA Ops:
  0.6 39.6 %copy-start = (bf16[1,1024,384]{2,1,0:T(8,128)(2,1)S(1)}, bf16[1,1024,384]{2,1,0:T(8,128)(2,1)}, u32[]{:S(2)}) copy-start(bf16[1,1024,384]{2,1,0:T(8,128)(2,1)} %param.11) | copy-start | bytes 2359300
  0.6 22.1 %copy-start.4 = (bf16[32,1024]{1,0:T(8,128)(2,1)S(1)}, bf16[32,1024]{1,0:T(8,128)(2,1)}, u32[]{:S(2)}) copy-start(bf16[32,1024]{1,0:T(8,128)(2,1)} %param.8) | copy-start | bytes 196612
  3.1 16.1 %copy-start.5 = (s32[32,8]{1,0:T(8,128)}, s32[32,8]{1,0:T(8,128)S(1)}, u32[]{:S(2)}) copy-start(s32[32,8]{1,0:T(8,128)S(1)} %copy.22) | copy-start | bytes 3076
  5.6 13.6 %all-to-all-start = ((bf16[8,1,32]{2,1,0:T(2,128)(2,1)}), bf16[8,1,32]{2,1,0:T(2,128)(2,1)S(1)}, u32[]{:S(2)}, u32[]{:S(2)}) async-start(bf16[8,1,32]{2,1,0:T(2,128)(2,1)} %all_to_all.25), calls=%async_computation | async-start | bytes 8192 | tf_op jit(solution)/shard_map/all_to_all | solution.py:74
  13.0 26.8 %copy-start.1 = (bf16[1,1024,384]{2,1,0:T(8,128)(2,1)S(1)}, bf16[1,1024,384]{2,1,0:T(8,128)(2,1)}, u32[]{:S(2)}) copy-start(bf16[1,1024,384]{2,1,0:T(8,128)(2,1)} %param.12) | copy-start | bytes 2359300
  19.2 16.8 %all-to-all-start.2 = ((bf16[8,32,1024]{2,1,0:T(8,128)(2,1)}), bf16[8,32,1024]{2,1,0:T(8,128)(2,1)S(1)}, u32[]{:S(2)}, u32[]{:S(2)}) async-start(bf16[8,32,1024]{2,1,0:T(8,128)(2,1)} %bitcast.5), calls=%async_computation.2 | async-start | bytes 1048576 | tf_op jit(solution)/shard_map/all_to_all | solution.py:72
  36.0 17.5 %all-to-all-start.1 = ((bf16[8,32,1024]{2,1,0:T(8,128)(2,1)}), bf16[8,32,1024]{2,1,0:T(8,128)(2,1)S(1)}, u32[]{:S(2)}, u32[]{:S(2)}) async-start(bf16[8,32,1024]{2,1,0:T(8,128)(2,1)} %bitcast.2), calls=%async_computation.1 | async-start | bytes 1048576 | tf_op jit(solution)/shard_map/all_to_all | solution.py:73
  39.7 35.1 %collective-permute-start = (bf16[256,1024]{1,0:T(8,128)(2,1)S(1)}, bf16[256,1024]{1,0:T(8,128)(2,1)}, u32[]{:S(2)}, u32[]{:S(2)}) collective-permute-start(bf16[256,1024]{1,0:T(8,128)(2,1)S(1)} %bitcast.43), channel_id=1, source_target_pairs={{0,1},{1,0},{2,3},{3,2},{4,5},{5,4},{6,7},{7,6},{8,9},{9,8},{10,11... | collective-permute-start | bytes 1572872 | tf_op jit(solution)/shard_map/ppermute | solution.py:14
  55.9 7.7 %copy-start.2 = (bf16[256,384]{1,0:T(8,128)(2,1)}, bf16[256,384]{1,0:T(8,128)(2,1)S(1)}, u32[]{:S(2)}) copy-start(bf16[256,384]{1,0:T(8,128)(2,1)S(1)} %get-tuple-element.8) | copy-start | bytes 589828
  55.9 7.7 %copy-start.3 = (bf16[256,384]{1,0:T(8,128)(2,1)}, bf16[256,384]{1,0:T(8,128)(2,1)S(1)}, u32[]{:S(2)}) copy-start(bf16[256,384]{1,0:T(8,128)(2,1)S(1)} %get-tuple-element.7) | copy-start | bytes 589828
  57.8 10.1 %all-to-all-start.4 = ((bf16[8,1,32]{2,1,0:T(2,128)(2,1)}), bf16[8,1,32]{2,1,0:T(2,128)(2,1)}, u32[]{:S(2)}, u32[]{:S(2)}) async-start(bf16[8,1,32]{2,1,0:T(2,128)(2,1)} %convert_element_type.79), calls=%async_computation.4 | async-start | bytes 8192 | tf_op jit(solution)/shard_map/all_to_all | solution.py:90
  62.4 12.5 %collective-permute-start.1 = (bf16[256,768]{1,0:T(8,128)(2,1)}, bf16[256,768]{1,0:T(8,128)(2,1)}, u32[]{:S(2)}, u32[]{:S(2)}) collective-permute-start(bf16[256,768]{1,0:T(8,128)(2,1)} %pad_maximum_fusion), channel_id=1, source_target_pairs={{0,1},{1,0},{2,3},{3,2},{4,5},{5,4},{6,7},{7,6},{8,9},{9,8},{10,11... | collective-permute-start | bytes 1179656 | tf_op jit(solution)/shard_map/ppermute | solution.py:14
  67.8 5.9 %copy-start.6 = (s32[32,8]{1,0:T(8,128)S(1)}, s32[32,8]{1,0:T(8,128)}, u32[]{:S(2)}) copy-start(s32[32,8]{1,0:T(8,128)} %copy-done.5) | copy-start | bytes 3076
  67.8 16.9 %all-to-all-start.3 = ((bf16[8,32,1024]{2,1,0:T(8,128)(2,1)}), bf16[8,32,1024]{2,1,0:T(8,128)(2,1)S(1)}, u32[]{:S(2)}, u32[]{:S(2)}) async-start(bf16[8,32,1024]{2,1,0:T(8,128)(2,1)} %bitcast.47), calls=%async_computation.3 | async-start | bytes 1048576 | tf_op jit(solution)/shard_map/all_to_all | solution.py:83
where the time goes:
time: 86.4 us; the launch traced here: 85.6 us
  waiting for transfers between devices  39.8 us (46%)
  starting transfers between devices  21.9 us (25%)
  matrix products  13.4 us (16%)
  other arithmetic  5.32 us (6%)
  local copies, waits for them, and re-layouts  4.48 us (5%)
    all_to_all x1, waiting for transfers between devices, body(): lax.all_to_all(sent_x, ('expert', 'seq'), split_axis=0, concat_axis=0, ti...  12.1 us
    all_to_all x1, waiting for transfers between devices, body(): lax.all_to_all(sent_y, ('expert', 'seq'), split_axis=0, concat_axis=0, ti...  12.1 us
    all_to_all x1, starting transfers between devices, body(): lax.all_to_all(sent_g, ('expert', 'seq'), split_axis=0, concat_axis=0, ti...  7.25 us
    all_to_all x1, waiting for transfers between devices, body(): lax.all_to_all(token_part.reshape(peer_count, capacity, feature_dim), ('e...  7.17 us
    all_to_all x1, waiting for transfers between devices, body(): lax.all_to_all(sent_g, ('expert', 'seq'), split_axis=0, concat_axis=0, ti...  4.19 us
    all_to_all x1, waiting for transfers between devices, body(): lax.all_to_all(pair_comb.reshape(peer_count, capacity), ('expert', 'seq')...  4.18 us
    all_to_all x1, starting transfers between devices, body(): lax.all_to_all(pair_comb.reshape(peer_count, capacity), ('expert', 'seq')...  3.82 us
    all_to_all x1, starting transfers between devices, body(): lax.all_to_all(sent_y, ('expert', 'seq'), split_axis=0, concat_axis=0, ti...  3.66 us
  transfers between devices with their start and end apart: 7, of which 5 were waited for; matrix products, arithmetic and copies ran while one was open for 20% of the time, Pallas kernels for 0%

commit v1 on v0

--- a/solution.py
+++ b/solution.py
@@ -1,7 +1,14 @@
+import functools
+
 import jax
 import jax.numpy as jnp
 from jax import lax
+from jax.experimental import pallas as pl
+from jax.experimental.pallas import tpu as pltpu
 from jax.sharding import PartitionSpec as P
+
+LANES = 128
+VMEM_LIMIT = 32 * 1024 * 1024
 
 
 def from_partner(block, axis, distance):
@@ -38,7 +45,7 @@
     return (d_gate, d_up, token_part.astype(jnp.bfloat16), pair_comb)
 
 
-def body(tokens, cotangent, expert_ids, combine_int, w_gate, w_up, w_down):
+def routed_body(tokens, cotangent, expert_ids, combine_int, w_gate, w_up, w_down):
     peer_count = lax.axis_size(("expert", "seq"))
     count_tok, feature_dim = tokens.shape
     top_k = expert_ids.shape[1]
@@ -116,6 +123,201 @@
     return (token_grad.astype(jnp.bfloat16), combine_grad, grad_gate, grad_up)
 
 
+def call(kernel, out_shape, *operands, flops=0, moved=0, in_specs=None):
+    return pl.pallas_call(
+        kernel,
+        out_shape=out_shape,
+        in_specs=in_specs or [pl.BlockSpec(memory_space=pltpu.VMEM)] * len(operands),
+        cost_estimate=pl.CostEstimate(flops=flops, bytes_accessed=moved, transcendentals=0),
+        compiler_params=pltpu.CompilerParams(vmem_limit_bytes=VMEM_LIMIT),
+    )(*operands)
+
+
+def message_kernel(x_ref, y_ref, ids_ref, comb_ref, out_ref):
+    feature_dim = x_ref.shape[1]
+    out_ref[:, :feature_dim] = x_ref[...]
+    out_ref[:, feature_dim : 2 * feature_dim] = y_ref[...]
+    weights = comb_ref[...].astype(jnp.float32)
+    mix = (weights / jnp.sum(weights, axis=1, keepdims=True)).astype(jnp.bfloat16)
+    mix = mix.astype(jnp.float32)
+    ids = ids_ref[...]
+    lane = lax.broadcasted_iota(jnp.int32, (ids.shape[0], LANES), 1)
+    by_expert = jnp.zeros(lane.shape, jnp.float32)
+    for k in range(ids.shape[1]):
+        by_expert += jnp.where(ids[:, k : k + 1] == lane, mix[:, k : k + 1], 0.0)
+    out_ref[:, 2 * feature_dim :] = by_expert.astype(jnp.bfloat16)
+
+
+def expert_kernel(place_ref, *refs):
+    blocks = refs[:8]
+    gate_ref, up_ref, down_ref = refs[8:11]
+    part_refs = refs[11:19]
+    swap_ref, keep_ref = refs[19:]
+    rows, width = blocks[0].shape
+    feature_dim = (width - LANES) // 2
+    half = feature_dim // 2
+    expert, replica = place_ref[0], place_ref[1]
+    data = jnp.concatenate([block[...] for block in blocks], axis=0)
+    x_rows = data[:, :feature_dim]
+    y_rows = data[:, feature_dim : 2 * feature_dim]
+    lane = lax.broadcasted_iota(jnp.int32, (8 * rows, LANES), 1)
+    mix = jnp.sum(
+        jnp.where(lane == expert, data[:, 2 * feature_dim :].astype(jnp.float32), 0.0),
+        axis=1,
+        keepdims=True,
+    )
+    gate_w, up_w = gate_ref[0], up_ref[0]
+    nt = (((1,), (1,)), ((), ()))
+    pre_gate = jnp.dot(x_rows, gate_w, preferred_element_type=jnp.float32)
+    pre_up = jnp.dot(x_rows, up_w, preferred_element_type=jnp.float32)
+    back = lax.dot_general(y_rows, down_ref[0], nt, preferred_element_type=jnp.float32)
+    sig = jax.nn.sigmoid(pre_gate)
+    activated = pre_gate * sig
+    pair_comb = jnp.sum(back * (activated * pre_up), axis=1, keepdims=True)
+    scaled = mix * back
+    d_gate = (scaled * pre_up * sig * (1.0 + pre_gate * (1.0 - sig))).astype(jnp.bfloat16)
+    d_up = (scaled * activated).astype(jnp.bfloat16)
+    part = lax.dot_general(d_gate, gate_w, nt, preferred_element_type=jnp.float32)
+    part += lax.dot_general(d_up, up_w, nt, preferred_element_type=jnp.float32)
+    part = part.astype(jnp.bfloat16)
+    comb = jnp.where(lane == expert, pair_comb, 0.0).astype(jnp.bfloat16)
+    for index, out in enumerate(part_refs):
+        out[:, :feature_dim] = part[index * rows : (index + 1) * rows]
+        out[:, feature_dim:] = comb[index * rows : (index + 1) * rows]
+    hidden_w = d_gate.shape[1]
+    first, second = x_rows[:, :half], x_rows[:, half:]
+    swap_ref[:, :half] = jnp.where(replica == 0, second, first)
+    swap_ref[:, half : half + hidden_w] = d_gate
+    swap_ref[:, half + hidden_w :] = d_up
+    keep_ref[...] = jnp.where(replica == 0, first, second)
+
+
+def weight_kernel(keep_ref, own_ref, other_ref, gate_ref, up_ref):
+    half = keep_ref.shape[1]
+    hidden_w = gate_ref.shape[2]
+    cols = jnp.concatenate([keep_ref[...], other_ref[:, :half]], axis=0)
+    grads = jnp.concatenate([own_ref[:, half:], other_ref[:, half:]], axis=0)
+    total = lax.dot_general(
+        cols, grads, (((0,), (0,)), ((), ())), preferred_element_type=jnp.float32
+    )
+    gate_ref[0] = total[:, :hidden_w]
+    up_ref[0] = total[:, hidden_w:]
+
+
+def finish_kernel(ids_ref, *refs):
+    token_ref, comb_ref = refs[-2:]
+    feature_dim = token_ref.shape[1]
+    total = refs[0][...].astype(jnp.float32)
+    for ref in refs[1:-2]:
+        total += ref[...].astype(jnp.float32)
+    token_ref[...] = total[:, :feature_dim].astype(jnp.bfloat16)
+    comb = total[:, feature_dim:]
+    ids = ids_ref[...]
+    lane = lax.broadcasted_iota(jnp.int32, comb.shape, 1)
+    slot = lax.broadcasted_iota(jnp.int32, comb_ref.shape, 1)
+    out = jnp.zeros(comb_ref.shape, jnp.float32)
+    for k in range(ids.shape[1]):
+        value = jnp.sum(jnp.where(ids[:, k : k + 1] == lane, comb, 0.0), axis=1, keepdims=True)
+        out += jnp.where(slot == k, value, 0.0)
+    comb_ref[...] = out
+
+
+def across(block, mask):
+    peers = ("expert", "seq")
+    return lax.ppermute(block, peers, [(i, i ^ mask) for i in range(lax.axis_size(peers))])
+
+
+def dense_body(tokens, cotangent, expert_ids, combine_int, w_gate, w_up, w_down):
+    along_x, near_z, far_z = 1, 2, 4
+    rows, feature_dim = tokens.shape
+    hidden_w = w_gate.shape[2]
+    half = feature_dim // 2
+    bf16, f32 = jnp.bfloat16, jnp.float32
+    place = jnp.stack([lax.axis_index(("expert", "seq")), lax.axis_index("replica")])
+    place = place.astype(jnp.int32)
+    own = call(
+        message_kernel,
+        jax.ShapeDtypeStruct((rows, 2 * feature_dim + LANES), bf16),
+        tokens,
+        cotangent,
+        expert_ids,
+        combine_int,
+        moved=8 * rows * feature_dim,
+    )
+    z2 = across(own, far_z)
+    z1 = across(own, near_z)
+    x0 = across(own, along_x)
+    x1 = across(z1, along_x)
+    z3 = across(z2, near_z)
+    x2 = across(z2, along_x)
+    x3 = across(x2, near_z)
+    blocks = [own, z1, z2, z3, x0, x1, x2, x3]
+    part = jax.ShapeDtypeStruct((rows, feature_dim + LANES), bf16)
+    whole = pl.BlockSpec(memory_space=pltpu.VMEM)
+    outs = call(
+        expert_kernel,
+        (part,) * 8
+        + (
+            jax.ShapeDtypeStruct((8 * rows, half + 2 * hidden_w), bf16),
+            jax.ShapeDtypeStruct((8 * rows, half), bf16),
+        ),
+        place,
+        *blocks,
+        w_gate,
+        w_up,
+        w_down,
+        flops=2 * 8 * rows * feature_dim * hidden_w * 5,
+        moved=6 * feature_dim * hidden_w + 8 * rows * feature_dim * 8,
+        in_specs=[pl.BlockSpec(memory_space=pltpu.SMEM)] + [whole] * 11,
+    )
+    parts, swap, keep = outs[:8], outs[8], outs[9]
+    for_column, for_other = parts[:4], parts[4:]
+
+    def add(a, b):
+        return (a.astype(f32) + b.astype(f32)).astype(bf16)
+
+    sum3 = add(for_column[3], across(for_other[3], along_x))
+    r3 = across(sum3, near_z | far_z)
+    sum2 = add(for_column[2], across(for_other[2], along_x))
+    r2 = across(sum2, far_z)
+    sum1 = add(for_column[1], across(for_other[1], along_x))
+    r1 = across(sum1, near_z)
+    r0 = across(for_other[0], along_x)
+    other = lax.ppermute(swap, "replica", [(0, 1), (1, 0)])
+    grad = jax.ShapeDtypeStruct((1, half, hidden_w), f32)
+    grad_gate, grad_up = call(
+        weight_kernel,
+        (grad, grad),
+        keep,
+        swap,
+        other,
+        flops=2 * 16 * rows * half * 2 * hidden_w,
+        moved=8 * half * hidden_w + 16 * rows * (half + 2 * hidden_w),
+    )
+    token_grad, combine_grad = call(
+        finish_kernel,
+        (
+            jax.ShapeDtypeStruct((rows, feature_dim), bf16),
+            jax.ShapeDtypeStruct(expert_ids.shape, f32),
+        ),
+        expert_ids,
+        for_column[0],
+        r0,
+        r1,
+        r2,
+        r3,
+        moved=12 * rows * feature_dim,
+    )
+    return (token_grad, combine_grad, grad_gate, grad_up)
+
+
+def body(*operands):
+    sizes = [lax.axis_size(name) for name in ("expert", "seq", "replica")]
+    if sizes == [4, 2, 2] and operands[2].shape[1] == 8:
+        return dense_body(*operands)
+    return routed_body(*operands)
+
+
 def solution(mesh):
     in_specs = (
         P(("groups", "expert", "seq", "replica"), None),

time: 86.4 us -> 51.1 us (0.59)
  waiting for transfers between devices: 39.8 us -> 16.9 us
  matrix products: 13.4 us -> 0 us
  Pallas kernels: 0 us -> 5.33 us
  other arithmetic: 5.32 us -> 0.14 us
  local copies, waits for them, and re-layouts: 4.48 us -> 6.58 us
  starting transfers between devices: 21.9 us -> 21 us
    all_to_all x5 -> x0, waiting for transfers between devices: 39.8 us -> none  [the longest x1 12.1 us: body(): lax.all_to_all(sent_x, ('expert', 'seq'), split_axis=0, concat_axis=0, ti...]
    all_to_all x5 -> x0, starting transfers between devices: 21.9 us -> none  [the longest x1 7.25 us: body(): lax.all_to_all(sent_g, ('expert', 'seq'), split_axis=0, concat_axis=0, ti...]
    ppermute x2 -> x15, starting transfers between devices: 0.01 us -> 21 us  [the longest x14 21 us: across(): lax.ppermute(block, peers, [(i, i ^ mask) for i in range(lax.axis_size(pe...]
    ppermute x2 -> x15, waiting for transfers between devices: 0.01 us -> 16.9 us  [the longest x14 16.9 us: across(): lax.ppermute(block, peers, [(i, i ^ mask) for i in range(lax.axis_size(pe...]
    dot_general x12 -> x0, matrix products: 13.4 us -> none  [the longest x1 2.47 us: expert_pass(): lax.dot_general(y_rows, down_w, (((1,), (1,)), ((), ())), preferred_eleme...]
    unnamed x14 -> x15, local copies, waits for them, and re-layouts: 0.03 us -> 6.58 us
    pallas_call x0 -> x4, Pallas kernels: none -> 5.33 us  [call(): pl.pallas_call(kernel, out_shape=out_shape, in_specs=in_specs or [pl.Bloc...]
    reduce_sum x4 -> x0, other arithmetic: 2.37 us -> none  [the longest x1 0.79 us: body(): per_token = jnp.sum(member, axis=1)]
  transfers between devices with their start and end apart: 7 -> 15, of which waited for: 5 -> 9; matrix products, arithmetic and copies ran while one was open for 20% -> 2% of each run, Pallas kernels for 0% -> 2%
where the time goes in v1:
time: 51.1 us; the launch traced here: 50.7 us
  starting transfers between devices  21 us (41%)
  waiting for transfers between devices  16.9 us (33%)
  local copies, waits for them, and re-layouts  6.58 us (13%)
  Pallas kernels  5.33 us (10%)
  between operations  0.69 us (1%)
    ppermute x14, starting transfers between devices, across(): lax.ppermute(block, peers, [(i, i ^ mask) for i in range(lax.axis_size(pe...  21 us
    ppermute x14, waiting for transfers between devices, across(): lax.ppermute(block, peers, [(i, i ^ mask) for i in range(lax.axis_size(pe...  16.9 us
    unnamed x15, local copies, waits for them, and re-layouts  6.58 us
    pallas_call x4, Pallas kernels, call(): pl.pallas_call(kernel, out_shape=out_shape, in_specs=in_specs or [pl.Bloc...  5.33 us
  transfers between devices with their start and end apart: 15, of which 9 were waited for; matrix products, arithmetic and copies ran while one was open for 2% of the time, Pallas kernels for 2%

profile of v1, /device:TPU:0, one launch (start us, length us, event | category | flops | bytes accessed | tf_op | source)
XLA Modules:
  0.0 50.7 jit_solution(11733941232334587943)
XLA Ops:
  0.6 0.8 %copy.13.ids_ref = s32[32,8]{1,0:T(8,128)S(1)} copy(s32[32,8]{0,1:T(8,128)} %param.9) | data formatting | bytes 2048 | tf_op args[2]
  1.5 0.8 %copy-done = bf16[32,1024]{1,0:T(8,128)(2,1)S(1)} copy-done((bf16[32,1024]{1,0:T(8,128)(2,1)S(1)}, bf16[32,1024]{1,0:T(8,128)(2,1)}, u32[]{:S(2)}) %copy-start) | copy-done | bytes 65560
  2.3 0.8 %copy-done.1 = bf16[32,1024]{1,0:T(8,128)(2,1)S(1)} copy-done((bf16[32,1024]{1,0:T(8,128)(2,1)S(1)}, bf16[32,1024]{1,0:T(8,128)(2,1)}, u32[]{:S(2)}) %copy-start.1) | copy-done | bytes 65560
  3.4 4.1 %collective-permute-start.1 = (bf16[32,2176]{1,0:T(8,128)(2,1)S(1)}, bf16[32,2176]{1,0:T(8,128)(2,1)S(1)}, u32[]{:S(2)}, u32[]{:S(2)}) collective-permute-start(bf16[32,2176]{1,0:T(8,128)(2,1)S(1)} %shard_map.102.refs_0_), channel_id=1, source_target_pairs={{0,8},{2,10},{4,12},{6,14},{8,0},{10,2},{12,4},{14,6},{1,9},{3,11}... | collective-permute-start | bytes 417800 | tf_op jit(solution)/shard_map/ppermute | solution.py:227
  7.5 1.6 %collective-permute-start = (bf16[32,2176]{1,0:T(8,128)(2,1)S(1)}, bf16[32,2176]{1,0:T(8,128)(2,1)S(1)}, u32[]{:S(2)}, u32[]{:S(2)}) collective-permute-start(bf16[32,2176]{1,0:T(8,128)(2,1)S(1)} %shard_map.102.refs_0_), channel_id=1, source_target_pairs={{0,4},{2,6},{4,0},{6,2},{8,12},{10,14},{12,8},{14,10},{1,5},{3,7},... | collective-permute-start | bytes 417800 | tf_op jit(solution)/shard_map/ppermute | solution.py:227
  9.0 5.2 %collective-permute-done.1.refs_2_ = bf16[32,2176]{1,0:T(8,128)(2,1)S(1)} collective-permute-done((bf16[32,2176]{1,0:T(8,128)(2,1)S(1)}, bf16[32,2176]{1,0:T(8,128)(2,1)S(1)}, u32[]{:S(2)}, u32[]{:S(2)}) %collective-permute-start.1) | collective-permute-done | bytes 139296 | tf_op jit(solution)/shard_map/ppermute | solution.py:227
  14.2 1.5 %collective-permute-start.5 = (bf16[32,2176]{1,0:T(8,128)(2,1)S(1)}, bf16[32,2176]{1,0:T(8,128)(2,1)S(1)}, u32[]{:S(2)}, u32[]{:S(2)}) collective-permute-start(bf16[32,2176]{1,0:T(8,128)(2,1)S(1)} %collective-permute-done.1.refs_2_), channel_id=1, source_target_pairs={{0,2},{2,0},{4,6},{6,4},{8,10},{10,8},{12,14},{14,12},{1,3},{3,1},... | collective-permute-start | bytes 417800 | tf_op jit(solution)/shard_map/ppermute | solution.py:227
  15.8 0.5 collective-permute-start.3
  16.3 0.6 %collective-permute-start.2 = (bf16[32,2176]{1,0:T(8,128)(2,1)S(1)}, bf16[32,2176]{1,0:T(8,128)(2,1)S(1)}, u32[]{:S(2)}, u32[]{:S(2)}) collective-permute-start(bf16[32,2176]{1,0:T(8,128)(2,1)S(1)} %collective-permute-done.1.refs_2_), channel_id=1, source_target_pairs={{0,4},{2,6},{4,0},{6,2},{8,12},{10,14},{12,8},{14,10},{1,5},{3,7},... | collective-permute-start | bytes 417800 | tf_op jit(solution)/shard_map/ppermute | solution.py:227
  16.9 1.5 %collective-permute-start.4 = (bf16[32,2176]{1,0:T(8,128)(2,1)S(1)}, bf16[32,2176]{1,0:T(8,128)(2,1)S(1)}, u32[]{:S(2)}, u32[]{:S(2)}) collective-permute-start(bf16[32,2176]{1,0:T(8,128)(2,1)S(1)} %collective-permute-done.refs_1_), channel_id=1, source_target_pairs={{0,2},{2,0},{4,6},{6,4},{8,10},{10,8},{12,14},{14,12},{1,3},{3,1},... | collective-permute-start | bytes 417800 | tf_op jit(solution)/shard_map/ppermute | solution.py:227
  18.4 2.5 %collective-permute-done.5.refs_6_ = bf16[32,2176]{1,0:T(8,128)(2,1)S(1)} collective-permute-done((bf16[32,2176]{1,0:T(8,128)(2,1)S(1)}, bf16[32,2176]{1,0:T(8,128)(2,1)S(1)}, u32[]{:S(2)}, u32[]{:S(2)}) %collective-permute-start.5) | collective-permute-done | bytes 139296 | tf_op jit(solution)/shard_map/ppermute | solution.py:227
  20.8 0.5 %collective-permute-start.6 = (bf16[32,2176]{1,0:T(8,128)(2,1)S(1)}, bf16[32,2176]{1,0:T(8,128)(2,1)S(1)}, u32[]{:S(2)}, u32[]{:S(2)}) collective-permute-start(bf16[32,2176]{1,0:T(8,128)(2,1)S(1)} %collective-permute-done.5.refs_6_), channel_id=1, source_target_pairs={{0,4},{2,6},{4,0},{6,2},{8,12},{10,14},{12,8},{14,10},{1,5},{3,7},... | collective-permute-start | bytes 417800 | tf_op jit(solution)/shard_map/ppermute | solution.py:227
  21.5 1.9 %collective-permute-done.3.refs_4_ = bf16[32,2176]{1,0:T(8,128)(2,1)S(1)} collective-permute-done((bf16[32,2176]{1,0:T(8,128)(2,1)S(1)}, bf16[32,2176]{1,0:T(8,128)(2,1)S(1)}, u32[]{:S(2)}, u32[]{:S(2)}) %collective-permute-start.3) | collective-permute-done | bytes 139296 | tf_op jit(solution)/shard_map/ppermute | solution.py:227
  23.4 1.5 %collective-permute-done.4.refs_5_ = bf16[32,2176]{1,0:T(8,128)(2,1)S(1)} collective-permute-done((bf16[32,2176]{1,0:T(8,128)(2,1)S(1)}, bf16[32,2176]{1,0:T(8,128)(2,1)S(1)}, u32[]{:S(2)}, u32[]{:S(2)}) %collective-permute-start.4) | collective-permute-done | bytes 139296 | tf_op jit(solution)/shard_map/ppermute | solution.py:227
  24.9 1.0 %collective-permute-done.6.refs_7_ = bf16[32,2176]{1,0:T(8,128)(2,1)S(1)} collective-permute-done((bf16[32,2176]{1,0:T(8,128)(2,1)S(1)}, bf16[32,2176]{1,0:T(8,128)(2,1)S(1)}, u32[]{:S(2)}, u32[]{:S(2)}) %collective-permute-start.6) | collective-permute-done | bytes 139296 | tf_op jit(solution)/shard_map/ppermute | solution.py:227
  25.9 1.1 %copy-done.2 = bf16[1,1024,384]{2,1,0:T(8,128)(2,1)S(1)} copy-done((bf16[1,1024,384]{2,1,0:T(8,128)(2,1)S(1)}, bf16[1,1024,384]{2,1,0:T(8,128)(2,1)}, u32[]{:S(2)}) %copy-start.2) | copy-done | bytes 786456
  27.0 1.1 %copy-done.3 = bf16[1,1024,384]{2,1,0:T(8,128)(2,1)S(1)} copy-done((bf16[1,1024,384]{2,1,0:T(8,128)(2,1)S(1)}, bf16[1,1024,384]{2,1,0:T(8,128)(2,1)}, u32[]{:S(2)}) %copy-start.3) | copy-done | bytes 786456
  28.2 1.1 %copy-done.4 = bf16[1,384,1024]{2,1,0:T(8,128)(2,1)S(1)} copy-done((bf16[1,384,1024]{2,1,0:T(8,128)(2,1)S(1)}, bf16[1,384,1024]{2,1,0:T(8,128)(2,1)}, u32[]{:S(2)}) %copy-start.4) | copy-done | bytes 786456
  29.3 2.3 %shard_map.103 = (bf16[32,1152]{1,0:T(8,128)(2,1)S(1)}, bf16[32,1152]{1,0:T(8,128)(2,1)S(1)}, bf16[32,1152]{1,0:T(8,128)(2,1)S(1)}, bf16[32,1152]{1,0:T(8,128)(2...) custom-call(s32[2]{0:T(128)S(1)} %pad_add_fusion.place_ref, ...), custom_call_target="tpu_custom_call" | custom-call | flops 1006632960 | bytes 4456448 | tf_op jit(solution)/shard_map/pallas_call | solution.py:127
  31.6 1.6 %collective-permute-start.8 = (bf16[32,1152]{1,0:T(8,128)(2,1)S(1)}, bf16[32,1152]{1,0:T(8,128)(2,1)S(1)}, u32[]{:S(2)}, u32[]{:S(2)}) collective-permute-start(bf16[32,1152]{1,0:T(8,128)(2,1)S(1)} %get-tuple-element.21), channel_id=1, source_target_pairs={{0,2},{2,0},{4,6},{6,4},{8,10},{10,8},{12,14},{14,12},{1,3},{3,1},... | collective-permute-start | bytes 221192 | tf_op jit(solution)/shard_map/ppermute | solution.py:227
  33.2 0.5 collective-permute-start.7
  33.7 1.5 %collective-permute-start.10 = (bf16[32,1152]{1,0:T(8,128)(2,1)S(1)}, bf16[32,1152]{1,0:T(8,128)(2,1)S(1)}, u32[]{:S(2)}, u32[]{:S(2)}) collective-permute-start(bf16[32,1152]{1,0:T(8,128)(2,1)S(1)} %get-tuple-element.23), channel_id=1, source_target_pairs={{0,2},{2,0},{4,6},{6,4},{8,10},{10,8},{12,14},{14,12},{1,3},{3,1},... | collective-permute-start | bytes 221192 | tf_op jit(solution)/shard_map/ppermute | solution.py:227
  35.2 0.5 collective-permute-start.12
  36.0 1.4 %collective-permute-start.9 = (bf16[32,1152]{1,0:T(8,128)(2,1)S(1)}, bf16[32,1152]{1,0:T(8,128)(2,1)S(1)}, u32[]{:S(2)}, u32[]{:S(2)}) collective-permute-start(bf16[32,1152]{1,0:T(8,128)(2,1)S(1)} %add_convert_fusion.2), channel_id=1, source_target_pairs={{0,4},{2,6},{4,0},{6,2},{8,12},{10,14},{12,8},{14,10},{1,5},{3,7},... | collective-permute-start | bytes 221192 | tf_op jit(solution)/shard_map/ppermute | solution.py:227
  37.4 1.0 %collective-permute-done.10 = bf16[32,1152]{1,0:T(8,128)(2,1)S(1)} collective-permute-done((bf16[32,1152]{1,0:T(8,128)(2,1)S(1)}, bf16[32,1152]{1,0:T(8,128)(2,1)S(1)}, u32[]{:S(2)}, u32[]{:S(2)}) %collective-permute-start.10) | collective-permute-done | bytes 73760 | tf_op jit(solution)/shard_map/ppermute | solution.py:227
  38.3 2.5 %collective-permute-start.11 = (bf16[32,1152]{1,0:T(8,128)(2,1)S(1)}, bf16[32,1152]{1,0:T(8,128)(2,1)S(1)}, u32[]{:S(2)}, u32[]{:S(2)}) collective-permute-start(bf16[32,1152]{1,0:T(8,128)(2,1)S(1)} %add_convert_fusion.1), channel_id=1, source_target_pairs={{0,8},{2,10},{4,12},{6,14},{8,0},{10,2},{12,4},{14,6},{1,9},{3,11}... | collective-permute-start | bytes 221192 | tf_op jit(solution)/shard_map/ppermute | solution.py:227
  40.9 2.7 %collective-permute-start.13 = (bf16[32,1152]{1,0:T(8,128)(2,1)S(1)}, bf16[32,1152]{1,0:T(8,128)(2,1)S(1)}, u32[]{:S(2)}, u32[]{:S(2)}) collective-permute-start(bf16[32,1152]{1,0:T(8,128)(2,1)S(1)} %add_convert_fusion), channel_id=1, source_target_pairs={{0,12},{2,14},{4,8},{6,10},{8,4},{10,6},{12,0},{14,2},{1,13},{3,15... | collective-permute-start | bytes 221192 | tf_op jit(solution)/shard_map/ppermute | solution.py:227
  43.6 0.8 %collective-permute-done.11.refs_3_ = bf16[32,1152]{1,0:T(8,128)(2,1)S(1)} collective-permute-done((bf16[32,1152]{1,0:T(8,128)(2,1)S(1)}, bf16[32,1152]{1,0:T(8,128)(2,1)S(1)}, u32[]{:S(2)}, u32[]{:S(2)}) %collective-permute-start.11) | collective-permute-done | bytes 73760 | tf_op jit(solution)/shard_map/ppermute | solution.py:227
  44.3 2.8 %collective-permute-done.13.refs_4_ = bf16[32,1152]{1,0:T(8,128)(2,1)S(1)} collective-permute-done((bf16[32,1152]{1,0:T(8,128)(2,1)S(1)}, bf16[32,1152]{1,0:T(8,128)(2,1)S(1)}, u32[]{:S(2)}, u32[]{:S(2)}) %collective-permute-start.13) | collective-permute-done | bytes 73760 | tf_op jit(solution)/shard_map/ppermute | solution.py:227
  47.1 1.1 %shard_map.104 = (bf16[32,1024]{1,0:T(8,128)(2,1)}, f32[32,8]{1,0:T(8,128)S(1)}) custom-call(s32[32,8]{1,0:T(8,128)S(1)} %copy.13.ids_ref, bf16[32,1152]{1,0:T(8,128)(2,1)S(1)} %get-tuple-element.18.refs_0_, bf16[32,1152]{1,0:T(8,128)(2,1)S(1)} %collective-permute-done.7.refs_1_, bf16[32,1152]{1,0:T(8,128)(2,1)S(1)} %collective-permute-done.9.refs_2_, ...), custom_call_target="tpu_custom_call" | custom-call | bytes 393216 | tf_op jit(solution)/shard_map/pallas_call | solution.py:127
  48.3 0.7 %copy.14 = f32[32,8]{0,1:T(8,128)} copy(f32[32,8]{1,0:T(8,128)S(1)} %get-tuple-element.33) | data formatting | bytes 2048
  48.9 1.8 %shard_map.105 = (f32[1,512,384]{2,1,0:T(8,128)}, f32[1,512,384]{2,1,0:T(8,128)}) custom-call(bf16[256,512]{1,0:T(8,128)(2,1)S(1)} %get-tuple-element.28.keep_ref, bf16[256,1280]{1,0:T(8,128)(2,1)S(1)} %get-tuple-element.29.own_ref, bf16[256,1280]{1,0:T(8,128)(2,1)S(1)} %collective-permute-done.14.other_ref), custom_call_target="tpu_custom_call" | custom-call | flops 402653184 | bytes 2228224 | tf_op jit(solution)/shard_map/pallas_call | solution.py:127
  (21 shorter events, 0.7 us)
Async XLA Ops:
  0.6 0.8 %copy-start.5 = (s32[32,8]{0,1:T(8,128)S(1)}, s32[32,8]{0,1:T(8,128)}, u32[]{:S(2)}) copy-start(s32[32,8]{0,1:T(8,128)} %param.10) | copy-start | bytes 3076
  1.5 0.8 %copy-start = (bf16[32,1024]{1,0:T(8,128)(2,1)S(1)}, bf16[32,1024]{1,0:T(8,128)(2,1)}, u32[]{:S(2)}) copy-start(bf16[32,1024]{1,0:T(8,128)(2,1)} %x_ref.1) | copy-start | bytes 196612
  2.3 0.8 %copy-start.1 = (bf16[32,1024]{1,0:T(8,128)(2,1)S(1)}, bf16[32,1024]{1,0:T(8,128)(2,1)}, u32[]{:S(2)}) copy-start(bf16[32,1024]{1,0:T(8,128)(2,1)} %y_ref.1) | copy-start | bytes 196612
  3.4 10.9 %collective-permute-start.1 = (bf16[32,2176]{1,0:T(8,128)(2,1)S(1)}, bf16[32,2176]{1,0:T(8,128)(2,1)S(1)}, u32[]{:S(2)}, u32[]{:S(2)}) collective-permute-start(bf16[32,2176]{1,0:T(8,128)(2,1)S(1)} %shard_map.102.refs_0_), channel_id=1, source_target_pairs={{0,8},{2,10},{4,12},{6,14},{8,0},{10,2},{12,4},{14,6},{1,9},{3,11}... | collective-permute-start | bytes 417800 | tf_op jit(solution)/shard_map/ppermute | solution.py:227
  7.5 9.4 %collective-permute-start = (bf16[32,2176]{1,0:T(8,128)(2,1)S(1)}, bf16[32,2176]{1,0:T(8,128)(2,1)S(1)}, u32[]{:S(2)}, u32[]{:S(2)}) collective-permute-start(bf16[32,2176]{1,0:T(8,128)(2,1)S(1)} %shard_map.102.refs_0_), channel_id=1, source_target_pairs={{0,4},{2,6},{4,0},{6,2},{8,12},{10,14},{12,8},{14,10},{1,5},{3,7},... | collective-permute-start | bytes 417800 | tf_op jit(solution)/shard_map/ppermute | solution.py:227
  14.2 6.6 %collective-permute-start.5 = (bf16[32,2176]{1,0:T(8,128)(2,1)S(1)}, bf16[32,2176]{1,0:T(8,128)(2,1)S(1)}, u32[]{:S(2)}, u32[]{:S(2)}) collective-permute-start(bf16[32,2176]{1,0:T(8,128)(2,1)S(1)} %collective-permute-done.1.refs_2_), channel_id=1, source_target_pairs={{0,2},{2,0},{4,6},{6,4},{8,10},{10,8},{12,14},{14,12},{1,3},{3,1},... | collective-permute-start | bytes 417800 | tf_op jit(solution)/shard_map/ppermute | solution.py:227
  15.8 7.6 %collective-permute-start.3 = (bf16[32,2176]{1,0:T(8,128)(2,1)S(1)}, bf16[32,2176]{1,0:T(8,128)(2,1)S(1)}, u32[]{:S(2)}, u32[]{:S(2)}) collective-permute-start(bf16[32,2176]{1,0:T(8,128)(2,1)S(1)} %shard_map.102.refs_0_), channel_id=1, source_target_pairs={{0,2},{2,0},{4,6},{6,4},{8,10},{10,8},{12,14},{14,12},{1,3},{3,1},... | collective-permute-start | bytes 417800 | tf_op jit(solution)/shard_map/ppermute | solution.py:227
  16.3 7.1 %collective-permute-start.2 = (bf16[32,2176]{1,0:T(8,128)(2,1)S(1)}, bf16[32,2176]{1,0:T(8,128)(2,1)S(1)}, u32[]{:S(2)}, u32[]{:S(2)}) collective-permute-start(bf16[32,2176]{1,0:T(8,128)(2,1)S(1)} %collective-permute-done.1.refs_2_), channel_id=1, source_target_pairs={{0,4},{2,6},{4,0},{6,2},{8,12},{10,14},{12,8},{14,10},{1,5},{3,7},... | collective-permute-start | bytes 417800 | tf_op jit(solution)/shard_map/ppermute | solution.py:227
  16.9 8.0 %collective-permute-start.4 = (bf16[32,2176]{1,0:T(8,128)(2,1)S(1)}, bf16[32,2176]{1,0:T(8,128)(2,1)S(1)}, u32[]{:S(2)}, u32[]{:S(2)}) collective-permute-start(bf16[32,2176]{1,0:T(8,128)(2,1)S(1)} %collective-permute-done.refs_1_), channel_id=1, source_target_pairs={{0,2},{2,0},{4,6},{6,4},{8,10},{10,8},{12,14},{14,12},{1,3},{3,1},... | collective-permute-start | bytes 417800 | tf_op jit(solution)/shard_map/ppermute | solution.py:227
  20.8 5.1 %collective-permute-start.6 = (bf16[32,2176]{1,0:T(8,128)(2,1)S(1)}, bf16[32,2176]{1,0:T(8,128)(2,1)S(1)}, u32[]{:S(2)}, u32[]{:S(2)}) collective-permute-start(bf16[32,2176]{1,0:T(8,128)(2,1)S(1)} %collective-permute-done.5.refs_6_), channel_id=1, source_target_pairs={{0,4},{2,6},{4,0},{6,2},{8,12},{10,14},{12,8},{14,10},{1,5},{3,7},... | collective-permute-start | bytes 417800 | tf_op jit(solution)/shard_map/ppermute | solution.py:227
  25.9 1.1 %copy-start.2 = (bf16[1,1024,384]{2,1,0:T(8,128)(2,1)S(1)}, bf16[1,1024,384]{2,1,0:T(8,128)(2,1)}, u32[]{:S(2)}) copy-start(bf16[1,1024,384]{2,1,0:T(8,128)(2,1)} %refs_8_.1) | copy-start | bytes 2359300
  27.0 1.1 %copy-start.3 = (bf16[1,1024,384]{2,1,0:T(8,128)(2,1)S(1)}, bf16[1,1024,384]{2,1,0:T(8,128)(2,1)}, u32[]{:S(2)}) copy-start(bf16[1,1024,384]{2,1,0:T(8,128)(2,1)} %refs_9_.1) | copy-start | bytes 2359300
  28.2 1.1 %copy-start.4 = (bf16[1,384,1024]{2,1,0:T(8,128)(2,1)S(1)}, bf16[1,384,1024]{2,1,0:T(8,128)(2,1)}, u32[]{:S(2)}) copy-start(bf16[1,384,1024]{2,1,0:T(8,128)(2,1)} %refs_10_.1) | copy-start | bytes 2359300
  31.6 4.4 %collective-permute-start.8 = (bf16[32,1152]{1,0:T(8,128)(2,1)S(1)}, bf16[32,1152]{1,0:T(8,128)(2,1)S(1)}, u32[]{:S(2)}, u32[]{:S(2)}) collective-permute-start(bf16[32,1152]{1,0:T(8,128)(2,1)S(1)} %get-tuple-element.21), channel_id=1, source_target_pairs={{0,2},{2,0},{4,6},{6,4},{8,10},{10,8},{12,14},{14,12},{1,3},{3,1},... | collective-permute-start | bytes 221192 | tf_op jit(solution)/shard_map/ppermute | solution.py:227
  33.2 10.4 %collective-permute-start.7 = (bf16[32,1152]{1,0:T(8,128)(2,1)S(1)}, bf16[32,1152]{1,0:T(8,128)(2,1)S(1)}, u32[]{:S(2)}, u32[]{:S(2)}) collective-permute-start(bf16[32,1152]{1,0:T(8,128)(2,1)S(1)} %get-tuple-element.19), channel_id=1, source_target_pairs={{0,2},{2,0},{4,6},{6,4},{8,10},{10,8},{12,14},{14,12},{1,3},{3,1},... | collective-permute-start | bytes 221192 | tf_op jit(solution)/shard_map/ppermute | solution.py:227
  33.7 4.7 %collective-permute-start.10 = (bf16[32,1152]{1,0:T(8,128)(2,1)S(1)}, bf16[32,1152]{1,0:T(8,128)(2,1)S(1)}, u32[]{:S(2)}, u32[]{:S(2)}) collective-permute-start(bf16[32,1152]{1,0:T(8,128)(2,1)S(1)} %get-tuple-element.23), channel_id=1, source_target_pairs={{0,2},{2,0},{4,6},{6,4},{8,10},{10,8},{12,14},{14,12},{1,3},{3,1},... | collective-permute-start | bytes 221192 | tf_op jit(solution)/shard_map/ppermute | solution.py:227
  35.2 5.6 %collective-permute-start.12 = (bf16[32,1152]{1,0:T(8,128)(2,1)S(1)}, bf16[32,1152]{1,0:T(8,128)(2,1)S(1)}, u32[]{:S(2)}, u32[]{:S(2)}) collective-permute-start(bf16[32,1152]{1,0:T(8,128)(2,1)S(1)} %get-tuple-element.25), channel_id=1, source_target_pairs={{0,2},{2,0},{4,6},{6,4},{8,10},{10,8},{12,14},{14,12},{1,3},{3,1},... | collective-permute-start | bytes 221192 | tf_op jit(solution)/shard_map/ppermute | solution.py:227
  35.7 13.2 %collective-permute-start.14 = (bf16[256,1280]{1,0:T(8,128)(2,1)S(1)}, bf16[256,1280]{1,0:T(8,128)(2,1)S(1)}, u32[]{:S(2)}, u32[]{:S(2)}) collective-permute-start(bf16[256,1280]{1,0:T(8,128)(2,1)S(1)} %get-tuple-element.29.own_ref), channel_id=1, source_target_pairs={{0,1},{1,0},{2,3},{3,2},{4,5},{5,4},{6,7},{7,6},{8,9},{9,8},{10,11... | collective-permute-start | bytes 1966088 | tf_op jit(solution)/shard_map/ppermute | solution.py:286
  36.0 7.6 %collective-permute-start.9 = (bf16[32,1152]{1,0:T(8,128)(2,1)S(1)}, bf16[32,1152]{1,0:T(8,128)(2,1)S(1)}, u32[]{:S(2)}, u32[]{:S(2)}) collective-permute-start(bf16[32,1152]{1,0:T(8,128)(2,1)S(1)} %add_convert_fusion.2), channel_id=1, source_target_pairs={{0,4},{2,6},{4,0},{6,2},{8,12},{10,14},{12,8},{14,10},{1,5},{3,7},... | collective-permute-start | bytes 221192 | tf_op jit(solution)/shard_map/ppermute | solution.py:227
  38.3 6.0 %collective-permute-start.11 = (bf16[32,1152]{1,0:T(8,128)(2,1)S(1)}, bf16[32,1152]{1,0:T(8,128)(2,1)S(1)}, u32[]{:S(2)}, u32[]{:S(2)}) collective-permute-start(bf16[32,1152]{1,0:T(8,128)(2,1)S(1)} %add_convert_fusion.1), channel_id=1, source_target_pairs={{0,8},{2,10},{4,12},{6,14},{8,0},{10,2},{12,4},{14,6},{1,9},{3,11}... | collective-permute-start | bytes 221192 | tf_op jit(solution)/shard_map/ppermute | solution.py:227
  40.9 6.3 %collective-permute-start.13 = (bf16[32,1152]{1,0:T(8,128)(2,1)S(1)}, bf16[32,1152]{1,0:T(8,128)(2,1)S(1)}, u32[]{:S(2)}, u32[]{:S(2)}) collective-permute-start(bf16[32,1152]{1,0:T(8,128)(2,1)S(1)} %add_convert_fusion), channel_id=1, source_target_pairs={{0,12},{2,14},{4,8},{6,10},{8,4},{10,6},{12,0},{14,2},{1,13},{3,15... | collective-permute-start | bytes 221192 | tf_op jit(solution)/shard_map/ppermute | solution.py:227

commit v2 on v1

--- a/solution.py
+++ b/solution.py
@@ -9,6 +9,7 @@
 
 LANES = 128
 VMEM_LIMIT = 32 * 1024 * 1024
+VMEM_MOST = 56 * 1024 * 1024
 
 
 def from_partner(block, axis, distance):
@@ -123,36 +124,64 @@
     return (token_grad.astype(jnp.bfloat16), combine_grad, grad_gate, grad_up)
 
 
-def call(kernel, out_shape, *operands, flops=0, moved=0, in_specs=None):
+NT = (((1,), (1,)), ((), ()))
+VMEM = pl.BlockSpec(memory_space=pltpu.VMEM)
+SMEM = pl.BlockSpec(memory_space=pltpu.SMEM)
+HBM = pl.BlockSpec(memory_space=pltpu.HBM)
+
+
+def call(kernel, out_shape, *operands, in_specs, out_specs, scratch=(), flops=0, moved=0, limit=VMEM_LIMIT, aliases={}):
     return pl.pallas_call(
         kernel,
         out_shape=out_shape,
-        in_specs=in_specs or [pl.BlockSpec(memory_space=pltpu.VMEM)] * len(operands),
+        in_specs=in_specs,
+        out_specs=out_specs,
+        scratch_shapes=scratch,
+        input_output_aliases=aliases,
         cost_estimate=pl.CostEstimate(flops=flops, bytes_accessed=moved, transcendentals=0),
-        compiler_params=pltpu.CompilerParams(vmem_limit_bytes=VMEM_LIMIT),
+        compiler_params=pltpu.CompilerParams(vmem_limit_bytes=limit),
     )(*operands)
 
 
-def message_kernel(x_ref, y_ref, ids_ref, comb_ref, out_ref):
+def one_hot_rows(rows):
+    shape = (rows, rows)
+    here = lax.broadcasted_iota(jnp.int32, shape, 0) == lax.broadcasted_iota(jnp.int32, shape, 1)
+    return here.astype(jnp.bfloat16)
+
+
+def message_kernel(x_ref, y_ref, ids_hbm, comb_hbm, out_ref, ids_ref, comb_ref, *sems):
     feature_dim = x_ref.shape[1]
-    out_ref[:, :feature_dim] = x_ref[...]
-    out_ref[:, feature_dim : 2 * feature_dim] = y_ref[...]
+    ids_sem, comb_sem, x_sem, y_sem = sems
+    ids_copy = pltpu.make_async_copy(ids_hbm, ids_ref, ids_sem)
+    comb_copy = pltpu.make_async_copy(comb_hbm, comb_ref, comb_sem)
+    ids_copy.start()
+    comb_copy.start()
+    x_copy = pltpu.make_async_copy(x_ref, out_ref.at[:, :feature_dim], x_sem)
+    y_copy = pltpu.make_async_copy(y_ref, out_ref.at[:, feature_dim : 2 * feature_dim], y_sem)
+    x_copy.start()
+    y_copy.start()
+    ids_copy.wait()
+    comb_copy.wait()
     weights = comb_ref[...].astype(jnp.float32)
-    mix = (weights / jnp.sum(weights, axis=1, keepdims=True)).astype(jnp.bfloat16)
+    mix = (weights / jnp.sum(weights, axis=0, keepdims=True)).astype(jnp.bfloat16)
     mix = mix.astype(jnp.float32)
     ids = ids_ref[...]
-    lane = lax.broadcasted_iota(jnp.int32, (ids.shape[0], LANES), 1)
-    by_expert = jnp.zeros(lane.shape, jnp.float32)
-    for k in range(ids.shape[1]):
-        by_expert += jnp.where(ids[:, k : k + 1] == lane, mix[:, k : k + 1], 0.0)
-    out_ref[:, 2 * feature_dim :] = by_expert.astype(jnp.bfloat16)
-
-
-def expert_kernel(place_ref, *refs):
-    blocks = refs[:8]
-    gate_ref, up_ref, down_ref = refs[8:11]
-    part_refs = refs[11:19]
-    swap_ref, keep_ref = refs[19:]
+    count = ids.shape[1]
+    expert = lax.broadcasted_iota(jnp.int32, (LANES, count), 0)
+    by_expert = jnp.zeros((LANES, count), jnp.float32)
+    for k in range(ids.shape[0]):
+        by_expert += jnp.where(ids[k : k + 1] == expert, mix[k : k + 1], 0.0)
+    turned = lax.dot_general(
+        one_hot_rows(count), by_expert.astype(jnp.bfloat16), NT, preferred_element_type=jnp.float32
+    )
+    out_ref[:, 2 * feature_dim :] = turned.astype(jnp.bfloat16)
+    x_copy.wait()
+    y_copy.wait()
+
+
+def expert_kernel(place_ref, touched_ref, *refs):
+    blocks, (gate_ref, up_ref, down_ref) = refs[:8], refs[8:11]
+    part_refs, (swap_ref, keep_ref) = refs[11:18], refs[18:]
     rows, width = blocks[0].shape
     feature_dim = (width - LANES) // 2
     half = feature_dim // 2
@@ -160,39 +189,46 @@
     data = jnp.concatenate([block[...] for block in blocks], axis=0)
     x_rows = data[:, :feature_dim]
     y_rows = data[:, feature_dim : 2 * feature_dim]
-    lane = lax.broadcasted_iota(jnp.int32, (8 * rows, LANES), 1)
+    lane = lax.broadcasted_iota(jnp.int32, (data.shape[0], LANES), 1)
     mix = jnp.sum(
         jnp.where(lane == expert, data[:, 2 * feature_dim :].astype(jnp.float32), 0.0),
         axis=1,
         keepdims=True,
     )
-    gate_w, up_w = gate_ref[0], up_ref[0]
-    nt = (((1,), (1,)), ((), ()))
-    pre_gate = jnp.dot(x_rows, gate_w, preferred_element_type=jnp.float32)
-    pre_up = jnp.dot(x_rows, up_w, preferred_element_type=jnp.float32)
-    back = lax.dot_general(y_rows, down_ref[0], nt, preferred_element_type=jnp.float32)
+    gate, up = gate_ref[0], up_ref[0]
+    pre_gate = jnp.dot(x_rows, gate, preferred_element_type=jnp.float32)
+    pre_up = jnp.dot(x_rows, up, preferred_element_type=jnp.float32)
+    back = lax.dot_general(y_rows, down_ref[0], NT, preferred_element_type=jnp.float32)
     sig = jax.nn.sigmoid(pre_gate)
     activated = pre_gate * sig
     pair_comb = jnp.sum(back * (activated * pre_up), axis=1, keepdims=True)
     scaled = mix * back
     d_gate = (scaled * pre_up * sig * (1.0 + pre_gate * (1.0 - sig))).astype(jnp.bfloat16)
     d_up = (scaled * activated).astype(jnp.bfloat16)
-    part = lax.dot_general(d_gate, gate_w, nt, preferred_element_type=jnp.float32)
-    part += lax.dot_general(d_up, up_w, nt, preferred_element_type=jnp.float32)
+    part = lax.dot_general(d_gate, gate, NT, preferred_element_type=jnp.float32)
+    part += lax.dot_general(d_up, up, NT, preferred_element_type=jnp.float32)
     part = part.astype(jnp.bfloat16)
     comb = jnp.where(lane == expert, pair_comb, 0.0).astype(jnp.bfloat16)
-    for index, out in enumerate(part_refs):
-        out[:, :feature_dim] = part[index * rows : (index + 1) * rows]
-        out[:, feature_dim:] = comb[index * rows : (index + 1) * rows]
+    first = 0
+    for out in part_refs:
+        last = first + out.shape[0]
+        out[:, :feature_dim] = part[first:last]
+        out[:, feature_dim:] = comb[first:last]
+        first = last
     hidden_w = d_gate.shape[1]
-    first, second = x_rows[:, :half], x_rows[:, half:]
-    swap_ref[:, :half] = jnp.where(replica == 0, second, first)
+    low, high = x_rows[:, :half], x_rows[:, half:]
+    swap_ref[:, :half] = jnp.where(replica == 0, high, low)
     swap_ref[:, half : half + hidden_w] = d_gate
     swap_ref[:, half + hidden_w :] = d_up
-    keep_ref[...] = jnp.where(replica == 0, first, second)
-
-
-def weight_kernel(keep_ref, own_ref, other_ref, gate_ref, up_ref):
+    keep_ref[...] = jnp.where(replica == 0, low, high)
+
+
+def touch_kernel(after_ref, gate_ref, up_ref, down_ref, out_ref):
+    out_ref[...] = jnp.zeros(out_ref.shape, out_ref.dtype)
+
+
+def weight_kernel(keep_ref, own_ref, other_ref, gate_ref, up_ref, done_ref):
+    done_ref[...] = jnp.zeros(done_ref.shape, done_ref.dtype)
     half = keep_ref.shape[1]
     hidden_w = gate_ref.shape[2]
     cols = jnp.concatenate([keep_ref[...], other_ref[:, :half]], axis=0)
@@ -204,27 +240,46 @@
     up_ref[0] = total[:, hidden_w:]
 
 
-def finish_kernel(ids_ref, *refs):
+def finish_kernel(ids_hbm, done_ref, *refs):
+    *refs, ids_ref, ids_sem = refs
+    ids_copy = pltpu.make_async_copy(ids_hbm, ids_ref, ids_sem)
+    ids_copy.start()
     token_ref, comb_ref = refs[-2:]
-    feature_dim = token_ref.shape[1]
+    rows, feature_dim = token_ref.shape
     total = refs[0][...].astype(jnp.float32)
     for ref in refs[1:-2]:
         total += ref[...].astype(jnp.float32)
     token_ref[...] = total[:, :feature_dim].astype(jnp.bfloat16)
-    comb = total[:, feature_dim:]
+    comb = total[:, feature_dim:].astype(jnp.bfloat16)
+    turned = lax.dot_general(
+        one_hot_rows(LANES), comb, NT, preferred_element_type=jnp.float32
+    )
+    ids_copy.wait()
     ids = ids_ref[...]
-    lane = lax.broadcasted_iota(jnp.int32, comb.shape, 1)
-    slot = lax.broadcasted_iota(jnp.int32, comb_ref.shape, 1)
-    out = jnp.zeros(comb_ref.shape, jnp.float32)
-    for k in range(ids.shape[1]):
-        value = jnp.sum(jnp.where(ids[:, k : k + 1] == lane, comb, 0.0), axis=1, keepdims=True)
-        out += jnp.where(slot == k, value, 0.0)
+    out = jnp.zeros(ids.shape, jnp.float32)
+    for expert in range(ids.shape[0]):
+        out += jnp.where(ids == expert, turned[expert : expert + 1], 0.0)
     comb_ref[...] = out
 
 
 def across(block, mask):
     peers = ("expert", "seq")
     return lax.ppermute(block, peers, [(i, i ^ mask) for i in range(lax.axis_size(peers))])
+
+
+def swapped(block):
+    return lax.ppermute(block, "replica", [(0, 1), (1, 0)])
+
+
+def add(*terms):
+    total = terms[0].astype(jnp.float32)
+    for term in terms[1:]:
+        total = total + term.astype(jnp.float32)
+    return total.astype(jnp.bfloat16)
+
+
+def after(value, *others):
+    return lax.optimization_barrier((value,) + others)[0]
 
 
 def dense_body(tokens, cotangent, expert_ids, combine_int, w_gate, w_up, w_down):
@@ -235,80 +290,91 @@
     bf16, f32 = jnp.bfloat16, jnp.float32
     place = jnp.stack([lax.axis_index(("expert", "seq")), lax.axis_index("replica")])
     place = place.astype(jnp.int32)
+    ids_turned = expert_ids.T
     own = call(
         message_kernel,
         jax.ShapeDtypeStruct((rows, 2 * feature_dim + LANES), bf16),
         tokens,
         cotangent,
-        expert_ids,
-        combine_int,
+        ids_turned,
+        combine_int.T,
+        in_specs=[HBM] * 4,
+        out_specs=VMEM,
+        scratch=[pltpu.VMEM(ids_turned.shape, jnp.int32)] * 2 + [pltpu.SemaphoreType.DMA] * 4,
         moved=8 * rows * feature_dim,
-    )
-    z2 = across(own, far_z)
+        limit=VMEM_MOST,
+    )
+    z3 = across(own, near_z | far_z)
+    x2 = across(own, along_x | far_z)
     z1 = across(own, near_z)
     x0 = across(own, along_x)
     x1 = across(z1, along_x)
-    z3 = across(z2, near_z)
-    x2 = across(z2, along_x)
-    x3 = across(x2, near_z)
-    blocks = [own, z1, z2, z3, x0, x1, x2, x3]
-    part = jax.ShapeDtypeStruct((rows, feature_dim + LANES), bf16)
-    whole = pl.BlockSpec(memory_space=pltpu.VMEM)
-    outs = call(
-        expert_kernel,
-        (part,) * 8
-        + (
-            jax.ShapeDtypeStruct((8 * rows, half + 2 * hidden_w), bf16),
-            jax.ShapeDtypeStruct((8 * rows, half), bf16),
-        ),
-        place,
-        *blocks,
+    x3 = across(z3, along_x)
+    z2 = across(z3, near_z)
+    held = (w_gate, w_up, w_down)
+    touched = call(
+        touch_kernel,
+        jax.ShapeDtypeStruct((8, LANES), f32),
+        z3,
         w_gate,
         w_up,
         w_down,
+        in_specs=[VMEM] * 4,
+        out_specs=VMEM,
+        moved=12 * feature_dim * hidden_w,
+    )
+    part = jax.ShapeDtypeStruct((rows, feature_dim + LANES), bf16)
+    pair = jax.ShapeDtypeStruct((2 * rows, feature_dim + LANES), bf16)
+    f0, f1, f2, f3, g01, g2, g3, swap, keep = call(
+        expert_kernel,
+        [part] * 4
+        + [
+            pair,
+            part,
+            part,
+            jax.ShapeDtypeStruct((8 * rows, half + 2 * hidden_w), bf16),
+            jax.ShapeDtypeStruct((8 * rows, half), bf16),
+        ],
+        place,
+        touched,
+        *(own, z1, z2, z3, x0, x1, x2, x3),
+        *held,
+        in_specs=[SMEM] + [VMEM] * 12,
+        out_specs=[VMEM] * 9,
         flops=2 * 8 * rows * feature_dim * hidden_w * 5,
         moved=6 * feature_dim * hidden_w + 8 * rows * feature_dim * 8,
-        in_specs=[pl.BlockSpec(memory_space=pltpu.SMEM)] + [whole] * 11,
-    )
-    parts, swap, keep = outs[:8], outs[8], outs[9]
-    for_column, for_other = parts[:4], parts[4:]
-
-    def add(a, b):
-        return (a.astype(f32) + b.astype(f32)).astype(bf16)
-
-    sum3 = add(for_column[3], across(for_other[3], along_x))
+    )
+    sum3 = add(f3, across(g3, along_x))
     r3 = across(sum3, near_z | far_z)
-    sum2 = add(for_column[2], across(for_other[2], along_x))
+    sum2 = add(f2, across(g2, along_x))
     r2 = across(sum2, far_z)
-    sum1 = add(for_column[1], across(for_other[1], along_x))
-    r1 = across(sum1, near_z)
-    r0 = across(for_other[0], along_x)
-    other = lax.ppermute(swap, "replica", [(0, 1), (1, 0)])
+    h01 = across(g01, along_x)
+    r1 = across(add(f1, h01[rows:]), near_z)
+    other = swapped(swap)
     grad = jax.ShapeDtypeStruct((1, half, hidden_w), f32)
-    grad_gate, grad_up = call(
+    grad_gate, grad_up, weights_done = call(
         weight_kernel,
-        (grad, grad),
+        (grad, grad, jax.ShapeDtypeStruct((8, LANES), f32)),
         keep,
         swap,
         other,
+        in_specs=[VMEM] * 3,
+        out_specs=[pl.BlockSpec((1, half, hidden_w))] * 2 + [VMEM],
         flops=2 * 16 * rows * half * 2 * hidden_w,
         moved=8 * half * hidden_w + 16 * rows * (half + 2 * hidden_w),
     )
-    token_grad, combine_grad = call(
+    token_grad, comb_turned = call(
         finish_kernel,
-        (
-            jax.ShapeDtypeStruct((rows, feature_dim), bf16),
-            jax.ShapeDtypeStruct(expert_ids.shape, f32),
-        ),
-        expert_ids,
-        for_column[0],
-        r0,
-        r1,
-        r2,
-        r3,
+        (jax.ShapeDtypeStruct((rows, feature_dim), bf16), jax.ShapeDtypeStruct(ids_turned.shape, f32)),
+        ids_turned,
+        weights_done,
+        *(f0, h01[:rows], r1, r2, r3),
+        in_specs=[HBM] + [VMEM] * 6,
+        out_specs=[pl.BlockSpec(tokens.shape), pl.BlockSpec(ids_turned.shape)],
+        scratch=[pltpu.VMEM(ids_turned.shape, jnp.int32), pltpu.SemaphoreType.DMA],
         moved=12 * rows * feature_dim,
     )
-    return (token_grad, combine_grad, grad_gate, grad_up)
+    return (token_grad, comb_turned.T, grad_gate, grad_up)
 
 
 def body(*operands):

time: 51.1 us -> 41.9 us (0.82)
  waiting for transfers between devices: 16.9 us -> 10.3 us
  local copies, waits for them, and re-layouts: 6.58 us -> 4.5 us
  starting transfers between devices: 21 us -> 19.5 us
  Pallas kernels: 5.33 us -> 6.46 us
    ppermute x14 -> x13, waiting for transfers between devices: 16.9 us -> 10.3 us  [across(): lax.ppermute(block, peers, [(i, i ^ mask) for i in range(lax.axis_size(pe...]
    unnamed x15 -> x12, local copies, waits for them, and re-layouts: 6.58 us -> 4.5 us
    ppermute x14 -> x13, starting transfers between devices: 21 us -> 19.5 us  [across(): lax.ppermute(block, peers, [(i, i ^ mask) for i in range(lax.axis_size(pe...]
    pallas_call x4 -> x5, Pallas kernels: 5.33 us -> 6.46 us  [call(): pl.pallas_call(kernel, out_shape=out_shape, in_specs=in_specs, out_specs=...]
  transfers between devices with their start and end apart: 15 -> 14, of which waited for: 9 -> 5; matrix products, arithmetic and copies ran while one was open for 2% -> 0% of each run, Pallas kernels for 2% -> 4%
where the time goes in v2:
time: 41.9 us; the launch traced here: 41.6 us
  starting transfers between devices  19.5 us (47%)
  waiting for transfers between devices  10.3 us (25%)
  Pallas kernels  6.46 us (15%)
  local copies, waits for them, and re-layouts  4.5 us (11%)
  between operations  0.73 us (2%)
    ppermute x13, starting transfers between devices, across(): lax.ppermute(block, peers, [(i, i ^ mask) for i in range(lax.axis_size(pe...  19.5 us
    ppermute x13, waiting for transfers between devices, across(): lax.ppermute(block, peers, [(i, i ^ mask) for i in range(lax.axis_size(pe...  10.3 us
    pallas_call x5, Pallas kernels, call(): pl.pallas_call(kernel, out_shape=out_shape, in_specs=in_specs, out_specs=...  6.46 us
    unnamed x12, local copies, waits for them, and re-layouts  4.5 us
  transfers between devices with their start and end apart: 14, of which 5 were waited for; matrix products, arithmetic and copies ran while one was open for 0% of the time, Pallas kernels for 4%

profile of v2, /device:TPU:0, one launch (start us, length us, event | category | flops | bytes accessed | tf_op | source)
XLA Modules:
  0.0 41.6 jit_solution(164096875187086830)
XLA Ops:
  0.6 1.6 %shard_map.102.refs_0_ = bf16[32,2176]{1,0:T(8,128)(2,1)} custom-call(bf16[32,1024]{1,0:T(8,128)(2,1)} %x_ref.1, bf16[32,1024]{1,0:T(8,128)(2,1)} %y_ref.1, s32[8,32]{1,0:T(8,128)} %bitcast.5, s32[8,32]{1,0:T(8,128)} %bitcast.7), custom_call_target="tpu_custom_call" | custom-call | bytes 262144 | tf_op jit(solution)/shard_map/pallas_call | solution.py:134
  2.3 3.1 %collective-permute-start.1 = (bf16[32,2176]{1,0:T(8,128)(2,1)}, bf16[32,2176]{1,0:T(8,128)(2,1)S(1)}, u32[]{:S(2)}, u32[]{:S(2)}) collective-permute-start(bf16[32,2176]{1,0:T(8,128)(2,1)} %shard_map.102.refs_0_), channel_id=1, source_target_pairs={{0,4},{2,6},{4,0},{6,2},{8,12},{10,14},{12,8},{14,10},{1,5},{3,7},... | collective-permute-start | bytes 417800 | tf_op jit(solution)/shard_map/ppermute | solution.py:267
  5.4 2.5 %collective-permute-start = (bf16[32,2176]{1,0:T(8,128)(2,1)}, bf16[32,2176]{1,0:T(8,128)(2,1)S(1)}, u32[]{:S(2)}, u32[]{:S(2)}) collective-permute-start(bf16[32,2176]{1,0:T(8,128)(2,1)} %shard_map.102.refs_0_), channel_id=1, source_target_pairs={{0,12},{2,14},{4,8},{6,10},{8,4},{10,6},{12,0},{14,2},{1,13},{3,15... | collective-permute-start | bytes 417800 | tf_op jit(solution)/shard_map/ppermute | solution.py:267
  7.8 1.0 %collective-permute-start.5 = (bf16[32,2176]{1,0:T(8,128)(2,1)}, bf16[32,2176]{1,0:T(8,128)(2,1)S(1)}, u32[]{:S(2)}, u32[]{:S(2)}) collective-permute-start(bf16[32,2176]{1,0:T(8,128)(2,1)} %shard_map.102.refs_0_), channel_id=1, source_target_pairs={{0,10},{2,8},{4,14},{6,12},{8,2},{10,0},{12,6},{14,4},{1,11},{3,9}... | collective-permute-start | bytes 417800 | tf_op jit(solution)/shard_map/ppermute | solution.py:267
  8.9 0.5 %collective-permute-start.3 = (bf16[32,2176]{1,0:T(8,128)(2,1)}, bf16[32,2176]{1,0:T(8,128)(2,1)S(1)}, u32[]{:S(2)}, u32[]{:S(2)}) collective-permute-start(bf16[32,2176]{1,0:T(8,128)(2,1)} %shard_map.102.refs_0_), channel_id=1, source_target_pairs={{0,2},{2,0},{4,6},{6,4},{8,10},{10,8},{12,14},{14,12},{1,3},{3,1},... | collective-permute-start | bytes 417800 | tf_op jit(solution)/shard_map/ppermute | solution.py:267
  9.4 0.0 collective-permute-done.1.refs_1_
  9.4 1.5 %collective-permute-start.4 = (bf16[32,2176]{1,0:T(8,128)(2,1)S(1)}, bf16[32,2176]{1,0:T(8,128)(2,1)S(1)}, u32[]{:S(2)}, u32[]{:S(2)}) collective-permute-start(bf16[32,2176]{1,0:T(8,128)(2,1)S(1)} %collective-permute-done.1.refs_1_), channel_id=1, source_target_pairs={{0,2},{2,0},{4,6},{6,4},{8,10},{10,8},{12,14},{14,12},{1,3},{3,1},... | collective-permute-start | bytes 417800 | tf_op jit(solution)/shard_map/ppermute | solution.py:267
  10.9 4.8 %collective-permute-done.after_ref.refs_3_ = bf16[32,2176]{1,0:T(8,128)(2,1)S(1)} collective-permute-done((bf16[32,2176]{1,0:T(8,128)(2,1)}, bf16[32,2176]{1,0:T(8,128)(2,1)S(1)}, u32[]{:S(2)}, u32[]{:S(2)}) %collective-permute-start) | collective-permute-done | bytes 139296 | tf_op jit(solution)/shard_map/ppermute | solution.py:267
  15.7 1.5 %collective-permute-start.6 = (bf16[32,2176]{1,0:T(8,128)(2,1)S(1)}, bf16[32,2176]{1,0:T(8,128)(2,1)S(1)}, u32[]{:S(2)}, u32[]{:S(2)}) collective-permute-start(bf16[32,2176]{1,0:T(8,128)(2,1)S(1)} %collective-permute-done.after_ref.refs_3_), channel_id=1, source_target_pairs={{0,2},{2,0},{4,6},{6,4},{8,10},{10,8},{12,14},{14,12},{1,3},{3,1},... | collective-permute-start | bytes 417800 | tf_op jit(solution)/shard_map/ppermute | solution.py:267
  17.2 3.5 %collective-permute-start.2 = (bf16[32,2176]{1,0:T(8,128)(2,1)S(1)}, bf16[32,2176]{1,0:T(8,128)(2,1)S(1)}, u32[]{:S(2)}, u32[]{:S(2)}) collective-permute-start(bf16[32,2176]{1,0:T(8,128)(2,1)S(1)} %collective-permute-done.after_ref.refs_3_), channel_id=1, source_target_pairs={{0,4},{2,6},{4,0},{6,2},{8,12},{10,14},{12,8},{14,10},{1,5},{3,7},... | collective-permute-start | bytes 417800 | tf_op jit(solution)/shard_map/ppermute | solution.py:267
  20.7 0.1 pad_add_fusion.place_ref
  20.7 1.1 %copy-done = bf16[1,1024,384]{2,1,0:T(8,128)(2,1)S(1)} copy-done((bf16[1,1024,384]{2,1,0:T(8,128)(2,1)S(1)}, bf16[1,1024,384]{2,1,0:T(8,128)(2,1)}, u32[]{:S(2)}) %copy-start) | copy-done | bytes 786456
  21.9 1.1 %copy-done.2 = bf16[1,1024,384]{2,1,0:T(8,128)(2,1)S(1)} copy-done((bf16[1,1024,384]{2,1,0:T(8,128)(2,1)S(1)}, bf16[1,1024,384]{2,1,0:T(8,128)(2,1)}, u32[]{:S(2)}) %copy-start.2) | copy-done | bytes 786456
  23.0 1.1 %copy-done.3 = bf16[1,384,1024]{2,1,0:T(8,128)(2,1)S(1)} copy-done((bf16[1,384,1024]{2,1,0:T(8,128)(2,1)S(1)}, bf16[1,384,1024]{2,1,0:T(8,128)(2,1)}, u32[]{:S(2)}) %copy-start.3) | copy-done | bytes 786456
  24.2 0.0 collective-permute-done.3.refs_4_
  24.2 0.0 collective-permute-done.6.refs_7_
  24.2 1.1 %copy-done.1 = bf16[1,1024,384]{2,1,0:T(8,128)(2,1)S(1)} copy-done((bf16[1,1024,384]{2,1,0:T(8,128)(2,1)S(1)}, bf16[1,1024,384]{2,1,0:T(8,128)(2,1)}, u32[]{:S(2)}) %copy-start.1) | copy-done | bytes 786456
  25.3 0.0 copy-done.4
  25.3 2.2 %shard_map.104 = (bf16[32,1152]{1,0:T(8,128)(2,1)S(1)}, bf16[32,1152]{1,0:T(8,128)(2,1)S(1)}, bf16[32,1152]{1,0:T(8,128)(2,1)S(1)}, bf16[32,1152]{1,0:T(8,128)(2...) custom-call(s32[2]{0:T(128)S(1)} %pad_add_fusion.place_ref, ...), custom_call_target="tpu_custom_call" | custom-call | flops 1006632960 | bytes 4456448 | tf_op jit(solution)/shard_map/pallas_call | solution.py:134
  27.5 0.1 collective-permute-start.10
  27.6 2.0 %collective-permute-start.12 = (bf16[32,1152]{1,0:T(8,128)(2,1)S(1)}, bf16[32,1152]{1,0:T(8,128)(2,1)S(1)}, u32[]{:S(2)}, u32[]{:S(2)}) collective-permute-start(bf16[32,1152]{1,0:T(8,128)(2,1)S(1)} %get-tuple-element.27), channel_id=1, source_target_pairs={{0,2},{2,0},{4,6},{6,4},{8,10},{10,8},{12,14},{14,12},{1,3},{3,1},... | collective-permute-start | bytes 221192 | tf_op jit(solution)/shard_map/ppermute | solution.py:267
  29.6 0.1 collective-permute-start.8
  29.7 2.2 %collective-permute-done.10 = bf16[32,1152]{1,0:T(8,128)(2,1)S(1)} collective-permute-done((bf16[32,1152]{1,0:T(8,128)(2,1)S(1)}, bf16[32,1152]{1,0:T(8,128)(2,1)S(1)}, u32[]{:S(2)}, u32[]{:S(2)}) %collective-permute-start.10) | collective-permute-done | bytes 73760 | tf_op jit(solution)/shard_map/ppermute | solution.py:267
  32.0 1.8 %collective-permute-start.11 = (bf16[32,1152]{1,0:T(8,128)(2,1)S(1)}, bf16[32,1152]{1,0:T(8,128)(2,1)S(1)}, u32[]{:S(2)}, u32[]{:S(2)}) collective-permute-start(bf16[32,1152]{1,0:T(8,128)(2,1)S(1)} %add_convert_fusion.1), channel_id=1, source_target_pairs={{0,8},{2,10},{4,12},{6,14},{8,0},{10,2},{12,4},{14,6},{1,9},{3,11}... | collective-permute-start | bytes 221192 | tf_op jit(solution)/shard_map/ppermute | solution.py:267
  33.8 1.8 %collective-permute-start.13 = (bf16[32,1152]{1,0:T(8,128)(2,1)S(1)}, bf16[32,1152]{1,0:T(8,128)(2,1)S(1)}, u32[]{:S(2)}, u32[]{:S(2)}) collective-permute-start(bf16[32,1152]{1,0:T(8,128)(2,1)S(1)} %add_convert_fusion), channel_id=1, source_target_pairs={{0,12},{2,14},{4,8},{6,10},{8,4},{10,6},{12,0},{14,2},{1,13},{3,15... | collective-permute-start | bytes 221192 | tf_op jit(solution)/shard_map/ppermute | solution.py:267
  35.6 0.1 collective-permute-start.9
  35.7 0.0 copy-start.5
  35.7 1.8 %shard_map.105 = (f32[1,512,384]{2,1,0:T(8,128)}, f32[1,512,384]{2,1,0:T(8,128)}, f32[8,128]{1,0:T(8,128)S(1)}) custom-call(bf16[256,512]{1,0:T(8,128)(2,1)S(1)} %get-tuple-element.18.keep_ref, bf16[256,1280]{1,0:T(8,128)(2,1)S(1)} %get-tuple-element.19.own_ref, bf16[256,1280]{1,0:T(8,128)(2,1)S(1)} %collective-permute-done.7.other_ref), custom_call_target="tpu_custom_call" | custom-call | flops 402653184 | bytes 2228224 | tf_op jit(solution)/shard_map/pallas_call | solution.py:134
  37.5 1.5 %collective-permute-done.11.refs_3_ = bf16[32,1152]{1,0:T(8,128)(2,1)S(1)} collective-permute-done((bf16[32,1152]{1,0:T(8,128)(2,1)S(1)}, bf16[32,1152]{1,0:T(8,128)(2,1)S(1)}, u32[]{:S(2)}, u32[]{:S(2)}) %collective-permute-start.11) | collective-permute-done | bytes 73760 | tf_op jit(solution)/shard_map/ppermute | solution.py:267
  39.0 1.1 %collective-permute-done.13.refs_4_ = bf16[32,1152]{1,0:T(8,128)(2,1)S(1)} collective-permute-done((bf16[32,1152]{1,0:T(8,128)(2,1)S(1)}, bf16[32,1152]{1,0:T(8,128)(2,1)S(1)}, u32[]{:S(2)}, u32[]{:S(2)}) %collective-permute-start.13) | collective-permute-done | bytes 73760 | tf_op jit(solution)/shard_map/ppermute | solution.py:267
  40.2 0.6 %collective-permute-done.9.refs_2_ = bf16[32,1152]{1,0:T(8,128)(2,1)S(1)} collective-permute-done((bf16[32,1152]{1,0:T(8,128)(2,1)S(1)}, bf16[32,1152]{1,0:T(8,128)(2,1)S(1)}, u32[]{:S(2)}, u32[]{:S(2)}) %collective-permute-start.9) | collective-permute-done | bytes 73760 | tf_op jit(solution)/shard_map/ppermute | solution.py:267
  40.8 0.8 %shard_map.106 = (bf16[32,1024]{1,0:T(8,128)(2,1)}, f32[8,32]{1,0:T(8,128)}) custom-call(s32[8,32]{1,0:T(8,128)S(1)} %bitcast.6, f32[8,128]{1,0:T(8,128)S(1)} %get-tuple-element.20.done_ref, bf16[32,1152]{1,0:T(8,128)(2,1)S(1)} %get-tuple-element.21.refs_0_, bf16[32,1152]{1,0:T(8,128)(2,1)S(1)} %slice.8.refs_1_, ...), custom_call_target="tpu_custom_call" | custom-call | bytes 393216 | tf_op jit(solution)/shard_map/pallas_call | solution.py:134
  (18 shorter events, 0.1 us)
Async XLA Ops:
  2.3 7.1 %collective-permute-start.1 = (bf16[32,2176]{1,0:T(8,128)(2,1)}, bf16[32,2176]{1,0:T(8,128)(2,1)S(1)}, u32[]{:S(2)}, u32[]{:S(2)}) collective-permute-start(bf16[32,2176]{1,0:T(8,128)(2,1)} %shard_map.102.refs_0_), channel_id=1, source_target_pairs={{0,4},{2,6},{4,0},{6,2},{8,12},{10,14},{12,8},{14,10},{1,5},{3,7},... | collective-permute-start | bytes 417800 | tf_op jit(solution)/shard_map/ppermute | solution.py:267
  5.4 10.3 %collective-permute-start = (bf16[32,2176]{1,0:T(8,128)(2,1)}, bf16[32,2176]{1,0:T(8,128)(2,1)S(1)}, u32[]{:S(2)}, u32[]{:S(2)}) collective-permute-start(bf16[32,2176]{1,0:T(8,128)(2,1)} %shard_map.102.refs_0_), channel_id=1, source_target_pairs={{0,12},{2,14},{4,8},{6,10},{8,4},{10,6},{12,0},{14,2},{1,13},{3,15... | collective-permute-start | bytes 417800 | tf_op jit(solution)/shard_map/ppermute | solution.py:267
  7.8 16.3 %collective-permute-start.5 = (bf16[32,2176]{1,0:T(8,128)(2,1)}, bf16[32,2176]{1,0:T(8,128)(2,1)S(1)}, u32[]{:S(2)}, u32[]{:S(2)}) collective-permute-start(bf16[32,2176]{1,0:T(8,128)(2,1)} %shard_map.102.refs_0_), channel_id=1, source_target_pairs={{0,10},{2,8},{4,14},{6,12},{8,2},{10,0},{12,6},{14,4},{1,11},{3,9}... | collective-permute-start | bytes 417800 | tf_op jit(solution)/shard_map/ppermute | solution.py:267
  8.9 15.3 %collective-permute-start.3 = (bf16[32,2176]{1,0:T(8,128)(2,1)}, bf16[32,2176]{1,0:T(8,128)(2,1)S(1)}, u32[]{:S(2)}, u32[]{:S(2)}) collective-permute-start(bf16[32,2176]{1,0:T(8,128)(2,1)} %shard_map.102.refs_0_), channel_id=1, source_target_pairs={{0,2},{2,0},{4,6},{6,4},{8,10},{10,8},{12,14},{14,12},{1,3},{3,1},... | collective-permute-start | bytes 417800 | tf_op jit(solution)/shard_map/ppermute | solution.py:267
  9.4 14.7 %collective-permute-start.4 = (bf16[32,2176]{1,0:T(8,128)(2,1)S(1)}, bf16[32,2176]{1,0:T(8,128)(2,1)S(1)}, u32[]{:S(2)}, u32[]{:S(2)}) collective-permute-start(bf16[32,2176]{1,0:T(8,128)(2,1)S(1)} %collective-permute-done.1.refs_1_), channel_id=1, source_target_pairs={{0,2},{2,0},{4,6},{6,4},{8,10},{10,8},{12,14},{14,12},{1,3},{3,1},... | collective-permute-start | bytes 417800 | tf_op jit(solution)/shard_map/ppermute | solution.py:267
  15.7 8.5 %collective-permute-start.6 = (bf16[32,2176]{1,0:T(8,128)(2,1)S(1)}, bf16[32,2176]{1,0:T(8,128)(2,1)S(1)}, u32[]{:S(2)}, u32[]{:S(2)}) collective-permute-start(bf16[32,2176]{1,0:T(8,128)(2,1)S(1)} %collective-permute-done.after_ref.refs_3_), channel_id=1, source_target_pairs={{0,2},{2,0},{4,6},{6,4},{8,10},{10,8},{12,14},{14,12},{1,3},{3,1},... | collective-permute-start | bytes 417800 | tf_op jit(solution)/shard_map/ppermute | solution.py:267
  17.2 7.0 %collective-permute-start.2 = (bf16[32,2176]{1,0:T(8,128)(2,1)S(1)}, bf16[32,2176]{1,0:T(8,128)(2,1)S(1)}, u32[]{:S(2)}, u32[]{:S(2)}) collective-permute-start(bf16[32,2176]{1,0:T(8,128)(2,1)S(1)} %collective-permute-done.after_ref.refs_3_), channel_id=1, source_target_pairs={{0,4},{2,6},{4,0},{6,2},{8,12},{10,14},{12,8},{14,10},{1,5},{3,7},... | collective-permute-start | bytes 417800 | tf_op jit(solution)/shard_map/ppermute | solution.py:267
  20.7 1.1 %copy-start = (bf16[1,1024,384]{2,1,0:T(8,128)(2,1)S(1)}, bf16[1,1024,384]{2,1,0:T(8,128)(2,1)}, u32[]{:S(2)}) copy-start(bf16[1,1024,384]{2,1,0:T(8,128)(2,1)} %refs_8_.1) | copy-start | bytes 2359300
  21.9 1.1 %copy-start.2 = (bf16[1,1024,384]{2,1,0:T(8,128)(2,1)S(1)}, bf16[1,1024,384]{2,1,0:T(8,128)(2,1)}, u32[]{:S(2)}) copy-start(bf16[1,1024,384]{2,1,0:T(8,128)(2,1)} %refs_9_.1) | copy-start | bytes 2359300
  23.0 1.1 %copy-start.3 = (bf16[1,384,1024]{2,1,0:T(8,128)(2,1)S(1)}, bf16[1,384,1024]{2,1,0:T(8,128)(2,1)}, u32[]{:S(2)}) copy-start(bf16[1,384,1024]{2,1,0:T(8,128)(2,1)} %refs_10_.1) | copy-start | bytes 2359300
  24.1 1.1 %copy-start.1 = (bf16[1,1024,384]{2,1,0:T(8,128)(2,1)S(1)}, bf16[1,1024,384]{2,1,0:T(8,128)(2,1)}, u32[]{:S(2)}) copy-start(bf16[1,1024,384]{2,1,0:T(8,128)(2,1)} %refs_8_.1) | copy-start | bytes 2359300
  24.1 1.1 %copy-start.4 = (bf16[32,2176]{1,0:T(8,128)(2,1)S(1)}, bf16[32,2176]{1,0:T(8,128)(2,1)}, u32[]{:S(2)}) copy-start(bf16[32,2176]{1,0:T(8,128)(2,1)} %shard_map.102.refs_0_) | copy-start | bytes 417796
  27.5 4.4 %collective-permute-start.10 = (bf16[32,1152]{1,0:T(8,128)(2,1)S(1)}, bf16[32,1152]{1,0:T(8,128)(2,1)S(1)}, u32[]{:S(2)}, u32[]{:S(2)}) collective-permute-start(bf16[32,1152]{1,0:T(8,128)(2,1)S(1)} %get-tuple-element.25), channel_id=1, source_target_pairs={{0,2},{2,0},{4,6},{6,4},{8,10},{10,8},{12,14},{14,12},{1,3},{3,1},... | collective-permute-start | bytes 221192 | tf_op jit(solution)/shard_map/ppermute | solution.py:267
  27.6 6.1 %collective-permute-start.12 = (bf16[32,1152]{1,0:T(8,128)(2,1)S(1)}, bf16[32,1152]{1,0:T(8,128)(2,1)S(1)}, u32[]{:S(2)}, u32[]{:S(2)}) collective-permute-start(bf16[32,1152]{1,0:T(8,128)(2,1)S(1)} %get-tuple-element.27), channel_id=1, source_target_pairs={{0,2},{2,0},{4,6},{6,4},{8,10},{10,8},{12,14},{14,12},{1,3},{3,1},... | collective-permute-start | bytes 221192 | tf_op jit(solution)/shard_map/ppermute | solution.py:267
  29.6 5.9 %collective-permute-start.8 = (bf16[64,1152]{1,0:T(8,128)(2,1)S(1)}, bf16[64,1152]{1,0:T(8,128)(2,1)S(1)}, u32[]{:S(2)}, u32[]{:S(2)}) collective-permute-start(bf16[64,1152]{1,0:T(8,128)(2,1)S(1)} %get-tuple-element.22), channel_id=1, source_target_pairs={{0,2},{2,0},{4,6},{6,4},{8,10},{10,8},{12,14},{14,12},{1,3},{3,1},... | collective-permute-start | bytes 442376 | tf_op jit(solution)/shard_map/ppermute | solution.py:267
  29.7 6.0 %collective-permute-start.7 = (bf16[256,1280]{1,0:T(8,128)(2,1)S(1)}, bf16[256,1280]{1,0:T(8,128)(2,1)S(1)}, u32[]{:S(2)}, u32[]{:S(2)}) collective-permute-start(bf16[256,1280]{1,0:T(8,128)(2,1)S(1)} %get-tuple-element.19.own_ref), channel_id=1, source_target_pairs={{0,1},{1,0},{2,3},{3,2},{4,5},{5,4},{6,7},{7,6},{8,9},{9,8},{10,11... | collective-permute-start | bytes 1966088 | tf_op jit(solution)/shard_map/ppermute | solution.py:271
  32.0 7.1 %collective-permute-start.11 = (bf16[32,1152]{1,0:T(8,128)(2,1)S(1)}, bf16[32,1152]{1,0:T(8,128)(2,1)S(1)}, u32[]{:S(2)}, u32[]{:S(2)}) collective-permute-start(bf16[32,1152]{1,0:T(8,128)(2,1)S(1)} %add_convert_fusion.1), channel_id=1, source_target_pairs={{0,8},{2,10},{4,12},{6,14},{8,0},{10,2},{12,4},{14,6},{1,9},{3,11}... | collective-permute-start | bytes 221192 | tf_op jit(solution)/shard_map/ppermute | solution.py:267
  33.8 6.4 %collective-permute-start.13 = (bf16[32,1152]{1,0:T(8,128)(2,1)S(1)}, bf16[32,1152]{1,0:T(8,128)(2,1)S(1)}, u32[]{:S(2)}, u32[]{:S(2)}) collective-permute-start(bf16[32,1152]{1,0:T(8,128)(2,1)S(1)} %add_convert_fusion), channel_id=1, source_target_pairs={{0,12},{2,14},{4,8},{6,10},{8,4},{10,6},{12,0},{14,2},{1,13},{3,15... | collective-permute-start | bytes 221192 | tf_op jit(solution)/shard_map/ppermute | solution.py:267
  35.6 5.2 %collective-permute-start.9 = (bf16[32,1152]{1,0:T(8,128)(2,1)S(1)}, bf16[32,1152]{1,0:T(8,128)(2,1)S(1)}, u32[]{:S(2)}, u32[]{:S(2)}) collective-permute-start(bf16[32,1152]{1,0:T(8,128)(2,1)S(1)} %add_convert_fusion.2), channel_id=1, source_target_pairs={{0,4},{2,6},{4,0},{6,2},{8,12},{10,14},{12,8},{14,10},{1,5},{3,7},... | collective-permute-start | bytes 221192 | tf_op jit(solution)/shard_map/ppermute | solution.py:267
  35.7 5.0 %copy-start.5 = (s32[32,8]{0,1:T(8,128)S(1)}, s32[32,8]{0,1:T(8,128)}, u32[]{:S(2)}) copy-start(s32[32,8]{0,1:T(8,128)} %param.9) | copy-start | bytes 3076

commit v3 on v2

--- a/solution.py
+++ b/solution.py
@@ -315,7 +315,7 @@
     touched = call(
         touch_kernel,
         jax.ShapeDtypeStruct((8, LANES), f32),
-        z3,
+        x0,
         w_gate,
         w_up,
         w_down,

time: 41.9 us -> 40 us (0.955)
  waiting for transfers between devices: 10.3 us -> 8.11 us
  starting transfers between devices: 19.5 us -> 20.8 us
  local copies, waits for them, and re-layouts: 4.5 us -> 3.42 us
    ppermute x13, waiting for transfers between devices: 10.3 us -> 8.11 us  [across(): lax.ppermute(block, peers, [(i, i ^ mask) for i in range(lax.axis_size(pe...]
    ppermute x13, starting transfers between devices: 19.5 us -> 20.8 us  [across(): lax.ppermute(block, peers, [(i, i ^ mask) for i in range(lax.axis_size(pe...]
    unnamed x12, local copies, waits for them, and re-layouts: 4.5 us -> 3.41 us
where the time goes in v3:
time: 40 us; the launch traced here: 39.7 us
  starting transfers between devices  20.8 us (52%)
  waiting for transfers between devices  8.11 us (20%)
  Pallas kernels  6.46 us (16%)
  local copies, waits for them, and re-layouts  3.42 us (9%)
  between operations  0.73 us (2%)
    ppermute x13, starting transfers between devices, across(): lax.ppermute(block, peers, [(i, i ^ mask) for i in range(lax.axis_size(pe...  20.8 us
    ppermute x13, waiting for transfers between devices, across(): lax.ppermute(block, peers, [(i, i ^ mask) for i in range(lax.axis_size(pe...  8.11 us
    pallas_call x5, Pallas kernels, call(): pl.pallas_call(kernel, out_shape=out_shape, in_specs=in_specs, out_specs=...  6.46 us
    unnamed x12, local copies, waits for them, and re-layouts  3.41 us
  transfers between devices with their start and end apart: 14, of which 5 were waited for; matrix products, arithmetic and copies ran while one was open for 0% of the time, Pallas kernels for 4%

profile of v3, /device:TPU:0, one launch (start us, length us, event | category | flops | bytes accessed | tf_op | source)
XLA Modules:
  0.0 39.7 jit_solution(14477561389231216277)
XLA Ops:
  0.6 1.6 %shard_map.102.refs_0_ = bf16[32,2176]{1,0:T(8,128)(2,1)} custom-call(bf16[32,1024]{1,0:T(8,128)(2,1)} %x_ref.1, bf16[32,1024]{1,0:T(8,128)(2,1)} %y_ref.1, s32[8,32]{1,0:T(8,128)} %bitcast.5, s32[8,32]{1,0:T(8,128)} %bitcast.7), custom_call_target="tpu_custom_call" | custom-call | bytes 262144 | tf_op jit(solution)/shard_map/pallas_call | solution.py:134
  2.3 5.1 %collective-permute-start.2 = (bf16[32,2176]{1,0:T(8,128)(2,1)}, bf16[32,2176]{1,0:T(8,128)(2,1)S(1)}, u32[]{:S(2)}, u32[]{:S(2)}) collective-permute-start(bf16[32,2176]{1,0:T(8,128)(2,1)} %shard_map.102.refs_0_), channel_id=1, source_target_pairs={{0,12},{2,14},{4,8},{6,10},{8,4},{10,6},{12,0},{14,2},{1,13},{3,15... | collective-permute-start | bytes 417800 | tf_op jit(solution)/shard_map/ppermute | solution.py:267
  7.4 0.0 collective-permute-start.1
  7.4 1.5 %collective-permute-start = (bf16[32,2176]{1,0:T(8,128)(2,1)}, bf16[32,2176]{1,0:T(8,128)(2,1)S(1)}, u32[]{:S(2)}, u32[]{:S(2)}) collective-permute-start(bf16[32,2176]{1,0:T(8,128)(2,1)} %shard_map.102.refs_0_), channel_id=1, source_target_pairs={{0,2},{2,0},{4,6},{6,4},{8,10},{10,8},{12,14},{14,12},{1,3},{3,1},... | collective-permute-start | bytes 417800 | tf_op jit(solution)/shard_map/ppermute | solution.py:267
  8.9 0.6 %collective-permute-start.5 = (bf16[32,2176]{1,0:T(8,128)(2,1)}, bf16[32,2176]{1,0:T(8,128)(2,1)S(1)}, u32[]{:S(2)}, u32[]{:S(2)}) collective-permute-start(bf16[32,2176]{1,0:T(8,128)(2,1)} %shard_map.102.refs_0_), channel_id=1, source_target_pairs={{0,10},{2,8},{4,14},{6,12},{8,2},{10,0},{12,6},{14,4},{1,11},{3,9}... | collective-permute-start | bytes 417800 | tf_op jit(solution)/shard_map/ppermute | solution.py:267
  9.5 2.7 %collective-permute-done.2.refs_3_ = bf16[32,2176]{1,0:T(8,128)(2,1)S(1)} collective-permute-done((bf16[32,2176]{1,0:T(8,128)(2,1)}, bf16[32,2176]{1,0:T(8,128)(2,1)S(1)}, u32[]{:S(2)}, u32[]{:S(2)}) %collective-permute-start.2) | collective-permute-done | bytes 139296 | tf_op jit(solution)/shard_map/ppermute | solution.py:267
  12.2 1.7 %collective-permute-start.6 = (bf16[32,2176]{1,0:T(8,128)(2,1)S(1)}, bf16[32,2176]{1,0:T(8,128)(2,1)S(1)}, u32[]{:S(2)}, u32[]{:S(2)}) collective-permute-start(bf16[32,2176]{1,0:T(8,128)(2,1)S(1)} %collective-permute-done.2.refs_3_), channel_id=1, source_target_pairs={{0,2},{2,0},{4,6},{6,4},{8,10},{10,8},{12,14},{14,12},{1,3},{3,1},... | collective-permute-start | bytes 417800 | tf_op jit(solution)/shard_map/ppermute | solution.py:267
  13.8 3.6 %collective-permute-start.3 = (bf16[32,2176]{1,0:T(8,128)(2,1)S(1)}, bf16[32,2176]{1,0:T(8,128)(2,1)S(1)}, u32[]{:S(2)}, u32[]{:S(2)}) collective-permute-start(bf16[32,2176]{1,0:T(8,128)(2,1)S(1)} %collective-permute-done.2.refs_3_), channel_id=1, source_target_pairs={{0,4},{2,6},{4,0},{6,2},{8,12},{10,14},{12,8},{14,10},{1,5},{3,7},... | collective-permute-start | bytes 417800 | tf_op jit(solution)/shard_map/ppermute | solution.py:267
  17.5 0.0 collective-permute-done.1.refs_1_
  17.5 0.3 collective-permute-start.4
  17.8 0.1 pad_add_fusion.place_ref
  17.9 0.0 collective-permute-done.after_ref.refs_4_
  17.9 1.1 %copy-done = bf16[1,1024,384]{2,1,0:T(8,128)(2,1)S(1)} copy-done((bf16[1,1024,384]{2,1,0:T(8,128)(2,1)S(1)}, bf16[1,1024,384]{2,1,0:T(8,128)(2,1)}, u32[]{:S(2)}) %copy-start) | copy-done | bytes 786456
  19.0 1.1 %copy-done.2 = bf16[1,1024,384]{2,1,0:T(8,128)(2,1)S(1)} copy-done((bf16[1,1024,384]{2,1,0:T(8,128)(2,1)S(1)}, bf16[1,1024,384]{2,1,0:T(8,128)(2,1)}, u32[]{:S(2)}) %copy-start.2) | copy-done | bytes 786456
  20.2 1.1 %copy-done.3 = bf16[1,384,1024]{2,1,0:T(8,128)(2,1)S(1)} copy-done((bf16[1,384,1024]{2,1,0:T(8,128)(2,1)S(1)}, bf16[1,384,1024]{2,1,0:T(8,128)(2,1)}, u32[]{:S(2)}) %copy-start.3) | copy-done | bytes 786456
  21.3 0.0 collective-permute-done.5.refs_6_
  21.3 0.0 collective-permute-done.6.refs_7_
  21.3 1.2 %collective-permute-done.4.refs_5_ = bf16[32,2176]{1,0:T(8,128)(2,1)S(1)} collective-permute-done((bf16[32,2176]{1,0:T(8,128)(2,1)S(1)}, bf16[32,2176]{1,0:T(8,128)(2,1)S(1)}, u32[]{:S(2)}, u32[]{:S(2)}) %collective-permute-start.4) | collective-permute-done | bytes 139296 | tf_op jit(solution)/shard_map/ppermute | solution.py:267
  22.5 2.2 %shard_map.104 = (bf16[32,1152]{1,0:T(8,128)(2,1)S(1)}, bf16[32,1152]{1,0:T(8,128)(2,1)S(1)}, bf16[32,1152]{1,0:T(8,128)(2,1)S(1)}, bf16[32,1152]{1,0:T(8,128)(2...) custom-call(s32[2]{0:T(128)S(1)} %pad_add_fusion.place_ref, ...), custom_call_target="tpu_custom_call" | custom-call | flops 1006632960 | bytes 4456448 | tf_op jit(solution)/shard_map/pallas_call | solution.py:134
  24.8 1.7 %collective-permute-start.10 = (bf16[32,1152]{1,0:T(8,128)(2,1)S(1)}, bf16[32,1152]{1,0:T(8,128)(2,1)S(1)}, u32[]{:S(2)}, u32[]{:S(2)}) collective-permute-start(bf16[32,1152]{1,0:T(8,128)(2,1)S(1)} %get-tuple-element.25), channel_id=1, source_target_pairs={{0,2},{2,0},{4,6},{6,4},{8,10},{10,8},{12,14},{14,12},{1,3},{3,1},... | collective-permute-start | bytes 221192 | tf_op jit(solution)/shard_map/ppermute | solution.py:267
  26.4 0.4 %collective-permute-start.12 = (bf16[32,1152]{1,0:T(8,128)(2,1)S(1)}, bf16[32,1152]{1,0:T(8,128)(2,1)S(1)}, u32[]{:S(2)}, u32[]{:S(2)}) collective-permute-start(bf16[32,1152]{1,0:T(8,128)(2,1)S(1)} %get-tuple-element.27), channel_id=1, source_target_pairs={{0,2},{2,0},{4,6},{6,4},{8,10},{10,8},{12,14},{14,12},{1,3},{3,1},... | collective-permute-start | bytes 221192 | tf_op jit(solution)/shard_map/ppermute | solution.py:267
  26.9 1.6 %collective-permute-start.8 = (bf16[64,1152]{1,0:T(8,128)(2,1)S(1)}, bf16[64,1152]{1,0:T(8,128)(2,1)S(1)}, u32[]{:S(2)}, u32[]{:S(2)}) collective-permute-start(bf16[64,1152]{1,0:T(8,128)(2,1)S(1)} %get-tuple-element.22), channel_id=1, source_target_pairs={{0,2},{2,0},{4,6},{6,4},{8,10},{10,8},{12,14},{14,12},{1,3},{3,1},... | collective-permute-start | bytes 442376 | tf_op jit(solution)/shard_map/ppermute | solution.py:267
  28.5 1.5 %collective-permute-done.10 = bf16[32,1152]{1,0:T(8,128)(2,1)S(1)} collective-permute-done((bf16[32,1152]{1,0:T(8,128)(2,1)S(1)}, bf16[32,1152]{1,0:T(8,128)(2,1)S(1)}, u32[]{:S(2)}, u32[]{:S(2)}) %collective-permute-start.10) | collective-permute-done | bytes 73760 | tf_op jit(solution)/shard_map/ppermute | solution.py:267
  30.0 1.7 %collective-permute-start.11 = (bf16[32,1152]{1,0:T(8,128)(2,1)S(1)}, bf16[32,1152]{1,0:T(8,128)(2,1)S(1)}, u32[]{:S(2)}, u32[]{:S(2)}) collective-permute-start(bf16[32,1152]{1,0:T(8,128)(2,1)S(1)} %add_convert_fusion.1), channel_id=1, source_target_pairs={{0,8},{2,10},{4,12},{6,14},{8,0},{10,2},{12,4},{14,6},{1,9},{3,11}... | collective-permute-start | bytes 221192 | tf_op jit(solution)/shard_map/ppermute | solution.py:267
  31.7 0.0 collective-permute-done.12
  31.7 2.6 %collective-permute-start.13 = (bf16[32,1152]{1,0:T(8,128)(2,1)S(1)}, bf16[32,1152]{1,0:T(8,128)(2,1)S(1)}, u32[]{:S(2)}, u32[]{:S(2)}) collective-permute-start(bf16[32,1152]{1,0:T(8,128)(2,1)S(1)} %add_convert_fusion), channel_id=1, source_target_pairs={{0,12},{2,14},{4,8},{6,10},{8,4},{10,6},{12,0},{14,2},{1,13},{3,15... | collective-permute-start | bytes 221192 | tf_op jit(solution)/shard_map/ppermute | solution.py:267
  34.3 0.1 collective-permute-start.9
  34.4 0.0 copy-start.5
  34.4 1.8 %shard_map.105 = (f32[1,512,384]{2,1,0:T(8,128)}, f32[1,512,384]{2,1,0:T(8,128)}, f32[8,128]{1,0:T(8,128)S(1)}) custom-call(bf16[256,512]{1,0:T(8,128)(2,1)S(1)} %get-tuple-element.18.keep_ref, bf16[256,1280]{1,0:T(8,128)(2,1)S(1)} %get-tuple-element.19.own_ref, bf16[256,1280]{1,0:T(8,128)(2,1)S(1)} %collective-permute-done.7.other_ref), custom_call_target="tpu_custom_call" | custom-call | flops 402653184 | bytes 2228224 | tf_op jit(solution)/shard_map/pallas_call | solution.py:134
  36.2 1.9 %collective-permute-done.11.refs_3_ = bf16[32,1152]{1,0:T(8,128)(2,1)S(1)} collective-permute-done((bf16[32,1152]{1,0:T(8,128)(2,1)S(1)}, bf16[32,1152]{1,0:T(8,128)(2,1)S(1)}, u32[]{:S(2)}, u32[]{:S(2)}) %collective-permute-start.11) | collective-permute-done | bytes 73760 | tf_op jit(solution)/shard_map/ppermute | solution.py:267
  38.1 0.8 %collective-permute-done.9.refs_2_ = bf16[32,1152]{1,0:T(8,128)(2,1)S(1)} collective-permute-done((bf16[32,1152]{1,0:T(8,128)(2,1)S(1)}, bf16[32,1152]{1,0:T(8,128)(2,1)S(1)}, u32[]{:S(2)}, u32[]{:S(2)}) %collective-permute-start.9) | collective-permute-done | bytes 73760 | tf_op jit(solution)/shard_map/ppermute | solution.py:267
  38.9 0.8 %shard_map.106 = (bf16[32,1024]{1,0:T(8,128)(2,1)}, f32[8,32]{1,0:T(8,128)}) custom-call(s32[8,32]{1,0:T(8,128)S(1)} %bitcast.6, f32[8,128]{1,0:T(8,128)S(1)} %get-tuple-element.20.done_ref, bf16[32,1152]{1,0:T(8,128)(2,1)S(1)} %get-tuple-element.21.refs_0_, bf16[32,1152]{1,0:T(8,128)(2,1)S(1)} %slice.8.refs_1_, ...), custom_call_target="tpu_custom_call" | custom-call | bytes 393216 | tf_op jit(solution)/shard_map/pallas_call | solution.py:134
  (18 shorter events, 0.1 us)
Async XLA Ops:
  2.3 9.9 %collective-permute-start.2 = (bf16[32,2176]{1,0:T(8,128)(2,1)}, bf16[32,2176]{1,0:T(8,128)(2,1)S(1)}, u32[]{:S(2)}, u32[]{:S(2)}) collective-permute-start(bf16[32,2176]{1,0:T(8,128)(2,1)} %shard_map.102.refs_0_), channel_id=1, source_target_pairs={{0,12},{2,14},{4,8},{6,10},{8,4},{10,6},{12,0},{14,2},{1,13},{3,15... | collective-permute-start | bytes 417800 | tf_op jit(solution)/shard_map/ppermute | solution.py:267
  7.4 10.1 %collective-permute-start.1 = (bf16[32,2176]{1,0:T(8,128)(2,1)}, bf16[32,2176]{1,0:T(8,128)(2,1)S(1)}, u32[]{:S(2)}, u32[]{:S(2)}) collective-permute-start(bf16[32,2176]{1,0:T(8,128)(2,1)} %shard_map.102.refs_0_), channel_id=1, source_target_pairs={{0,4},{2,6},{4,0},{6,2},{8,12},{10,14},{12,8},{14,10},{1,5},{3,7},... | collective-permute-start | bytes 417800 | tf_op jit(solution)/shard_map/ppermute | solution.py:267
  7.4 10.5 %collective-permute-start = (bf16[32,2176]{1,0:T(8,128)(2,1)}, bf16[32,2176]{1,0:T(8,128)(2,1)S(1)}, u32[]{:S(2)}, u32[]{:S(2)}) collective-permute-start(bf16[32,2176]{1,0:T(8,128)(2,1)} %shard_map.102.refs_0_), channel_id=1, source_target_pairs={{0,2},{2,0},{4,6},{6,4},{8,10},{10,8},{12,14},{14,12},{1,3},{3,1},... | collective-permute-start | bytes 417800 | tf_op jit(solution)/shard_map/ppermute | solution.py:267
  8.9 12.4 %collective-permute-start.5 = (bf16[32,2176]{1,0:T(8,128)(2,1)}, bf16[32,2176]{1,0:T(8,128)(2,1)S(1)}, u32[]{:S(2)}, u32[]{:S(2)}) collective-permute-start(bf16[32,2176]{1,0:T(8,128)(2,1)} %shard_map.102.refs_0_), channel_id=1, source_target_pairs={{0,10},{2,8},{4,14},{6,12},{8,2},{10,0},{12,6},{14,4},{1,11},{3,9}... | collective-permute-start | bytes 417800 | tf_op jit(solution)/shard_map/ppermute | solution.py:267
  12.2 9.2 %collective-permute-start.6 = (bf16[32,2176]{1,0:T(8,128)(2,1)S(1)}, bf16[32,2176]{1,0:T(8,128)(2,1)S(1)}, u32[]{:S(2)}, u32[]{:S(2)}) collective-permute-start(bf16[32,2176]{1,0:T(8,128)(2,1)S(1)} %collective-permute-done.2.refs_3_), channel_id=1, source_target_pairs={{0,2},{2,0},{4,6},{6,4},{8,10},{10,8},{12,14},{14,12},{1,3},{3,1},... | collective-permute-start | bytes 417800 | tf_op jit(solution)/shard_map/ppermute | solution.py:267
  13.8 7.5 %collective-permute-start.3 = (bf16[32,2176]{1,0:T(8,128)(2,1)S(1)}, bf16[32,2176]{1,0:T(8,128)(2,1)S(1)}, u32[]{:S(2)}, u32[]{:S(2)}) collective-permute-start(bf16[32,2176]{1,0:T(8,128)(2,1)S(1)} %collective-permute-done.2.refs_3_), channel_id=1, source_target_pairs={{0,4},{2,6},{4,0},{6,2},{8,12},{10,14},{12,8},{14,10},{1,5},{3,7},... | collective-permute-start | bytes 417800 | tf_op jit(solution)/shard_map/ppermute | solution.py:267
  17.5 5.1 %collective-permute-start.4 = (bf16[32,2176]{1,0:T(8,128)(2,1)S(1)}, bf16[32,2176]{1,0:T(8,128)(2,1)S(1)}, u32[]{:S(2)}, u32[]{:S(2)}) collective-permute-start(bf16[32,2176]{1,0:T(8,128)(2,1)S(1)} %collective-permute-done.1.refs_1_), channel_id=1, source_target_pairs={{0,2},{2,0},{4,6},{6,4},{8,10},{10,8},{12,14},{14,12},{1,3},{3,1},... | collective-permute-start | bytes 417800 | tf_op jit(solution)/shard_map/ppermute | solution.py:267
  17.9 1.1 %copy-start = (bf16[1,1024,384]{2,1,0:T(8,128)(2,1)S(1)}, bf16[1,1024,384]{2,1,0:T(8,128)(2,1)}, u32[]{:S(2)}) copy-start(bf16[1,1024,384]{2,1,0:T(8,128)(2,1)} %refs_8_.1) | copy-start | bytes 2359300
  19.0 1.1 %copy-start.2 = (bf16[1,1024,384]{2,1,0:T(8,128)(2,1)S(1)}, bf16[1,1024,384]{2,1,0:T(8,128)(2,1)}, u32[]{:S(2)}) copy-start(bf16[1,1024,384]{2,1,0:T(8,128)(2,1)} %refs_9_.1) | copy-start | bytes 2359300
  20.2 1.1 %copy-start.3 = (bf16[1,384,1024]{2,1,0:T(8,128)(2,1)S(1)}, bf16[1,384,1024]{2,1,0:T(8,128)(2,1)}, u32[]{:S(2)}) copy-start(bf16[1,384,1024]{2,1,0:T(8,128)(2,1)} %refs_10_.1) | copy-start | bytes 2359300
  21.3 1.2 %copy-start.1 = (bf16[1,1024,384]{2,1,0:T(8,128)(2,1)S(1)}, bf16[1,1024,384]{2,1,0:T(8,128)(2,1)}, u32[]{:S(2)}) copy-start(bf16[1,1024,384]{2,1,0:T(8,128)(2,1)} %refs_8_.1) | copy-start | bytes 2359300
  21.3 1.2 %copy-start.4 = (bf16[32,2176]{1,0:T(8,128)(2,1)S(1)}, bf16[32,2176]{1,0:T(8,128)(2,1)}, u32[]{:S(2)}) copy-start(bf16[32,2176]{1,0:T(8,128)(2,1)} %shard_map.102.refs_0_) | copy-start | bytes 417796
  24.8 5.2 %collective-permute-start.10 = (bf16[32,1152]{1,0:T(8,128)(2,1)S(1)}, bf16[32,1152]{1,0:T(8,128)(2,1)S(1)}, u32[]{:S(2)}, u32[]{:S(2)}) collective-permute-start(bf16[32,1152]{1,0:T(8,128)(2,1)S(1)} %get-tuple-element.25), channel_id=1, source_target_pairs={{0,2},{2,0},{4,6},{6,4},{8,10},{10,8},{12,14},{14,12},{1,3},{3,1},... | collective-permute-start | bytes 221192 | tf_op jit(solution)/shard_map/ppermute | solution.py:267
  26.4 5.3 %collective-permute-start.12 = (bf16[32,1152]{1,0:T(8,128)(2,1)S(1)}, bf16[32,1152]{1,0:T(8,128)(2,1)S(1)}, u32[]{:S(2)}, u32[]{:S(2)}) collective-permute-start(bf16[32,1152]{1,0:T(8,128)(2,1)S(1)} %get-tuple-element.27), channel_id=1, source_target_pairs={{0,2},{2,0},{4,6},{6,4},{8,10},{10,8},{12,14},{14,12},{1,3},{3,1},... | collective-permute-start | bytes 221192 | tf_op jit(solution)/shard_map/ppermute | solution.py:267
  26.9 7.4 %collective-permute-start.8 = (bf16[64,1152]{1,0:T(8,128)(2,1)S(1)}, bf16[64,1152]{1,0:T(8,128)(2,1)S(1)}, u32[]{:S(2)}, u32[]{:S(2)}) collective-permute-start(bf16[64,1152]{1,0:T(8,128)(2,1)S(1)} %get-tuple-element.22), channel_id=1, source_target_pairs={{0,2},{2,0},{4,6},{6,4},{8,10},{10,8},{12,14},{14,12},{1,3},{3,1},... | collective-permute-start | bytes 442376 | tf_op jit(solution)/shard_map/ppermute | solution.py:267
  28.5 5.9 %collective-permute-start.7 = (bf16[256,1280]{1,0:T(8,128)(2,1)S(1)}, bf16[256,1280]{1,0:T(8,128)(2,1)S(1)}, u32[]{:S(2)}, u32[]{:S(2)}) collective-permute-start(bf16[256,1280]{1,0:T(8,128)(2,1)S(1)} %get-tuple-element.19.own_ref), channel_id=1, source_target_pairs={{0,1},{1,0},{2,3},{3,2},{4,5},{5,4},{6,7},{7,6},{8,9},{9,8},{10,11... | collective-permute-start | bytes 1966088 | tf_op jit(solution)/shard_map/ppermute | solution.py:271
  30.0 8.1 %collective-permute-start.11 = (bf16[32,1152]{1,0:T(8,128)(2,1)S(1)}, bf16[32,1152]{1,0:T(8,128)(2,1)S(1)}, u32[]{:S(2)}, u32[]{:S(2)}) collective-permute-start(bf16[32,1152]{1,0:T(8,128)(2,1)S(1)} %add_convert_fusion.1), channel_id=1, source_target_pairs={{0,8},{2,10},{4,12},{6,14},{8,0},{10,2},{12,4},{14,6},{1,9},{3,11}... | collective-permute-start | bytes 221192 | tf_op jit(solution)/shard_map/ppermute | solution.py:267
  31.7 6.4 %collective-permute-start.13 = (bf16[32,1152]{1,0:T(8,128)(2,1)S(1)}, bf16[32,1152]{1,0:T(8,128)(2,1)S(1)}, u32[]{:S(2)}, u32[]{:S(2)}) collective-permute-start(bf16[32,1152]{1,0:T(8,128)(2,1)S(1)} %add_convert_fusion), channel_id=1, source_target_pairs={{0,12},{2,14},{4,8},{6,10},{8,4},{10,6},{12,0},{14,2},{1,13},{3,15... | collective-permute-start | bytes 221192 | tf_op jit(solution)/shard_map/ppermute | solution.py:267
  34.3 4.6 %collective-permute-start.9 = (bf16[32,1152]{1,0:T(8,128)(2,1)S(1)}, bf16[32,1152]{1,0:T(8,128)(2,1)S(1)}, u32[]{:S(2)}, u32[]{:S(2)}) collective-permute-start(bf16[32,1152]{1,0:T(8,128)(2,1)S(1)} %add_convert_fusion.2), channel_id=1, source_target_pairs={{0,4},{2,6},{4,0},{6,2},{8,12},{10,14},{12,8},{14,10},{1,5},{3,7},... | collective-permute-start | bytes 221192 | tf_op jit(solution)/shard_map/ppermute | solution.py:267
  34.4 4.5 %copy-start.5 = (s32[32,8]{0,1:T(8,128)S(1)}, s32[32,8]{0,1:T(8,128)}, u32[]{:S(2)}) copy-start(s32[32,8]{0,1:T(8,128)} %param.9) | copy-start | bytes 3076

commit v4 on v3

--- a/solution.py
+++ b/solution.py
@@ -325,19 +325,17 @@
     )
     part = jax.ShapeDtypeStruct((rows, feature_dim + LANES), bf16)
     pair = jax.ShapeDtypeStruct((2 * rows, feature_dim + LANES), bf16)
-    f0, f1, f2, f3, g01, g2, g3, swap, keep = call(
+    f0, fg1, f2, f3, g0, g2, g3, swap, keep = call(
         expert_kernel,
-        [part] * 4
+        [part, pair]
+        + [part] * 5
         + [
-            pair,
-            part,
-            part,
             jax.ShapeDtypeStruct((8 * rows, half + 2 * hidden_w), bf16),
             jax.ShapeDtypeStruct((8 * rows, half), bf16),
         ],
         place,
         touched,
-        *(own, z1, z2, z3, x0, x1, x2, x3),
+        *(own, z1, x1, z2, z3, x0, x2, x3),
         *held,
         in_specs=[SMEM] + [VMEM] * 12,
         out_specs=[VMEM] * 9,
@@ -348,8 +346,8 @@
     r3 = across(sum3, near_z | far_z)
     sum2 = add(f2, across(g2, along_x))
     r2 = across(sum2, far_z)
-    h01 = across(g01, along_x)
-    r1 = across(add(f1, h01[rows:]), near_z)
+    r1 = across(fg1, near_z)
+    r0 = across(add(g0, r1[rows:]), along_x)
     other = swapped(swap)
     grad = jax.ShapeDtypeStruct((1, half, hidden_w), f32)
     grad_gate, grad_up, weights_done = call(
@@ -368,7 +366,7 @@
         (jax.ShapeDtypeStruct((rows, feature_dim), bf16), jax.ShapeDtypeStruct(ids_turned.shape, f32)),
         ids_turned,
         weights_done,
-        *(f0, h01[:rows], r1, r2, r3),
+        *(f0, r1[:rows], r0, r2, r3),
         in_specs=[HBM] + [VMEM] * 6,
         out_specs=[pl.BlockSpec(tokens.shape), pl.BlockSpec(ids_turned.shape)],
         scratch=[pltpu.VMEM(ids_turned.shape, jnp.int32), pltpu.SemaphoreType.DMA],

time: 40 us -> 39.2 us (0.980)
  waiting for transfers between devices: 8.11 us -> 6.65 us
  starting transfers between devices: 20.8 us -> 21.5 us
    ppermute x13, waiting for transfers between devices: 8.11 us -> 6.64 us  [across(): lax.ppermute(block, peers, [(i, i ^ mask) for i in range(lax.axis_size(pe...]
    ppermute x13, starting transfers between devices: 20.8 us -> 21.5 us  [across(): lax.ppermute(block, peers, [(i, i ^ mask) for i in range(lax.axis_size(pe...]
  transfers between devices with their start and end apart: 14 -> 14, of which waited for: 5 -> 4; matrix products, arithmetic and copies ran while one was open for 0% -> 0% of each run, Pallas kernels for 4% -> 5%
where the time goes in v4:
time: 39.2 us; the launch traced here: 38.9 us
  starting transfers between devices  21.5 us (55%)
  waiting for transfers between devices  6.65 us (17%)
  Pallas kernels  6.47 us (17%)
  local copies, waits for them, and re-layouts  3.42 us (9%)
  between operations  0.71 us (2%)
    ppermute x13, starting transfers between devices, across(): lax.ppermute(block, peers, [(i, i ^ mask) for i in range(lax.axis_size(pe...  21.5 us
    ppermute x13, waiting for transfers between devices, across(): lax.ppermute(block, peers, [(i, i ^ mask) for i in range(lax.axis_size(pe...  6.64 us
    pallas_call x5, Pallas kernels, call(): pl.pallas_call(kernel, out_shape=out_shape, in_specs=in_specs, out_specs=...  6.47 us
    unnamed x12, local copies, waits for them, and re-layouts  3.41 us
  transfers between devices with their start and end apart: 14, of which 4 were waited for; matrix products, arithmetic and copies ran while one was open for 0% of the time, Pallas kernels for 5%

profile of v4, /device:TPU:0, one launch (start us, length us, event | category | flops | bytes accessed | tf_op | source)
XLA Modules:
  0.0 38.9 jit_solution(4579039109127584335)
XLA Ops:
  0.6 1.6 %shard_map.102.refs_0_ = bf16[32,2176]{1,0:T(8,128)(2,1)} custom-call(bf16[32,1024]{1,0:T(8,128)(2,1)} %x_ref.1, bf16[32,1024]{1,0:T(8,128)(2,1)} %y_ref.1, s32[8,32]{1,0:T(8,128)} %bitcast.5, s32[8,32]{1,0:T(8,128)} %bitcast.7), custom_call_target="tpu_custom_call" | custom-call | bytes 262144 | tf_op jit(solution)/shard_map/pallas_call | solution.py:134
  2.3 5.1 %collective-permute-start.3 = (bf16[32,2176]{1,0:T(8,128)(2,1)}, bf16[32,2176]{1,0:T(8,128)(2,1)S(1)}, u32[]{:S(2)}, u32[]{:S(2)}) collective-permute-start(bf16[32,2176]{1,0:T(8,128)(2,1)} %shard_map.102.refs_0_), channel_id=1, source_target_pairs={{0,12},{2,14},{4,8},{6,10},{8,4},{10,6},{12,0},{14,2},{1,13},{3,15... | collective-permute-start | bytes 417800 | tf_op jit(solution)/shard_map/ppermute | solution.py:267
  7.4 0.0 collective-permute-start.1
  7.4 1.5 %collective-permute-start = (bf16[32,2176]{1,0:T(8,128)(2,1)}, bf16[32,2176]{1,0:T(8,128)(2,1)S(1)}, u32[]{:S(2)}, u32[]{:S(2)}) collective-permute-start(bf16[32,2176]{1,0:T(8,128)(2,1)} %shard_map.102.refs_0_), channel_id=1, source_target_pairs={{0,2},{2,0},{4,6},{6,4},{8,10},{10,8},{12,14},{14,12},{1,3},{3,1},... | collective-permute-start | bytes 417800 | tf_op jit(solution)/shard_map/ppermute | solution.py:267
  8.9 0.6 %collective-permute-start.5 = (bf16[32,2176]{1,0:T(8,128)(2,1)}, bf16[32,2176]{1,0:T(8,128)(2,1)S(1)}, u32[]{:S(2)}, u32[]{:S(2)}) collective-permute-start(bf16[32,2176]{1,0:T(8,128)(2,1)} %shard_map.102.refs_0_), channel_id=1, source_target_pairs={{0,10},{2,8},{4,14},{6,12},{8,2},{10,0},{12,6},{14,4},{1,11},{3,9}... | collective-permute-start | bytes 417800 | tf_op jit(solution)/shard_map/ppermute | solution.py:267
  9.5 2.7 %collective-permute-done.3.refs_4_ = bf16[32,2176]{1,0:T(8,128)(2,1)S(1)} collective-permute-done((bf16[32,2176]{1,0:T(8,128)(2,1)}, bf16[32,2176]{1,0:T(8,128)(2,1)S(1)}, u32[]{:S(2)}, u32[]{:S(2)}) %collective-permute-start.3) | collective-permute-done | bytes 139296 | tf_op jit(solution)/shard_map/ppermute | solution.py:267
  12.2 1.7 %collective-permute-start.6 = (bf16[32,2176]{1,0:T(8,128)(2,1)S(1)}, bf16[32,2176]{1,0:T(8,128)(2,1)S(1)}, u32[]{:S(2)}, u32[]{:S(2)}) collective-permute-start(bf16[32,2176]{1,0:T(8,128)(2,1)S(1)} %collective-permute-done.3.refs_4_), channel_id=1, source_target_pairs={{0,2},{2,0},{4,6},{6,4},{8,10},{10,8},{12,14},{14,12},{1,3},{3,1},... | collective-permute-start | bytes 417800 | tf_op jit(solution)/shard_map/ppermute | solution.py:267
  13.8 3.6 %collective-permute-start.4 = (bf16[32,2176]{1,0:T(8,128)(2,1)S(1)}, bf16[32,2176]{1,0:T(8,128)(2,1)S(1)}, u32[]{:S(2)}, u32[]{:S(2)}) collective-permute-start(bf16[32,2176]{1,0:T(8,128)(2,1)S(1)} %collective-permute-done.3.refs_4_), channel_id=1, source_target_pairs={{0,4},{2,6},{4,0},{6,2},{8,12},{10,14},{12,8},{14,10},{1,5},{3,7},... | collective-permute-start | bytes 417800 | tf_op jit(solution)/shard_map/ppermute | solution.py:267
  17.5 0.3 collective-permute-start.2
  17.8 0.1 pad_add_fusion.place_ref
  17.9 0.0 collective-permute-done.after_ref.refs_5_
  17.9 1.1 %copy-done = bf16[1,1024,384]{2,1,0:T(8,128)(2,1)S(1)} copy-done((bf16[1,1024,384]{2,1,0:T(8,128)(2,1)S(1)}, bf16[1,1024,384]{2,1,0:T(8,128)(2,1)}, u32[]{:S(2)}) %copy-start) | copy-done | bytes 786456
  19.0 1.1 %copy-done.2 = bf16[1,1024,384]{2,1,0:T(8,128)(2,1)S(1)} copy-done((bf16[1,1024,384]{2,1,0:T(8,128)(2,1)S(1)}, bf16[1,1024,384]{2,1,0:T(8,128)(2,1)}, u32[]{:S(2)}) %copy-start.2) | copy-done | bytes 786456
  20.2 1.1 %copy-done.3 = bf16[1,384,1024]{2,1,0:T(8,128)(2,1)S(1)} copy-done((bf16[1,384,1024]{2,1,0:T(8,128)(2,1)S(1)}, bf16[1,384,1024]{2,1,0:T(8,128)(2,1)}, u32[]{:S(2)}) %copy-start.3) | copy-done | bytes 786456
  21.3 0.0 collective-permute-done.5.refs_6_
  21.3 0.0 collective-permute-done.4.refs_3_
  21.3 1.2 %collective-permute-done.2.refs_2_ = bf16[32,2176]{1,0:T(8,128)(2,1)S(1)} collective-permute-done((bf16[32,2176]{1,0:T(8,128)(2,1)S(1)}, bf16[32,2176]{1,0:T(8,128)(2,1)S(1)}, u32[]{:S(2)}, u32[]{:S(2)}) %collective-permute-start.2) | collective-permute-done | bytes 139296 | tf_op jit(solution)/shard_map/ppermute | solution.py:267
  22.5 2.2 %shard_map.104 = (bf16[32,1152]{1,0:T(8,128)(2,1)S(1)}, bf16[64,1152]{1,0:T(8,128)(2,1)S(1)}, bf16[32,1152]{1,0:T(8,128)(2,1)S(1)}, bf16[32,1152]{1,0:T(8,128)(2...) custom-call(s32[2]{0:T(128)S(1)} %pad_add_fusion.place_ref, ...), custom_call_target="tpu_custom_call" | custom-call | flops 1006632960 | bytes 4456448 | tf_op jit(solution)/shard_map/pallas_call | solution.py:134
  24.8 1.7 %collective-permute-start.10 = (bf16[32,1152]{1,0:T(8,128)(2,1)S(1)}, bf16[32,1152]{1,0:T(8,128)(2,1)S(1)}, u32[]{:S(2)}, u32[]{:S(2)}) collective-permute-start(bf16[32,1152]{1,0:T(8,128)(2,1)S(1)} %get-tuple-element.25), channel_id=1, source_target_pairs={{0,2},{2,0},{4,6},{6,4},{8,10},{10,8},{12,14},{14,12},{1,3},{3,1},... | collective-permute-start | bytes 221192 | tf_op jit(solution)/shard_map/ppermute | solution.py:267
  26.4 0.4 %collective-permute-start.12 = (bf16[32,1152]{1,0:T(8,128)(2,1)S(1)}, bf16[32,1152]{1,0:T(8,128)(2,1)S(1)}, u32[]{:S(2)}, u32[]{:S(2)}) collective-permute-start(bf16[32,1152]{1,0:T(8,128)(2,1)S(1)} %get-tuple-element.27), channel_id=1, source_target_pairs={{0,2},{2,0},{4,6},{6,4},{8,10},{10,8},{12,14},{14,12},{1,3},{3,1},... | collective-permute-start | bytes 221192 | tf_op jit(solution)/shard_map/ppermute | solution.py:267
  26.9 1.7 %collective-permute-start.8 = (bf16[64,1152]{1,0:T(8,128)(2,1)S(1)}, bf16[64,1152]{1,0:T(8,128)(2,1)S(1)}, u32[]{:S(2)}, u32[]{:S(2)}) collective-permute-start(bf16[64,1152]{1,0:T(8,128)(2,1)S(1)} %get-tuple-element.22), channel_id=1, source_target_pairs={{0,4},{2,6},{4,0},{6,2},{8,12},{10,14},{12,8},{14,10},{1,5},{3,7},... | collective-permute-start | bytes 442376 | tf_op jit(solution)/shard_map/ppermute | solution.py:267
  28.5 1.1 %collective-permute-done.10 = bf16[32,1152]{1,0:T(8,128)(2,1)S(1)} collective-permute-done((bf16[32,1152]{1,0:T(8,128)(2,1)S(1)}, bf16[32,1152]{1,0:T(8,128)(2,1)S(1)}, u32[]{:S(2)}, u32[]{:S(2)}) %collective-permute-start.10) | collective-permute-done | bytes 73760 | tf_op jit(solution)/shard_map/ppermute | solution.py:267
  29.7 1.9 %collective-permute-start.11 = (bf16[32,1152]{1,0:T(8,128)(2,1)S(1)}, bf16[32,1152]{1,0:T(8,128)(2,1)S(1)}, u32[]{:S(2)}, u32[]{:S(2)}) collective-permute-start(bf16[32,1152]{1,0:T(8,128)(2,1)S(1)} %add_convert_fusion.1), channel_id=1, source_target_pairs={{0,8},{2,10},{4,12},{6,14},{8,0},{10,2},{12,4},{14,6},{1,9},{3,11}... | collective-permute-start | bytes 221192 | tf_op jit(solution)/shard_map/ppermute | solution.py:267
  31.6 1.8 %collective-permute-start.13 = (bf16[32,1152]{1,0:T(8,128)(2,1)S(1)}, bf16[32,1152]{1,0:T(8,128)(2,1)S(1)}, u32[]{:S(2)}, u32[]{:S(2)}) collective-permute-start(bf16[32,1152]{1,0:T(8,128)(2,1)S(1)} %add_convert_fusion), channel_id=1, source_target_pairs={{0,12},{2,14},{4,8},{6,10},{8,4},{10,6},{12,0},{14,2},{1,13},{3,15... | collective-permute-start | bytes 221192 | tf_op jit(solution)/shard_map/ppermute | solution.py:267
  33.4 0.0 collective-permute-done.8
  33.4 1.2 %collective-permute-start.9 = (bf16[32,1152]{1,0:T(8,128)(2,1)S(1)}, bf16[32,1152]{1,0:T(8,128)(2,1)S(1)}, u32[]{:S(2)}, u32[]{:S(2)}) collective-permute-start(bf16[32,1152]{1,0:T(8,128)(2,1)S(1)} %add_convert_fusion.2), channel_id=1, source_target_pairs={{0,2},{2,0},{4,6},{6,4},{8,10},{10,8},{12,14},{14,12},{1,3},{3,1},... | collective-permute-start | bytes 221192 | tf_op jit(solution)/shard_map/ppermute | solution.py:267
  34.6 0.0 copy-start.5
  34.7 1.8 %shard_map.105 = (f32[1,512,384]{2,1,0:T(8,128)}, f32[1,512,384]{2,1,0:T(8,128)}, f32[8,128]{1,0:T(8,128)S(1)}) custom-call(bf16[256,512]{1,0:T(8,128)(2,1)S(1)} %get-tuple-element.18.keep_ref, bf16[256,1280]{1,0:T(8,128)(2,1)S(1)} %get-tuple-element.19.own_ref, bf16[256,1280]{1,0:T(8,128)(2,1)S(1)} %collective-permute-done.7.other_ref), custom_call_target="tpu_custom_call" | custom-call | flops 402653184 | bytes 2228224 | tf_op jit(solution)/shard_map/pallas_call | solution.py:134
  36.4 1.6 %collective-permute-done.11.refs_3_ = bf16[32,1152]{1,0:T(8,128)(2,1)S(1)} collective-permute-done((bf16[32,1152]{1,0:T(8,128)(2,1)S(1)}, bf16[32,1152]{1,0:T(8,128)(2,1)S(1)}, u32[]{:S(2)}, u32[]{:S(2)}) %collective-permute-start.11) | collective-permute-done | bytes 73760 | tf_op jit(solution)/shard_map/ppermute | solution.py:267
  38.1 0.0 collective-permute-done.13.refs_4_
  38.1 0.0 collective-permute-done.9.refs_2_
  38.1 0.8 %shard_map.106 = (bf16[32,1024]{1,0:T(8,128)(2,1)}, f32[8,32]{1,0:T(8,128)}) custom-call(s32[8,32]{1,0:T(8,128)S(1)} %bitcast.6, f32[8,128]{1,0:T(8,128)S(1)} %get-tuple-element.20.done_ref, bf16[32,1152]{1,0:T(8,128)(2,1)S(1)} %get-tuple-element.21.refs_0_, bf16[32,1152]{1,0:T(8,128)(2,1)S(1)} %slice.8.refs_1_, ...), custom_call_target="tpu_custom_call" | custom-call | bytes 393216 | tf_op jit(solution)/shard_map/pallas_call | solution.py:134
  (18 shorter events, 0.1 us)
Async XLA Ops:
  2.3 9.9 %collective-permute-start.3 = (bf16[32,2176]{1,0:T(8,128)(2,1)}, bf16[32,2176]{1,0:T(8,128)(2,1)S(1)}, u32[]{:S(2)}, u32[]{:S(2)}) collective-permute-start(bf16[32,2176]{1,0:T(8,128)(2,1)} %shard_map.102.refs_0_), channel_id=1, source_target_pairs={{0,12},{2,14},{4,8},{6,10},{8,4},{10,6},{12,0},{14,2},{1,13},{3,15... | collective-permute-start | bytes 417800 | tf_op jit(solution)/shard_map/ppermute | solution.py:267
  7.4 10.1 %collective-permute-start.1 = (bf16[32,2176]{1,0:T(8,128)(2,1)}, bf16[32,2176]{1,0:T(8,128)(2,1)S(1)}, u32[]{:S(2)}, u32[]{:S(2)}) collective-permute-start(bf16[32,2176]{1,0:T(8,128)(2,1)} %shard_map.102.refs_0_), channel_id=1, source_target_pairs={{0,4},{2,6},{4,0},{6,2},{8,12},{10,14},{12,8},{14,10},{1,5},{3,7},... | collective-permute-start | bytes 417800 | tf_op jit(solution)/shard_map/ppermute | solution.py:267
  7.4 10.5 %collective-permute-start = (bf16[32,2176]{1,0:T(8,128)(2,1)}, bf16[32,2176]{1,0:T(8,128)(2,1)S(1)}, u32[]{:S(2)}, u32[]{:S(2)}) collective-permute-start(bf16[32,2176]{1,0:T(8,128)(2,1)} %shard_map.102.refs_0_), channel_id=1, source_target_pairs={{0,2},{2,0},{4,6},{6,4},{8,10},{10,8},{12,14},{14,12},{1,3},{3,1},... | collective-permute-start | bytes 417800 | tf_op jit(solution)/shard_map/ppermute | solution.py:267
  8.9 12.4 %collective-permute-start.5 = (bf16[32,2176]{1,0:T(8,128)(2,1)}, bf16[32,2176]{1,0:T(8,128)(2,1)S(1)}, u32[]{:S(2)}, u32[]{:S(2)}) collective-permute-start(bf16[32,2176]{1,0:T(8,128)(2,1)} %shard_map.102.refs_0_), channel_id=1, source_target_pairs={{0,10},{2,8},{4,14},{6,12},{8,2},{10,0},{12,6},{14,4},{1,11},{3,9}... | collective-permute-start | bytes 417800 | tf_op jit(solution)/shard_map/ppermute | solution.py:267
  12.2 9.2 %collective-permute-start.6 = (bf16[32,2176]{1,0:T(8,128)(2,1)S(1)}, bf16[32,2176]{1,0:T(8,128)(2,1)S(1)}, u32[]{:S(2)}, u32[]{:S(2)}) collective-permute-start(bf16[32,2176]{1,0:T(8,128)(2,1)S(1)} %collective-permute-done.3.refs_4_), channel_id=1, source_target_pairs={{0,2},{2,0},{4,6},{6,4},{8,10},{10,8},{12,14},{14,12},{1,3},{3,1},... | collective-permute-start | bytes 417800 | tf_op jit(solution)/shard_map/ppermute | solution.py:267
  13.8 7.5 %collective-permute-start.4 = (bf16[32,2176]{1,0:T(8,128)(2,1)S(1)}, bf16[32,2176]{1,0:T(8,128)(2,1)S(1)}, u32[]{:S(2)}, u32[]{:S(2)}) collective-permute-start(bf16[32,2176]{1,0:T(8,128)(2,1)S(1)} %collective-permute-done.3.refs_4_), channel_id=1, source_target_pairs={{0,4},{2,6},{4,0},{6,2},{8,12},{10,14},{12,8},{14,10},{1,5},{3,7},... | collective-permute-start | bytes 417800 | tf_op jit(solution)/shard_map/ppermute | solution.py:267
  17.5 5.1 %collective-permute-start.2 = (bf16[32,2176]{1,0:T(8,128)(2,1)S(1)}, bf16[32,2176]{1,0:T(8,128)(2,1)S(1)}, u32[]{:S(2)}, u32[]{:S(2)}) collective-permute-start(bf16[32,2176]{1,0:T(8,128)(2,1)S(1)} %collective-permute-done.1.refs_1_), channel_id=1, source_target_pairs={{0,2},{2,0},{4,6},{6,4},{8,10},{10,8},{12,14},{14,12},{1,3},{3,1},... | collective-permute-start | bytes 417800 | tf_op jit(solution)/shard_map/ppermute | solution.py:267
  17.9 1.1 %copy-start = (bf16[1,1024,384]{2,1,0:T(8,128)(2,1)S(1)}, bf16[1,1024,384]{2,1,0:T(8,128)(2,1)}, u32[]{:S(2)}) copy-start(bf16[1,1024,384]{2,1,0:T(8,128)(2,1)} %refs_8_.1) | copy-start | bytes 2359300
  19.0 1.1 %copy-start.2 = (bf16[1,1024,384]{2,1,0:T(8,128)(2,1)S(1)}, bf16[1,1024,384]{2,1,0:T(8,128)(2,1)}, u32[]{:S(2)}) copy-start(bf16[1,1024,384]{2,1,0:T(8,128)(2,1)} %refs_9_.1) | copy-start | bytes 2359300
  20.2 1.1 %copy-start.3 = (bf16[1,384,1024]{2,1,0:T(8,128)(2,1)S(1)}, bf16[1,384,1024]{2,1,0:T(8,128)(2,1)}, u32[]{:S(2)}) copy-start(bf16[1,384,1024]{2,1,0:T(8,128)(2,1)} %refs_10_.1) | copy-start | bytes 2359300
  21.3 1.2 %copy-start.1 = (bf16[1,1024,384]{2,1,0:T(8,128)(2,1)S(1)}, bf16[1,1024,384]{2,1,0:T(8,128)(2,1)}, u32[]{:S(2)}) copy-start(bf16[1,1024,384]{2,1,0:T(8,128)(2,1)} %refs_8_.1) | copy-start | bytes 2359300
  21.3 1.2 %copy-start.4 = (bf16[32,2176]{1,0:T(8,128)(2,1)S(1)}, bf16[32,2176]{1,0:T(8,128)(2,1)}, u32[]{:S(2)}) copy-start(bf16[32,2176]{1,0:T(8,128)(2,1)} %shard_map.102.refs_0_) | copy-start | bytes 417796
  24.8 4.9 %collective-permute-start.10 = (bf16[32,1152]{1,0:T(8,128)(2,1)S(1)}, bf16[32,1152]{1,0:T(8,128)(2,1)S(1)}, u32[]{:S(2)}, u32[]{:S(2)}) collective-permute-start(bf16[32,1152]{1,0:T(8,128)(2,1)S(1)} %get-tuple-element.25), channel_id=1, source_target_pairs={{0,2},{2,0},{4,6},{6,4},{8,10},{10,8},{12,14},{14,12},{1,3},{3,1},... | collective-permute-start | bytes 221192 | tf_op jit(solution)/shard_map/ppermute | solution.py:267
  26.4 5.2 %collective-permute-start.12 = (bf16[32,1152]{1,0:T(8,128)(2,1)S(1)}, bf16[32,1152]{1,0:T(8,128)(2,1)S(1)}, u32[]{:S(2)}, u32[]{:S(2)}) collective-permute-start(bf16[32,1152]{1,0:T(8,128)(2,1)S(1)} %get-tuple-element.27), channel_id=1, source_target_pairs={{0,2},{2,0},{4,6},{6,4},{8,10},{10,8},{12,14},{14,12},{1,3},{3,1},... | collective-permute-start | bytes 221192 | tf_op jit(solution)/shard_map/ppermute | solution.py:267
  26.9 6.5 %collective-permute-start.8 = (bf16[64,1152]{1,0:T(8,128)(2,1)S(1)}, bf16[64,1152]{1,0:T(8,128)(2,1)S(1)}, u32[]{:S(2)}, u32[]{:S(2)}) collective-permute-start(bf16[64,1152]{1,0:T(8,128)(2,1)S(1)} %get-tuple-element.22), channel_id=1, source_target_pairs={{0,4},{2,6},{4,0},{6,2},{8,12},{10,14},{12,8},{14,10},{1,5},{3,7},... | collective-permute-start | bytes 442376 | tf_op jit(solution)/shard_map/ppermute | solution.py:267
  28.5 6.1 %collective-permute-start.7 = (bf16[256,1280]{1,0:T(8,128)(2,1)S(1)}, bf16[256,1280]{1,0:T(8,128)(2,1)S(1)}, u32[]{:S(2)}, u32[]{:S(2)}) collective-permute-start(bf16[256,1280]{1,0:T(8,128)(2,1)S(1)} %get-tuple-element.19.own_ref), channel_id=1, source_target_pairs={{0,1},{1,0},{2,3},{3,2},{4,5},{5,4},{6,7},{7,6},{8,9},{9,8},{10,11... | collective-permute-start | bytes 1966088 | tf_op jit(solution)/shard_map/ppermute | solution.py:271
  29.7 8.4 %collective-permute-start.11 = (bf16[32,1152]{1,0:T(8,128)(2,1)S(1)}, bf16[32,1152]{1,0:T(8,128)(2,1)S(1)}, u32[]{:S(2)}, u32[]{:S(2)}) collective-permute-start(bf16[32,1152]{1,0:T(8,128)(2,1)S(1)} %add_convert_fusion.1), channel_id=1, source_target_pairs={{0,8},{2,10},{4,12},{6,14},{8,0},{10,2},{12,4},{14,6},{1,9},{3,11}... | collective-permute-start | bytes 221192 | tf_op jit(solution)/shard_map/ppermute | solution.py:267
  31.6 6.5 %collective-permute-start.13 = (bf16[32,1152]{1,0:T(8,128)(2,1)S(1)}, bf16[32,1152]{1,0:T(8,128)(2,1)S(1)}, u32[]{:S(2)}, u32[]{:S(2)}) collective-permute-start(bf16[32,1152]{1,0:T(8,128)(2,1)S(1)} %add_convert_fusion), channel_id=1, source_target_pairs={{0,12},{2,14},{4,8},{6,10},{8,4},{10,6},{12,0},{14,2},{1,13},{3,15... | collective-permute-start | bytes 221192 | tf_op jit(solution)/shard_map/ppermute | solution.py:267
  33.4 4.6 %collective-permute-start.9 = (bf16[32,1152]{1,0:T(8,128)(2,1)S(1)}, bf16[32,1152]{1,0:T(8,128)(2,1)S(1)}, u32[]{:S(2)}, u32[]{:S(2)}) collective-permute-start(bf16[32,1152]{1,0:T(8,128)(2,1)S(1)} %add_convert_fusion.2), channel_id=1, source_target_pairs={{0,2},{2,0},{4,6},{6,4},{8,10},{10,8},{12,14},{14,12},{1,3},{3,1},... | collective-permute-start | bytes 221192 | tf_op jit(solution)/shard_map/ppermute | solution.py:267
  34.6 3.4 %copy-start.5 = (s32[32,8]{0,1:T(8,128)S(1)}, s32[32,8]{0,1:T(8,128)}, u32[]{:S(2)}) copy-start(s32[32,8]{0,1:T(8,128)} %param.9) | copy-start | bytes 3076

commit v5 on v4

--- a/solution.py
+++ b/solution.py
@@ -179,9 +179,8 @@
     y_copy.wait()
 
 
-def expert_kernel(place_ref, touched_ref, *refs):
-    blocks, (gate_ref, up_ref, down_ref) = refs[:8], refs[8:11]
-    part_refs, (swap_ref, keep_ref) = refs[11:18], refs[18:]
+def expert_rows(place_ref, blocks, weight_refs, part_refs, swap_ref, keep_ref):
+    gate_ref, up_ref, down_ref = weight_refs
     rows, width = blocks[0].shape
     feature_dim = (width - LANES) // 2
     half = feature_dim // 2
@@ -217,14 +216,33 @@
         first = last
     hidden_w = d_gate.shape[1]
     low, high = x_rows[:, :half], x_rows[:, half:]
-    swap_ref[:, :half] = jnp.where(replica == 0, high, low)
-    swap_ref[:, half : half + hidden_w] = d_gate
-    swap_ref[:, half + hidden_w :] = d_up
-    keep_ref[...] = jnp.where(replica == 0, low, high)
-
-
-def touch_kernel(after_ref, gate_ref, up_ref, down_ref, out_ref):
-    out_ref[...] = jnp.zeros(out_ref.shape, out_ref.dtype)
+    count = data.shape[0]
+    swap_ref[:count, :half] = jnp.where(replica == 0, high, low)
+    swap_ref[:count, half : half + hidden_w] = d_gate
+    swap_ref[:count, half + hidden_w :] = d_up
+    keep_ref[:count] = jnp.where(replica == 0, low, high)
+
+
+def far_kernel(place_ref, *refs):
+    expert_rows(place_ref, refs[:4], refs[4:7], refs[7:11], *refs[11:])
+
+
+def near_kernel(place_ref, far_swap_ref, far_keep_ref, *refs):
+    expert_rows(place_ref, refs[:4], refs[4:7], refs[7:10], *refs[10:])
+    first = refs[0].shape[0] * 4
+    refs[10][first:] = far_swap_ref[...]
+    refs[11][first:] = far_keep_ref[...]
+
+
+def hold_kernel(after_ref, *refs):
+    count = len(refs) // 2
+    for source, target in zip(refs[:count], refs[count:]):
+        step = source.shape[1] // 8
+
+        @pl.loop(0, 8)
+        def _(index):
+            part = pl.ds(pl.multiple_of(index * step, step), step)
+            target[0, part] = source[0, part]
 
 
 def weight_kernel(keep_ref, own_ref, other_ref, gate_ref, up_ref, done_ref):
@@ -311,36 +329,52 @@
     x1 = across(z1, along_x)
     x3 = across(z3, along_x)
     z2 = across(z3, near_z)
-    held = (w_gate, w_up, w_down)
-    touched = call(
-        touch_kernel,
-        jax.ShapeDtypeStruct((8, LANES), f32),
+    held = call(
+        hold_kernel,
+        [jax.ShapeDtypeStruct(w.shape, bf16) for w in (w_gate, w_up, w_down)],
         x0,
         w_gate,
         w_up,
         w_down,
         in_specs=[VMEM] * 4,
-        out_specs=VMEM,
+        out_specs=[VMEM] * 3,
         moved=12 * feature_dim * hidden_w,
     )
     part = jax.ShapeDtypeStruct((rows, feature_dim + LANES), bf16)
     pair = jax.ShapeDtypeStruct((2 * rows, feature_dim + LANES), bf16)
-    f0, fg1, f2, f3, g0, g2, g3, swap, keep = call(
-        expert_kernel,
-        [part, pair]
-        + [part] * 5
-        + [
-            jax.ShapeDtypeStruct((8 * rows, half + 2 * hidden_w), bf16),
-            jax.ShapeDtypeStruct((8 * rows, half), bf16),
-        ],
+
+    def work(blocks):
+        return {
+            "flops": 2 * blocks * rows * feature_dim * hidden_w * 5,
+            "moved": 6 * feature_dim * hidden_w + blocks * rows * feature_dim * 8,
+        }
+
+    def exchanged(blocks):
+        return [
+            jax.ShapeDtypeStruct((blocks * rows, half + 2 * hidden_w), bf16),
+            jax.ShapeDtypeStruct((blocks * rows, half), bf16),
+        ]
+
+    f2, f3, g2, g3, *far = call(
+        far_kernel,
+        [part] * 4 + exchanged(4),
         place,
-        touched,
-        *(own, z1, x1, z2, z3, x0, x2, x3),
+        *(z2, z3, x2, x3),
         *held,
-        in_specs=[SMEM] + [VMEM] * 12,
-        out_specs=[VMEM] * 9,
-        flops=2 * 8 * rows * feature_dim * hidden_w * 5,
-        moved=6 * feature_dim * hidden_w + 8 * rows * feature_dim * 8,
+        in_specs=[SMEM] + [VMEM] * 7,
+        out_specs=[VMEM] * 6,
+        **work(4),
+    )
+    f0, fg1, g0, swap, keep = call(
+        near_kernel,
+        [part, pair, part] + exchanged(8),
+        place,
+        *far,
+        *(own, z1, x1, x0),
+        *held,
+        in_specs=[SMEM] + [VMEM] * 9,
+        out_specs=[VMEM] * 5,
+        **work(4),
     )
     sum3 = add(f3, across(g3, along_x))
     r3 = across(sum3, near_z | far_z)
@@ -348,7 +382,7 @@
     r2 = across(sum2, far_z)
     r1 = across(fg1, near_z)
     r0 = across(add(g0, r1[rows:]), along_x)
-    other = swapped(swap)
+    other = swapped(after(swap, sum2))
     grad = jax.ShapeDtypeStruct((1, half, hidden_w), f32)
     grad_gate, grad_up, weights_done = call(
         weight_kernel,

time: 39.2 us -> 38.1 us (0.972)
  waiting for transfers between devices: 6.65 us -> 4.11 us
  Pallas kernels: 6.47 us -> 8.07 us
    ppermute x13, waiting for transfers between devices: 6.64 us -> 4.1 us  [across(): lax.ppermute(block, peers, [(i, i ^ mask) for i in range(lax.axis_size(pe...]
    pallas_call x5 -> x6, Pallas kernels: 6.47 us -> 8.07 us  [call(): pl.pallas_call(kernel, out_shape=out_shape, in_specs=in_specs, out_specs=...]
    unnamed x12 -> x10, local copies, waits for them, and re-layouts: 3.41 us -> 3.41 us
  transfers between devices with their start and end apart: 14 -> 14, of which waited for: 4 -> 4; matrix products, arithmetic and copies ran while one was open for 0% -> 0% of each run, Pallas kernels for 5% -> 15%
where the time goes in v5:
time: 38.1 us; the launch traced here: 37.8 us
  starting transfers between devices  21.3 us (56%)
  Pallas kernels  8.07 us (21%)
  waiting for transfers between devices  4.11 us (11%)
  local copies, waits for them, and re-layouts  3.42 us (9%)
  between operations  0.73 us (2%)
    ppermute x13, starting transfers between devices, across(): lax.ppermute(block, peers, [(i, i ^ mask) for i in range(lax.axis_size(pe...  21.3 us
    pallas_call x6, Pallas kernels, call(): pl.pallas_call(kernel, out_shape=out_shape, in_specs=in_specs, out_specs=...  8.07 us
    ppermute x13, waiting for transfers between devices, across(): lax.ppermute(block, peers, [(i, i ^ mask) for i in range(lax.axis_size(pe...  4.1 us
    unnamed x10, local copies, waits for them, and re-layouts  3.41 us
  transfers between devices with their start and end apart: 14, of which 4 were waited for; matrix products, arithmetic and copies ran while one was open for 0% of the time, Pallas kernels for 15%

profile of v5, /device:TPU:0, one launch (start us, length us, event | category | flops | bytes accessed | tf_op | source)
XLA Modules:
  0.0 37.8 jit_solution(838619427111174748)
XLA Ops:
  0.6 1.6 %shard_map.102.refs_0_ = bf16[32,2176]{1,0:T(8,128)(2,1)} custom-call(bf16[32,1024]{1,0:T(8,128)(2,1)} %x_ref.1, bf16[32,1024]{1,0:T(8,128)(2,1)} %y_ref.1, s32[8,32]{1,0:T(8,128)} %bitcast.5, s32[8,32]{1,0:T(8,128)} %bitcast.7), custom_call_target="tpu_custom_call" | custom-call | bytes 262144 | tf_op jit(solution)/shard_map/pallas_call | solution.py:134
  2.3 5.1 %collective-permute-start = (bf16[32,2176]{1,0:T(8,128)(2,1)}, bf16[32,2176]{1,0:T(8,128)(2,1)S(1)}, u32[]{:S(2)}, u32[]{:S(2)}) collective-permute-start(bf16[32,2176]{1,0:T(8,128)(2,1)} %shard_map.102.refs_0_), channel_id=1, source_target_pairs={{0,12},{2,14},{4,8},{6,10},{8,4},{10,6},{12,0},{14,2},{1,13},{3,15... | collective-permute-start | bytes 417800 | tf_op jit(solution)/shard_map/ppermute | solution.py:285
  7.4 0.0 collective-permute-start.5
  7.4 1.5 %collective-permute-start.4 = (bf16[32,2176]{1,0:T(8,128)(2,1)}, bf16[32,2176]{1,0:T(8,128)(2,1)S(1)}, u32[]{:S(2)}, u32[]{:S(2)}) collective-permute-start(bf16[32,2176]{1,0:T(8,128)(2,1)} %shard_map.102.refs_0_), channel_id=1, source_target_pairs={{0,2},{2,0},{4,6},{6,4},{8,10},{10,8},{12,14},{14,12},{1,3},{3,1},... | collective-permute-start | bytes 417800 | tf_op jit(solution)/shard_map/ppermute | solution.py:285
  8.9 0.6 %collective-permute-start.2 = (bf16[32,2176]{1,0:T(8,128)(2,1)}, bf16[32,2176]{1,0:T(8,128)(2,1)S(1)}, u32[]{:S(2)}, u32[]{:S(2)}) collective-permute-start(bf16[32,2176]{1,0:T(8,128)(2,1)} %shard_map.102.refs_0_), channel_id=1, source_target_pairs={{0,10},{2,8},{4,14},{6,12},{8,2},{10,0},{12,6},{14,4},{1,11},{3,9}... | collective-permute-start | bytes 417800 | tf_op jit(solution)/shard_map/ppermute | solution.py:285
  9.5 2.7 %collective-permute-done.refs_1_ = bf16[32,2176]{1,0:T(8,128)(2,1)S(1)} collective-permute-done((bf16[32,2176]{1,0:T(8,128)(2,1)}, bf16[32,2176]{1,0:T(8,128)(2,1)S(1)}, u32[]{:S(2)}, u32[]{:S(2)}) %collective-permute-start) | collective-permute-done | bytes 139296 | tf_op jit(solution)/shard_map/ppermute | solution.py:285
  12.2 1.7 %collective-permute-start.3 = (bf16[32,2176]{1,0:T(8,128)(2,1)S(1)}, bf16[32,2176]{1,0:T(8,128)(2,1)S(1)}, u32[]{:S(2)}, u32[]{:S(2)}) collective-permute-start(bf16[32,2176]{1,0:T(8,128)(2,1)S(1)} %collective-permute-done.refs_1_), channel_id=1, source_target_pairs={{0,2},{2,0},{4,6},{6,4},{8,10},{10,8},{12,14},{14,12},{1,3},{3,1},... | collective-permute-start | bytes 417800 | tf_op jit(solution)/shard_map/ppermute | solution.py:285
  13.8 3.6 %collective-permute-start.1 = (bf16[32,2176]{1,0:T(8,128)(2,1)S(1)}, bf16[32,2176]{1,0:T(8,128)(2,1)S(1)}, u32[]{:S(2)}, u32[]{:S(2)}) collective-permute-start(bf16[32,2176]{1,0:T(8,128)(2,1)S(1)} %collective-permute-done.refs_1_), channel_id=1, source_target_pairs={{0,4},{2,6},{4,0},{6,2},{8,12},{10,14},{12,8},{14,10},{1,5},{3,7},... | collective-permute-start | bytes 417800 | tf_op jit(solution)/shard_map/ppermute | solution.py:285
  17.5 0.0 collective-permute-done.5.refs_1_
  17.5 0.3 collective-permute-start.6
  17.8 0.1 pad_add_fusion.place_ref
  17.9 1.1 %copy-done = bf16[1,1024,384]{2,1,0:T(8,128)(2,1)S(1)} copy-done((bf16[1,1024,384]{2,1,0:T(8,128)(2,1)S(1)}, bf16[1,1024,384]{2,1,0:T(8,128)(2,1)}, u32[]{:S(2)}) %copy-start) | copy-done | bytes 786456
  19.0 1.1 %copy-done.1 = bf16[1,1024,384]{2,1,0:T(8,128)(2,1)S(1)} copy-done((bf16[1,1024,384]{2,1,0:T(8,128)(2,1)S(1)}, bf16[1,1024,384]{2,1,0:T(8,128)(2,1)}, u32[]{:S(2)}) %copy-start.1) | copy-done | bytes 786456
  20.2 1.1 %copy-done.2 = bf16[1,384,1024]{2,1,0:T(8,128)(2,1)S(1)} copy-done((bf16[1,384,1024]{2,1,0:T(8,128)(2,1)S(1)}, bf16[1,384,1024]{2,1,0:T(8,128)(2,1)}, u32[]{:S(2)}) %copy-start.2) | copy-done | bytes 786456
  21.3 0.3 shard_map.103
  21.6 0.0 collective-permute-done.2.refs_2_
  21.6 0.0 collective-permute-done.3.refs_3_
  21.6 0.0 copy-start.3
  21.6 1.8 %shard_map.104 = (bf16[32,1152]{1,0:T(8,128)(2,1)S(1)}, bf16[32,1152]{1,0:T(8,128)(2,1)S(1)}, bf16[32,1152]{1,0:T(8,128)(2,1)S(1)}, bf16[32,1152]{1,0:T(8,128)(2...) custom-call(s32[2]{0:T(128)S(1)} %pad_add_fusion.place_ref, ...), custom_call_target="tpu_custom_call" | custom-call | flops 503316480 | bytes 3407872 | tf_op jit(solution)/shard_map/pallas_call | solution.py:134
  23.4 1.8 %collective-permute-start.7 = (bf16[32,1152]{1,0:T(8,128)(2,1)S(1)}, bf16[32,1152]{1,0:T(8,128)(2,1)S(1)}, u32[]{:S(2)}, u32[]{:S(2)}) collective-permute-start(bf16[32,1152]{1,0:T(8,128)(2,1)S(1)} %get-tuple-element.32), channel_id=1, source_target_pairs={{0,2},{2,0},{4,6},{6,4},{8,10},{10,8},{12,14},{14,12},{1,3},{3,1},... | collective-permute-start | bytes 221192 | tf_op jit(solution)/shard_map/ppermute | solution.py:285
  25.2 0.3 collective-permute-start.12
  25.5 1.8 %shard_map.105 = (bf16[32,1152]{1,0:T(8,128)(2,1)S(1)}, bf16[64,1152]{1,0:T(8,128)(2,1)S(1)}, bf16[32,1152]{1,0:T(8,128)(2,1)S(1)}, bf16[256,1280]{1,0:T(8,128)(2,1)S(1)}, bf16[256,512]{1,0:T(8,128)(2,1)S(1)}) custom-call(s32[2]{0:T(128)S(1)} %pad_add_fusion.place_ref, bf16[128,1280]{1,0:T(8,128)(2,1)S(1)} %get-tuple-element.27.far_swap_ref, ...), custom_call_target="tpu_custom_call" | custom-call | flops 503316480 | bytes 3407872 | tf_op jit(solution)/shard_map/pallas_call | solution.py:134
  27.3 1.1 %collective-permute-start.9 = (bf16[64,1152]{1,0:T(8,128)(2,1)S(1)}, bf16[64,1152]{1,0:T(8,128)(2,1)S(1)}, u32[]{:S(2)}, u32[]{:S(2)}) collective-permute-start(bf16[64,1152]{1,0:T(8,128)(2,1)S(1)} %get-tuple-element.36), channel_id=1, source_target_pairs={{0,4},{2,6},{4,0},{6,2},{8,12},{10,14},{12,8},{14,10},{1,5},{3,7},... | collective-permute-start | bytes 442376 | tf_op jit(solution)/shard_map/ppermute | solution.py:285
  28.4 1.5 %collective-permute-start.11 = (bf16[32,1152]{1,0:T(8,128)(2,1)S(1)}, bf16[32,1152]{1,0:T(8,128)(2,1)S(1)}, u32[]{:S(2)}, u32[]{:S(2)}) collective-permute-start(bf16[32,1152]{1,0:T(8,128)(2,1)S(1)} %add_convert_fusion.2), channel_id=1, source_target_pairs={{0,8},{2,10},{4,12},{6,14},{8,0},{10,2},{12,4},{14,6},{1,9},{3,11}... | collective-permute-start | bytes 221192 | tf_op jit(solution)/shard_map/ppermute | solution.py:285
  29.9 2.0 %collective-permute-start.13 = (bf16[32,1152]{1,0:T(8,128)(2,1)S(1)}, bf16[32,1152]{1,0:T(8,128)(2,1)S(1)}, u32[]{:S(2)}, u32[]{:S(2)}) collective-permute-start(bf16[32,1152]{1,0:T(8,128)(2,1)S(1)} %add_convert_fusion), channel_id=1, source_target_pairs={{0,12},{2,14},{4,8},{6,10},{8,4},{10,6},{12,0},{14,2},{1,13},{3,15... | collective-permute-start | bytes 221192 | tf_op jit(solution)/shard_map/ppermute | solution.py:285
  31.9 0.6 %collective-permute-done.9 = bf16[64,1152]{1,0:T(8,128)(2,1)S(1)} collective-permute-done((bf16[64,1152]{1,0:T(8,128)(2,1)S(1)}, bf16[64,1152]{1,0:T(8,128)(2,1)S(1)}, u32[]{:S(2)}, u32[]{:S(2)}) %collective-permute-start.9) | collective-permute-done | bytes 147488 | tf_op jit(solution)/shard_map/ppermute | solution.py:285
  32.5 1.8 %collective-permute-start.10 = (bf16[32,1152]{1,0:T(8,128)(2,1)S(1)}, bf16[32,1152]{1,0:T(8,128)(2,1)S(1)}, u32[]{:S(2)}, u32[]{:S(2)}) collective-permute-start(bf16[32,1152]{1,0:T(8,128)(2,1)S(1)} %add_convert_fusion.1), channel_id=1, source_target_pairs={{0,2},{2,0},{4,6},{6,4},{8,10},{10,8},{12,14},{14,12},{1,3},{3,1},... | collective-permute-start | bytes 221192 | tf_op jit(solution)/shard_map/ppermute | solution.py:285
  34.3 0.0 copy-start.4
  34.3 1.8 %shard_map.106 = (f32[1,512,384]{2,1,0:T(8,128)}, f32[1,512,384]{2,1,0:T(8,128)}, f32[8,128]{1,0:T(8,128)S(1)}) custom-call(bf16[256,512]{1,0:T(8,128)(2,1)S(1)} %get-tuple-element.29.keep_ref, bf16[256,1280]{1,0:T(8,128)(2,1)S(1)} %get-tuple-element.33.own_ref, bf16[256,1280]{1,0:T(8,128)(2,1)S(1)} %collective-permute-done.8.other_ref), custom_call_target="tpu_custom_call" | custom-call | flops 402653184 | bytes 2228224 | tf_op jit(solution)/shard_map/pallas_call | solution.py:134
  36.1 0.5 %collective-permute-done.13.refs_4_ = bf16[32,1152]{1,0:T(8,128)(2,1)S(1)} collective-permute-done((bf16[32,1152]{1,0:T(8,128)(2,1)S(1)}, bf16[32,1152]{1,0:T(8,128)(2,1)S(1)}, u32[]{:S(2)}, u32[]{:S(2)}) %collective-permute-start.13) | collective-permute-done | bytes 73760 | tf_op jit(solution)/shard_map/ppermute | solution.py:285
  36.5 0.4 %collective-permute-done.10.refs_2_ = bf16[32,1152]{1,0:T(8,128)(2,1)S(1)} collective-permute-done((bf16[32,1152]{1,0:T(8,128)(2,1)S(1)}, bf16[32,1152]{1,0:T(8,128)(2,1)S(1)}, u32[]{:S(2)}, u32[]{:S(2)}) %collective-permute-start.10) | collective-permute-done | bytes 73760 | tf_op jit(solution)/shard_map/ppermute | solution.py:285
  36.9 0.8 %shard_map.107 = (bf16[32,1024]{1,0:T(8,128)(2,1)}, f32[8,32]{1,0:T(8,128)}) custom-call(s32[8,32]{1,0:T(8,128)S(1)} %bitcast.6, f32[8,128]{1,0:T(8,128)S(1)} %get-tuple-element.34.done_ref, bf16[32,1152]{1,0:T(8,128)(2,1)S(1)} %get-tuple-element.35.refs_0_, bf16[32,1152]{1,0:T(8,128)(2,1)S(1)} %slice.8.refs_1_, ...), custom_call_target="tpu_custom_call" | custom-call | bytes 393216 | tf_op jit(solution)/shard_map/pallas_call | solution.py:134
  (17 shorter events, 0.1 us)
Async XLA Ops:
  2.3 9.9 %collective-permute-start = (bf16[32,2176]{1,0:T(8,128)(2,1)}, bf16[32,2176]{1,0:T(8,128)(2,1)S(1)}, u32[]{:S(2)}, u32[]{:S(2)}) collective-permute-start(bf16[32,2176]{1,0:T(8,128)(2,1)} %shard_map.102.refs_0_), channel_id=1, source_target_pairs={{0,12},{2,14},{4,8},{6,10},{8,4},{10,6},{12,0},{14,2},{1,13},{3,15... | collective-permute-start | bytes 417800 | tf_op jit(solution)/shard_map/ppermute | solution.py:285
  7.4 10.1 %collective-permute-start.5 = (bf16[32,2176]{1,0:T(8,128)(2,1)}, bf16[32,2176]{1,0:T(8,128)(2,1)S(1)}, u32[]{:S(2)}, u32[]{:S(2)}) collective-permute-start(bf16[32,2176]{1,0:T(8,128)(2,1)} %shard_map.102.refs_0_), channel_id=1, source_target_pairs={{0,4},{2,6},{4,0},{6,2},{8,12},{10,14},{12,8},{14,10},{1,5},{3,7},... | collective-permute-start | bytes 417800 | tf_op jit(solution)/shard_map/ppermute | solution.py:285
  7.4 10.5 %collective-permute-start.4 = (bf16[32,2176]{1,0:T(8,128)(2,1)}, bf16[32,2176]{1,0:T(8,128)(2,1)S(1)}, u32[]{:S(2)}, u32[]{:S(2)}) collective-permute-start(bf16[32,2176]{1,0:T(8,128)(2,1)} %shard_map.102.refs_0_), channel_id=1, source_target_pairs={{0,2},{2,0},{4,6},{6,4},{8,10},{10,8},{12,14},{14,12},{1,3},{3,1},... | collective-permute-start | bytes 417800 | tf_op jit(solution)/shard_map/ppermute | solution.py:285
  8.9 12.7 %collective-permute-start.2 = (bf16[32,2176]{1,0:T(8,128)(2,1)}, bf16[32,2176]{1,0:T(8,128)(2,1)S(1)}, u32[]{:S(2)}, u32[]{:S(2)}) collective-permute-start(bf16[32,2176]{1,0:T(8,128)(2,1)} %shard_map.102.refs_0_), channel_id=1, source_target_pairs={{0,10},{2,8},{4,14},{6,12},{8,2},{10,0},{12,6},{14,4},{1,11},{3,9}... | collective-permute-start | bytes 417800 | tf_op jit(solution)/shard_map/ppermute | solution.py:285
  12.2 9.5 %collective-permute-start.3 = (bf16[32,2176]{1,0:T(8,128)(2,1)S(1)}, bf16[32,2176]{1,0:T(8,128)(2,1)S(1)}, u32[]{:S(2)}, u32[]{:S(2)}) collective-permute-start(bf16[32,2176]{1,0:T(8,128)(2,1)S(1)} %collective-permute-done.refs_1_), channel_id=1, source_target_pairs={{0,2},{2,0},{4,6},{6,4},{8,10},{10,8},{12,14},{14,12},{1,3},{3,1},... | collective-permute-start | bytes 417800 | tf_op jit(solution)/shard_map/ppermute | solution.py:285
  13.8 7.8 %collective-permute-start.1 = (bf16[32,2176]{1,0:T(8,128)(2,1)S(1)}, bf16[32,2176]{1,0:T(8,128)(2,1)S(1)}, u32[]{:S(2)}, u32[]{:S(2)}) collective-permute-start(bf16[32,2176]{1,0:T(8,128)(2,1)S(1)} %collective-permute-done.refs_1_), channel_id=1, source_target_pairs={{0,4},{2,6},{4,0},{6,2},{8,12},{10,14},{12,8},{14,10},{1,5},{3,7},... | collective-permute-start | bytes 417800 | tf_op jit(solution)/shard_map/ppermute | solution.py:285
  17.5 8.0 %collective-permute-start.6 = (bf16[32,2176]{1,0:T(8,128)(2,1)S(1)}, bf16[32,2176]{1,0:T(8,128)(2,1)S(1)}, u32[]{:S(2)}, u32[]{:S(2)}) collective-permute-start(bf16[32,2176]{1,0:T(8,128)(2,1)S(1)} %collective-permute-done.5.refs_1_), channel_id=1, source_target_pairs={{0,2},{2,0},{4,6},{6,4},{8,10},{10,8},{12,14},{14,12},{1,3},{3,1},... | collective-permute-start | bytes 417800 | tf_op jit(solution)/shard_map/ppermute | solution.py:285
  17.9 1.1 %copy-start = (bf16[1,1024,384]{2,1,0:T(8,128)(2,1)S(1)}, bf16[1,1024,384]{2,1,0:T(8,128)(2,1)}, u32[]{:S(2)}) copy-start(bf16[1,1024,384]{2,1,0:T(8,128)(2,1)} %refs_0_.1) | copy-start | bytes 2359300
  19.0 1.1 %copy-start.1 = (bf16[1,1024,384]{2,1,0:T(8,128)(2,1)S(1)}, bf16[1,1024,384]{2,1,0:T(8,128)(2,1)}, u32[]{:S(2)}) copy-start(bf16[1,1024,384]{2,1,0:T(8,128)(2,1)} %refs_1_.1) | copy-start | bytes 2359300
  20.2 1.1 %copy-start.2 = (bf16[1,384,1024]{2,1,0:T(8,128)(2,1)S(1)}, bf16[1,384,1024]{2,1,0:T(8,128)(2,1)}, u32[]{:S(2)}) copy-start(bf16[1,384,1024]{2,1,0:T(8,128)(2,1)} %refs_2_.1) | copy-start | bytes 2359300
  21.6 3.9 %copy-start.3 = (bf16[32,2176]{1,0:T(8,128)(2,1)S(1)}, bf16[32,2176]{1,0:T(8,128)(2,1)}, u32[]{:S(2)}) copy-start(bf16[32,2176]{1,0:T(8,128)(2,1)} %shard_map.102.refs_0_) | copy-start | bytes 417796
  23.4 4.9 %collective-permute-start.7 = (bf16[32,1152]{1,0:T(8,128)(2,1)S(1)}, bf16[32,1152]{1,0:T(8,128)(2,1)S(1)}, u32[]{:S(2)}, u32[]{:S(2)}) collective-permute-start(bf16[32,1152]{1,0:T(8,128)(2,1)S(1)} %get-tuple-element.32), channel_id=1, source_target_pairs={{0,2},{2,0},{4,6},{6,4},{8,10},{10,8},{12,14},{14,12},{1,3},{3,1},... | collective-permute-start | bytes 221192 | tf_op jit(solution)/shard_map/ppermute | solution.py:285
  25.2 4.7 %collective-permute-start.12 = (bf16[32,1152]{1,0:T(8,128)(2,1)S(1)}, bf16[32,1152]{1,0:T(8,128)(2,1)S(1)}, u32[]{:S(2)}, u32[]{:S(2)}) collective-permute-start(bf16[32,1152]{1,0:T(8,128)(2,1)S(1)} %get-tuple-element.39), channel_id=1, source_target_pairs={{0,2},{2,0},{4,6},{6,4},{8,10},{10,8},{12,14},{14,12},{1,3},{3,1},... | collective-permute-start | bytes 221192 | tf_op jit(solution)/shard_map/ppermute | solution.py:285
  27.3 5.2 %collective-permute-start.9 = (bf16[64,1152]{1,0:T(8,128)(2,1)S(1)}, bf16[64,1152]{1,0:T(8,128)(2,1)S(1)}, u32[]{:S(2)}, u32[]{:S(2)}) collective-permute-start(bf16[64,1152]{1,0:T(8,128)(2,1)S(1)} %get-tuple-element.36), channel_id=1, source_target_pairs={{0,4},{2,6},{4,0},{6,2},{8,12},{10,14},{12,8},{14,10},{1,5},{3,7},... | collective-permute-start | bytes 442376 | tf_op jit(solution)/shard_map/ppermute | solution.py:285
  28.4 7.7 %collective-permute-start.11 = (bf16[32,1152]{1,0:T(8,128)(2,1)S(1)}, bf16[32,1152]{1,0:T(8,128)(2,1)S(1)}, u32[]{:S(2)}, u32[]{:S(2)}) collective-permute-start(bf16[32,1152]{1,0:T(8,128)(2,1)S(1)} %add_convert_fusion.2), channel_id=1, source_target_pairs={{0,8},{2,10},{4,12},{6,14},{8,0},{10,2},{12,4},{14,6},{1,9},{3,11}... | collective-permute-start | bytes 221192 | tf_op jit(solution)/shard_map/ppermute | solution.py:285
  29.9 4.4 %collective-permute-start.8 = (bf16[256,1280]{1,0:T(8,128)(2,1)S(1)}, bf16[256,1280]{1,0:T(8,128)(2,1)S(1)}, u32[]{:S(2)}, u32[]{:S(2)}) collective-permute-start(bf16[256,1280]{1,0:T(8,128)(2,1)S(1)} %get-tuple-element.33.own_ref), channel_id=1, source_target_pairs={{0,1},{1,0},{2,3},{3,2},{4,5},{5,4},{6,7},{7,6},{8,9},{9,8},{10,11... | collective-permute-start | bytes 1966088 | tf_op jit(solution)/shard_map/ppermute | solution.py:289
  29.9 6.6 %collective-permute-start.13 = (bf16[32,1152]{1,0:T(8,128)(2,1)S(1)}, bf16[32,1152]{1,0:T(8,128)(2,1)S(1)}, u32[]{:S(2)}, u32[]{:S(2)}) collective-permute-start(bf16[32,1152]{1,0:T(8,128)(2,1)S(1)} %add_convert_fusion), channel_id=1, source_target_pairs={{0,12},{2,14},{4,8},{6,10},{8,4},{10,6},{12,0},{14,2},{1,13},{3,15... | collective-permute-start | bytes 221192 | tf_op jit(solution)/shard_map/ppermute | solution.py:285
  32.5 4.4 %collective-permute-start.10 = (bf16[32,1152]{1,0:T(8,128)(2,1)S(1)}, bf16[32,1152]{1,0:T(8,128)(2,1)S(1)}, u32[]{:S(2)}, u32[]{:S(2)}) collective-permute-start(bf16[32,1152]{1,0:T(8,128)(2,1)S(1)} %add_convert_fusion.1), channel_id=1, source_target_pairs={{0,2},{2,0},{4,6},{6,4},{8,10},{10,8},{12,14},{14,12},{1,3},{3,1},... | collective-permute-start | bytes 221192 | tf_op jit(solution)/shard_map/ppermute | solution.py:285
  34.3 2.6 %copy-start.4 = (s32[32,8]{0,1:T(8,128)S(1)}, s32[32,8]{0,1:T(8,128)}, u32[]{:S(2)}) copy-start(s32[32,8]{0,1:T(8,128)} %param.9) | copy-start | bytes 3076

commit v6 on v5

--- a/solution.py
+++ b/solution.py
@@ -329,17 +329,19 @@
     x1 = across(z1, along_x)
     x3 = across(z3, along_x)
     z2 = across(z3, near_z)
-    held = call(
-        hold_kernel,
-        [jax.ShapeDtypeStruct(w.shape, bf16) for w in (w_gate, w_up, w_down)],
-        x0,
-        w_gate,
-        w_up,
-        w_down,
-        in_specs=[VMEM] * 4,
-        out_specs=[VMEM] * 3,
-        moved=12 * feature_dim * hidden_w,
-    )
+
+    def hold(after_block, *weights):
+        return call(
+            hold_kernel,
+            [jax.ShapeDtypeStruct(w.shape, bf16) for w in weights],
+            after_block,
+            *weights,
+            in_specs=[VMEM] * (1 + len(weights)),
+            out_specs=[VMEM] * len(weights),
+            moved=4 * len(weights) * feature_dim * hidden_w,
+        )
+
+    held = hold(x0, w_gate, w_up) + hold(z3, w_down)
     part = jax.ShapeDtypeStruct((rows, feature_dim + LANES), bf16)
     pair = jax.ShapeDtypeStruct((2 * rows, feature_dim + LANES), bf16)
 

time: 38.1 us -> 37.8 us (level)
  local copies, waits for them, and re-layouts: 3.42 us -> 2.43 us
  waiting for transfers between devices: 4.11 us -> 4.89 us
    unnamed x10, local copies, waits for them, and re-layouts: 3.41 us -> 2.42 us
    ppermute x13, waiting for transfers between devices: 4.1 us -> 4.89 us  [across(): lax.ppermute(block, peers, [(i, i ^ mask) for i in range(lax.axis_size(pe...]
    pallas_call x6 -> x7, Pallas kernels: 8.07 us -> 8.03 us  [call(): pl.pallas_call(kernel, out_shape=out_shape, in_specs=in_specs, out_specs=...]
  transfers between devices with their start and end apart: 14 -> 14, of which waited for: 4 -> 5; matrix products, arithmetic and copies ran while one was open for 0% -> 0% of each run, Pallas kernels for 15% -> 15%
where the time goes in v6:
time: 37.8 us; the launch traced here: 37.6 us
  starting transfers between devices  21.4 us (57%)
  Pallas kernels  8.03 us (21%)
  waiting for transfers between devices  4.89 us (13%)
  local copies, waits for them, and re-layouts  2.43 us (6%)
  between operations  0.74 us (2%)
    ppermute x13, starting transfers between devices, across(): lax.ppermute(block, peers, [(i, i ^ mask) for i in range(lax.axis_size(pe...  21.4 us
    pallas_call x7, Pallas kernels, call(): pl.pallas_call(kernel, out_shape=out_shape, in_specs=in_specs, out_specs=...  8.03 us
    ppermute x13, waiting for transfers between devices, across(): lax.ppermute(block, peers, [(i, i ^ mask) for i in range(lax.axis_size(pe...  4.89 us
    unnamed x10, local copies, waits for them, and re-layouts  2.42 us
  transfers between devices with their start and end apart: 14, of which 5 were waited for; matrix products, arithmetic and copies ran while one was open for 0% of the time, Pallas kernels for 15%

profile of v6, /device:TPU:0, one launch (start us, length us, event | category | flops | bytes accessed | tf_op | source)
XLA Modules:
  0.0 37.6 jit_solution(16722194097926629475)
XLA Ops:
  0.6 1.6 %shard_map.102.refs_0_ = bf16[32,2176]{1,0:T(8,128)(2,1)} custom-call(bf16[32,1024]{1,0:T(8,128)(2,1)} %x_ref.1, bf16[32,1024]{1,0:T(8,128)(2,1)} %y_ref.1, s32[8,32]{1,0:T(8,128)} %bitcast.5, s32[8,32]{1,0:T(8,128)} %bitcast.7), custom_call_target="tpu_custom_call" | custom-call | bytes 262144 | tf_op jit(solution)/shard_map/pallas_call | solution.py:134
  2.3 5.1 %collective-permute-start = (bf16[32,2176]{1,0:T(8,128)(2,1)}, bf16[32,2176]{1,0:T(8,128)(2,1)S(1)}, u32[]{:S(2)}, u32[]{:S(2)}) collective-permute-start(bf16[32,2176]{1,0:T(8,128)(2,1)} %shard_map.102.refs_0_), channel_id=1, source_target_pairs={{0,12},{2,14},{4,8},{6,10},{8,4},{10,6},{12,0},{14,2},{1,13},{3,15... | collective-permute-start | bytes 417800 | tf_op jit(solution)/shard_map/ppermute | solution.py:285
  7.4 0.0 collective-permute-start.5
  7.4 1.5 %collective-permute-start.4 = (bf16[32,2176]{1,0:T(8,128)(2,1)}, bf16[32,2176]{1,0:T(8,128)(2,1)S(1)}, u32[]{:S(2)}, u32[]{:S(2)}) collective-permute-start(bf16[32,2176]{1,0:T(8,128)(2,1)} %shard_map.102.refs_0_), channel_id=1, source_target_pairs={{0,2},{2,0},{4,6},{6,4},{8,10},{10,8},{12,14},{14,12},{1,3},{3,1},... | collective-permute-start | bytes 417800 | tf_op jit(solution)/shard_map/ppermute | solution.py:285
  8.9 0.6 %collective-permute-start.2 = (bf16[32,2176]{1,0:T(8,128)(2,1)}, bf16[32,2176]{1,0:T(8,128)(2,1)S(1)}, u32[]{:S(2)}, u32[]{:S(2)}) collective-permute-start(bf16[32,2176]{1,0:T(8,128)(2,1)} %shard_map.102.refs_0_), channel_id=1, source_target_pairs={{0,10},{2,8},{4,14},{6,12},{8,2},{10,0},{12,6},{14,4},{1,11},{3,9}... | collective-permute-start | bytes 417800 | tf_op jit(solution)/shard_map/ppermute | solution.py:285
  9.5 2.7 %collective-permute-done.after_ref.refs_1_ = bf16[32,2176]{1,0:T(8,128)(2,1)S(1)} collective-permute-done((bf16[32,2176]{1,0:T(8,128)(2,1)}, bf16[32,2176]{1,0:T(8,128)(2,1)S(1)}, u32[]{:S(2)}, u32[]{:S(2)}) %collective-permute-start) | collective-permute-done | bytes 139296 | tf_op jit(solution)/shard_map/ppermute | solution.py:285
  12.2 1.7 %collective-permute-start.3 = (bf16[32,2176]{1,0:T(8,128)(2,1)S(1)}, bf16[32,2176]{1,0:T(8,128)(2,1)S(1)}, u32[]{:S(2)}, u32[]{:S(2)}) collective-permute-start(bf16[32,2176]{1,0:T(8,128)(2,1)S(1)} %collective-permute-done.after_ref.refs_1_), channel_id=1, source_target_pairs={{0,2},{2,0},{4,6},{6,4},{8,10},{10,8},{12,14},{14,12},{1,3},{3,1},... | collective-permute-start | bytes 417800 | tf_op jit(solution)/shard_map/ppermute | solution.py:285
  13.8 3.6 %collective-permute-start.1 = (bf16[32,2176]{1,0:T(8,128)(2,1)S(1)}, bf16[32,2176]{1,0:T(8,128)(2,1)S(1)}, u32[]{:S(2)}, u32[]{:S(2)}) collective-permute-start(bf16[32,2176]{1,0:T(8,128)(2,1)S(1)} %collective-permute-done.after_ref.refs_1_), channel_id=1, source_target_pairs={{0,4},{2,6},{4,0},{6,2},{8,12},{10,14},{12,8},{14,10},{1,5},{3,7},... | collective-permute-start | bytes 417800 | tf_op jit(solution)/shard_map/ppermute | solution.py:285
  17.5 0.0 collective-permute-done.5.refs_1_
  17.5 0.3 collective-permute-start.6
  17.8 0.1 pad_add_fusion.place_ref
  17.9 1.1 %copy-done = bf16[1,384,1024]{2,1,0:T(8,128)(2,1)S(1)} copy-done((bf16[1,384,1024]{2,1,0:T(8,128)(2,1)S(1)}, bf16[1,384,1024]{2,1,0:T(8,128)(2,1)}, u32[]{:S(2)}) %copy-start) | copy-done | bytes 786456
  19.0 0.1 shard_map.104.refs_6_
  19.1 0.0 collective-permute-done.4.after_ref.refs_3_
  19.1 1.0 %copy-done.1 = bf16[1,1024,384]{2,1,0:T(8,128)(2,1)S(1)} copy-done((bf16[1,1024,384]{2,1,0:T(8,128)(2,1)S(1)}, bf16[1,1024,384]{2,1,0:T(8,128)(2,1)}, u32[]{:S(2)}) %copy-start.1) | copy-done | bytes 786456
  20.2 0.2 copy-done.2
  20.4 0.2 shard_map.103
  20.6 0.2 collective-permute-done.1.refs_0_
  20.9 1.8 %shard_map.105 = (bf16[32,1152]{1,0:T(8,128)(2,1)S(1)}, bf16[32,1152]{1,0:T(8,128)(2,1)S(1)}, bf16[32,1152]{1,0:T(8,128)(2,1)S(1)}, bf16[32,1152]{1,0:T(8,128)(2...) custom-call(s32[2]{0:T(128)S(1)} %pad_add_fusion.place_ref, ...), custom_call_target="tpu_custom_call" | custom-call | flops 503316480 | bytes 3407872 | tf_op jit(solution)/shard_map/pallas_call | solution.py:134
  22.6 1.5 %collective-permute-start.7 = (bf16[32,1152]{1,0:T(8,128)(2,1)S(1)}, bf16[32,1152]{1,0:T(8,128)(2,1)S(1)}, u32[]{:S(2)}, u32[]{:S(2)}) collective-permute-start(bf16[32,1152]{1,0:T(8,128)(2,1)S(1)} %get-tuple-element.30), channel_id=1, source_target_pairs={{0,2},{2,0},{4,6},{6,4},{8,10},{10,8},{12,14},{14,12},{1,3},{3,1},... | collective-permute-start | bytes 221192 | tf_op jit(solution)/shard_map/ppermute | solution.py:285
  24.2 0.5 %collective-permute-start.12 = (bf16[32,1152]{1,0:T(8,128)(2,1)S(1)}, bf16[32,1152]{1,0:T(8,128)(2,1)S(1)}, u32[]{:S(2)}, u32[]{:S(2)}) collective-permute-start(bf16[32,1152]{1,0:T(8,128)(2,1)S(1)} %get-tuple-element.37), channel_id=1, source_target_pairs={{0,2},{2,0},{4,6},{6,4},{8,10},{10,8},{12,14},{14,12},{1,3},{3,1},... | collective-permute-start | bytes 221192 | tf_op jit(solution)/shard_map/ppermute | solution.py:285
  24.7 1.8 %shard_map.106 = (bf16[32,1152]{1,0:T(8,128)(2,1)S(1)}, bf16[64,1152]{1,0:T(8,128)(2,1)S(1)}, bf16[32,1152]{1,0:T(8,128)(2,1)S(1)}, bf16[256,1280]{1,0:T(8,128)(2,1)S(1)}, bf16[256,512]{1,0:T(8,128)(2,1)S(1)}) custom-call(s32[2]{0:T(128)S(1)} %pad_add_fusion.place_ref, bf16[128,1280]{1,0:T(8,128)(2,1)S(1)} %get-tuple-element.25.far_swap_ref, ...), custom_call_target="tpu_custom_call" | custom-call | flops 503316480 | bytes 3407872 | tf_op jit(solution)/shard_map/pallas_call | solution.py:134
  26.5 1.8 %collective-permute-start.9 = (bf16[64,1152]{1,0:T(8,128)(2,1)S(1)}, bf16[64,1152]{1,0:T(8,128)(2,1)S(1)}, u32[]{:S(2)}, u32[]{:S(2)}) collective-permute-start(bf16[64,1152]{1,0:T(8,128)(2,1)S(1)} %get-tuple-element.34), channel_id=1, source_target_pairs={{0,4},{2,6},{4,0},{6,2},{8,12},{10,14},{12,8},{14,10},{1,5},{3,7},... | collective-permute-start | bytes 442376 | tf_op jit(solution)/shard_map/ppermute | solution.py:285
  28.4 1.5 %collective-permute-start.11 = (bf16[32,1152]{1,0:T(8,128)(2,1)S(1)}, bf16[32,1152]{1,0:T(8,128)(2,1)S(1)}, u32[]{:S(2)}, u32[]{:S(2)}) collective-permute-start(bf16[32,1152]{1,0:T(8,128)(2,1)S(1)} %add_convert_fusion.2), channel_id=1, source_target_pairs={{0,8},{2,10},{4,12},{6,14},{8,0},{10,2},{12,4},{14,6},{1,9},{3,11}... | collective-permute-start | bytes 221192 | tf_op jit(solution)/shard_map/ppermute | solution.py:285
  29.9 1.4 %collective-permute-start.13 = (bf16[32,1152]{1,0:T(8,128)(2,1)S(1)}, bf16[32,1152]{1,0:T(8,128)(2,1)S(1)}, u32[]{:S(2)}, u32[]{:S(2)}) collective-permute-start(bf16[32,1152]{1,0:T(8,128)(2,1)S(1)} %add_convert_fusion), channel_id=1, source_target_pairs={{0,12},{2,14},{4,8},{6,10},{8,4},{10,6},{12,0},{14,2},{1,13},{3,15... | collective-permute-start | bytes 221192 | tf_op jit(solution)/shard_map/ppermute | solution.py:285
  31.4 1.0 %collective-permute-done.9 = bf16[64,1152]{1,0:T(8,128)(2,1)S(1)} collective-permute-done((bf16[64,1152]{1,0:T(8,128)(2,1)S(1)}, bf16[64,1152]{1,0:T(8,128)(2,1)S(1)}, u32[]{:S(2)}, u32[]{:S(2)}) %collective-permute-start.9) | collective-permute-done | bytes 147488 | tf_op jit(solution)/shard_map/ppermute | solution.py:285
  32.4 1.6 %collective-permute-start.10 = (bf16[32,1152]{1,0:T(8,128)(2,1)S(1)}, bf16[32,1152]{1,0:T(8,128)(2,1)S(1)}, u32[]{:S(2)}, u32[]{:S(2)}) collective-permute-start(bf16[32,1152]{1,0:T(8,128)(2,1)S(1)} %add_convert_fusion.1), channel_id=1, source_target_pairs={{0,2},{2,0},{4,6},{6,4},{8,10},{10,8},{12,14},{14,12},{1,3},{3,1},... | collective-permute-start | bytes 221192 | tf_op jit(solution)/shard_map/ppermute | solution.py:285
  34.0 0.0 copy-start.4
  34.0 1.8 %shard_map.107 = (f32[1,512,384]{2,1,0:T(8,128)}, f32[1,512,384]{2,1,0:T(8,128)}, f32[8,128]{1,0:T(8,128)S(1)}) custom-call(bf16[256,512]{1,0:T(8,128)(2,1)S(1)} %get-tuple-element.27.keep_ref, bf16[256,1280]{1,0:T(8,128)(2,1)S(1)} %get-tuple-element.31.own_ref, bf16[256,1280]{1,0:T(8,128)(2,1)S(1)} %collective-permute-done.8.other_ref), custom_call_target="tpu_custom_call" | custom-call | flops 402653184 | bytes 2228224 | tf_op jit(solution)/shard_map/pallas_call | solution.py:134
  35.7 0.8 %collective-permute-done.13.refs_4_ = bf16[32,1152]{1,0:T(8,128)(2,1)S(1)} collective-permute-done((bf16[32,1152]{1,0:T(8,128)(2,1)S(1)}, bf16[32,1152]{1,0:T(8,128)(2,1)S(1)}, u32[]{:S(2)}, u32[]{:S(2)}) %collective-permute-start.13) | collective-permute-done | bytes 73760 | tf_op jit(solution)/shard_map/ppermute | solution.py:285
  36.5 0.2 collective-permute-done.10.refs_2_
  36.8 0.8 %shard_map.108 = (bf16[32,1024]{1,0:T(8,128)(2,1)}, f32[8,32]{1,0:T(8,128)}) custom-call(s32[8,32]{1,0:T(8,128)S(1)} %bitcast.6, f32[8,128]{1,0:T(8,128)S(1)} %get-tuple-element.32.done_ref, bf16[32,1152]{1,0:T(8,128)(2,1)S(1)} %get-tuple-element.33.refs_0_, bf16[32,1152]{1,0:T(8,128)(2,1)S(1)} %slice.8.refs_1_, ...), custom_call_target="tpu_custom_call" | custom-call | bytes 393216 | tf_op jit(solution)/shard_map/pallas_call | solution.py:134
  (18 shorter events, 0.1 us)
Async XLA Ops:
  2.3 9.9 %collective-permute-start = (bf16[32,2176]{1,0:T(8,128)(2,1)}, bf16[32,2176]{1,0:T(8,128)(2,1)S(1)}, u32[]{:S(2)}, u32[]{:S(2)}) collective-permute-start(bf16[32,2176]{1,0:T(8,128)(2,1)} %shard_map.102.refs_0_), channel_id=1, source_target_pairs={{0,12},{2,14},{4,8},{6,10},{8,4},{10,6},{12,0},{14,2},{1,13},{3,15... | collective-permute-start | bytes 417800 | tf_op jit(solution)/shard_map/ppermute | solution.py:285
  7.4 10.1 %collective-permute-start.5 = (bf16[32,2176]{1,0:T(8,128)(2,1)}, bf16[32,2176]{1,0:T(8,128)(2,1)S(1)}, u32[]{:S(2)}, u32[]{:S(2)}) collective-permute-start(bf16[32,2176]{1,0:T(8,128)(2,1)} %shard_map.102.refs_0_), channel_id=1, source_target_pairs={{0,4},{2,6},{4,0},{6,2},{8,12},{10,14},{12,8},{14,10},{1,5},{3,7},... | collective-permute-start | bytes 417800 | tf_op jit(solution)/shard_map/ppermute | solution.py:285
  7.4 11.7 %collective-permute-start.4 = (bf16[32,2176]{1,0:T(8,128)(2,1)}, bf16[32,2176]{1,0:T(8,128)(2,1)S(1)}, u32[]{:S(2)}, u32[]{:S(2)}) collective-permute-start(bf16[32,2176]{1,0:T(8,128)(2,1)} %shard_map.102.refs_0_), channel_id=1, source_target_pairs={{0,2},{2,0},{4,6},{6,4},{8,10},{10,8},{12,14},{14,12},{1,3},{3,1},... | collective-permute-start | bytes 417800 | tf_op jit(solution)/shard_map/ppermute | solution.py:285
  8.9 11.7 %collective-permute-start.2 = (bf16[32,2176]{1,0:T(8,128)(2,1)}, bf16[32,2176]{1,0:T(8,128)(2,1)S(1)}, u32[]{:S(2)}, u32[]{:S(2)}) collective-permute-start(bf16[32,2176]{1,0:T(8,128)(2,1)} %shard_map.102.refs_0_), channel_id=1, source_target_pairs={{0,10},{2,8},{4,14},{6,12},{8,2},{10,0},{12,6},{14,4},{1,11},{3,9}... | collective-permute-start | bytes 417800 | tf_op jit(solution)/shard_map/ppermute | solution.py:285
  12.2 8.5 %collective-permute-start.3 = (bf16[32,2176]{1,0:T(8,128)(2,1)S(1)}, bf16[32,2176]{1,0:T(8,128)(2,1)S(1)}, u32[]{:S(2)}, u32[]{:S(2)}) collective-permute-start(bf16[32,2176]{1,0:T(8,128)(2,1)S(1)} %collective-permute-done.after_ref.refs_1_), channel_id=1, source_target_pairs={{0,2},{2,0},{4,6},{6,4},{8,10},{10,8},{12,14},{14,12},{1,3},{3,1},... | collective-permute-start | bytes 417800 | tf_op jit(solution)/shard_map/ppermute | solution.py:285
  13.8 7.0 %collective-permute-start.1 = (bf16[32,2176]{1,0:T(8,128)(2,1)S(1)}, bf16[32,2176]{1,0:T(8,128)(2,1)S(1)}, u32[]{:S(2)}, u32[]{:S(2)}) collective-permute-start(bf16[32,2176]{1,0:T(8,128)(2,1)S(1)} %collective-permute-done.after_ref.refs_1_), channel_id=1, source_target_pairs={{0,4},{2,6},{4,0},{6,2},{8,12},{10,14},{12,8},{14,10},{1,5},{3,7},... | collective-permute-start | bytes 417800 | tf_op jit(solution)/shard_map/ppermute | solution.py:285
  17.5 7.3 %collective-permute-start.6 = (bf16[32,2176]{1,0:T(8,128)(2,1)S(1)}, bf16[32,2176]{1,0:T(8,128)(2,1)S(1)}, u32[]{:S(2)}, u32[]{:S(2)}) collective-permute-start(bf16[32,2176]{1,0:T(8,128)(2,1)S(1)} %collective-permute-done.5.refs_1_), channel_id=1, source_target_pairs={{0,2},{2,0},{4,6},{6,4},{8,10},{10,8},{12,14},{14,12},{1,3},{3,1},... | collective-permute-start | bytes 417800 | tf_op jit(solution)/shard_map/ppermute | solution.py:285
  17.9 1.1 %copy-start = (bf16[1,384,1024]{2,1,0:T(8,128)(2,1)S(1)}, bf16[1,384,1024]{2,1,0:T(8,128)(2,1)}, u32[]{:S(2)}) copy-start(bf16[1,384,1024]{2,1,0:T(8,128)(2,1)} %refs_0_.3) | copy-start | bytes 2359300
  19.0 1.1 %copy-start.1 = (bf16[1,1024,384]{2,1,0:T(8,128)(2,1)S(1)}, bf16[1,1024,384]{2,1,0:T(8,128)(2,1)}, u32[]{:S(2)}) copy-start(bf16[1,1024,384]{2,1,0:T(8,128)(2,1)} %refs_0_.2) | copy-start | bytes 2359300
  19.0 1.4 %copy-start.2 = (bf16[1,1024,384]{2,1,0:T(8,128)(2,1)S(1)}, bf16[1,1024,384]{2,1,0:T(8,128)(2,1)}, u32[]{:S(2)}) copy-start(bf16[1,1024,384]{2,1,0:T(8,128)(2,1)} %refs_1_.1) | copy-start | bytes 2359300
  20.9 3.9 %copy-start.3 = (bf16[32,2176]{1,0:T(8,128)(2,1)S(1)}, bf16[32,2176]{1,0:T(8,128)(2,1)}, u32[]{:S(2)}) copy-start(bf16[32,2176]{1,0:T(8,128)(2,1)} %shard_map.102.refs_0_) | copy-start | bytes 417796
  22.6 5.7 %collective-permute-start.7 = (bf16[32,1152]{1,0:T(8,128)(2,1)S(1)}, bf16[32,1152]{1,0:T(8,128)(2,1)S(1)}, u32[]{:S(2)}, u32[]{:S(2)}) collective-permute-start(bf16[32,1152]{1,0:T(8,128)(2,1)S(1)} %get-tuple-element.30), channel_id=1, source_target_pairs={{0,2},{2,0},{4,6},{6,4},{8,10},{10,8},{12,14},{14,12},{1,3},{3,1},... | collective-permute-start | bytes 221192 | tf_op jit(solution)/shard_map/ppermute | solution.py:285
  24.2 5.7 %collective-permute-start.12 = (bf16[32,1152]{1,0:T(8,128)(2,1)S(1)}, bf16[32,1152]{1,0:T(8,128)(2,1)S(1)}, u32[]{:S(2)}, u32[]{:S(2)}) collective-permute-start(bf16[32,1152]{1,0:T(8,128)(2,1)S(1)} %get-tuple-element.37), channel_id=1, source_target_pairs={{0,2},{2,0},{4,6},{6,4},{8,10},{10,8},{12,14},{14,12},{1,3},{3,1},... | collective-permute-start | bytes 221192 | tf_op jit(solution)/shard_map/ppermute | solution.py:285
  26.5 5.8 %collective-permute-start.9 = (bf16[64,1152]{1,0:T(8,128)(2,1)S(1)}, bf16[64,1152]{1,0:T(8,128)(2,1)S(1)}, u32[]{:S(2)}, u32[]{:S(2)}) collective-permute-start(bf16[64,1152]{1,0:T(8,128)(2,1)S(1)} %get-tuple-element.34), channel_id=1, source_target_pairs={{0,4},{2,6},{4,0},{6,2},{8,12},{10,14},{12,8},{14,10},{1,5},{3,7},... | collective-permute-start | bytes 442376 | tf_op jit(solution)/shard_map/ppermute | solution.py:285
  28.4 7.4 %collective-permute-start.11 = (bf16[32,1152]{1,0:T(8,128)(2,1)S(1)}, bf16[32,1152]{1,0:T(8,128)(2,1)S(1)}, u32[]{:S(2)}, u32[]{:S(2)}) collective-permute-start(bf16[32,1152]{1,0:T(8,128)(2,1)S(1)} %add_convert_fusion.2), channel_id=1, source_target_pairs={{0,8},{2,10},{4,12},{6,14},{8,0},{10,2},{12,4},{14,6},{1,9},{3,11}... | collective-permute-start | bytes 221192 | tf_op jit(solution)/shard_map/ppermute | solution.py:285
  29.9 4.1 %collective-permute-start.8 = (bf16[256,1280]{1,0:T(8,128)(2,1)S(1)}, bf16[256,1280]{1,0:T(8,128)(2,1)S(1)}, u32[]{:S(2)}, u32[]{:S(2)}) collective-permute-start(bf16[256,1280]{1,0:T(8,128)(2,1)S(1)} %get-tuple-element.31.own_ref), channel_id=1, source_target_pairs={{0,1},{1,0},{2,3},{3,2},{4,5},{5,4},{6,7},{7,6},{8,9},{9,8},{10,11... | collective-permute-start | bytes 1966088 | tf_op jit(solution)/shard_map/ppermute | solution.py:289
  29.9 6.6 %collective-permute-start.13 = (bf16[32,1152]{1,0:T(8,128)(2,1)S(1)}, bf16[32,1152]{1,0:T(8,128)(2,1)S(1)}, u32[]{:S(2)}, u32[]{:S(2)}) collective-permute-start(bf16[32,1152]{1,0:T(8,128)(2,1)S(1)} %add_convert_fusion), channel_id=1, source_target_pairs={{0,12},{2,14},{4,8},{6,10},{8,4},{10,6},{12,0},{14,2},{1,13},{3,15... | collective-permute-start | bytes 221192 | tf_op jit(solution)/shard_map/ppermute | solution.py:285
  32.4 4.4 %collective-permute-start.10 = (bf16[32,1152]{1,0:T(8,128)(2,1)S(1)}, bf16[32,1152]{1,0:T(8,128)(2,1)S(1)}, u32[]{:S(2)}, u32[]{:S(2)}) collective-permute-start(bf16[32,1152]{1,0:T(8,128)(2,1)S(1)} %add_convert_fusion.1), channel_id=1, source_target_pairs={{0,2},{2,0},{4,6},{6,4},{8,10},{10,8},{12,14},{14,12},{1,3},{3,1},... | collective-permute-start | bytes 221192 | tf_op jit(solution)/shard_map/ppermute | solution.py:285
  34.0 2.8 %copy-start.4 = (s32[32,8]{0,1:T(8,128)S(1)}, s32[32,8]{0,1:T(8,128)}, u32[]{:S(2)}) copy-start(s32[32,8]{0,1:T(8,128)} %param.9) | copy-start | bytes 3076

commit v7 on v6

--- a/solution.py
+++ b/solution.py
@@ -179,12 +179,11 @@
     y_copy.wait()
 
 
-def expert_rows(place_ref, blocks, weight_refs, part_refs, swap_ref, keep_ref):
-    gate_ref, up_ref, down_ref = weight_refs
+def expert_rows(place_ref, blocks, weight_refs, part_refs, grad_ref):
+    pair_ref, down_ref = weight_refs
     rows, width = blocks[0].shape
     feature_dim = (width - LANES) // 2
-    half = feature_dim // 2
-    expert, replica = place_ref[0], place_ref[1]
+    expert = place_ref[0]
     data = jnp.concatenate([block[...] for block in blocks], axis=0)
     x_rows = data[:, :feature_dim]
     y_rows = data[:, feature_dim : 2 * feature_dim]
@@ -194,9 +193,10 @@
         axis=1,
         keepdims=True,
     )
-    gate, up = gate_ref[0], up_ref[0]
-    pre_gate = jnp.dot(x_rows, gate, preferred_element_type=jnp.float32)
-    pre_up = jnp.dot(x_rows, up, preferred_element_type=jnp.float32)
+    pair = pair_ref[0]
+    hidden_w = pair.shape[1] // 2
+    pre = jnp.dot(x_rows, pair, preferred_element_type=jnp.float32)
+    pre_gate, pre_up = pre[:, :hidden_w], pre[:, hidden_w:]
     back = lax.dot_general(y_rows, down_ref[0], NT, preferred_element_type=jnp.float32)
     sig = jax.nn.sigmoid(pre_gate)
     activated = pre_gate * sig
@@ -204,8 +204,8 @@
     scaled = mix * back
     d_gate = (scaled * pre_up * sig * (1.0 + pre_gate * (1.0 - sig))).astype(jnp.bfloat16)
     d_up = (scaled * activated).astype(jnp.bfloat16)
-    part = lax.dot_general(d_gate, gate, NT, preferred_element_type=jnp.float32)
-    part += lax.dot_general(d_up, up, NT, preferred_element_type=jnp.float32)
+    d_both = jnp.concatenate([d_gate, d_up], axis=1)
+    part = lax.dot_general(d_both, pair, NT, preferred_element_type=jnp.float32)
     part = part.astype(jnp.bfloat16)
     comb = jnp.where(lane == expert, pair_comb, 0.0).astype(jnp.bfloat16)
     first = 0
@@ -214,33 +214,40 @@
         out[:, :feature_dim] = part[first:last]
         out[:, feature_dim:] = comb[first:last]
         first = last
-    hidden_w = d_gate.shape[1]
-    low, high = x_rows[:, :half], x_rows[:, half:]
-    count = data.shape[0]
-    swap_ref[:count, :half] = jnp.where(replica == 0, high, low)
-    swap_ref[:count, half : half + hidden_w] = d_gate
-    swap_ref[:count, half + hidden_w :] = d_up
-    keep_ref[:count] = jnp.where(replica == 0, low, high)
+    grad_ref[: data.shape[0], grad_ref.shape[1] - 2 * hidden_w :] = d_both
 
 
 def far_kernel(place_ref, *refs):
-    expert_rows(place_ref, refs[:4], refs[4:7], refs[7:11], *refs[11:])
-
-
-def near_kernel(place_ref, far_swap_ref, far_keep_ref, *refs):
-    expert_rows(place_ref, refs[:4], refs[4:7], refs[7:10], *refs[10:])
-    first = refs[0].shape[0] * 4
-    refs[10][first:] = far_swap_ref[...]
-    refs[11][first:] = far_keep_ref[...]
+    expert_rows(place_ref, refs[:4], refs[4:6], refs[6:10], refs[10])
+
+
+def near_kernel(place_ref, far_grad_ref, *refs):
+    near, weights, far = refs[:4], refs[4:6], refs[6:10]
+    swap_ref, keep_ref = refs[13:]
+    expert_rows(place_ref, near, weights, refs[10:13], swap_ref)
+    rows, half = near[0].shape[0], keep_ref.shape[1]
+    swap_ref[4 * rows :, half:] = far_grad_ref[...]
+    first = place_ref[1] == 0
+    for index, block in enumerate((*near, *far)):
+        low, high = block[:, :half], block[:, half : 2 * half]
+        place = slice(index * rows, (index + 1) * rows)
+        swap_ref[place, :half] = jnp.where(first, high, low)
+        keep_ref[place] = jnp.where(first, low, high)
 
 
 def hold_kernel(after_ref, *refs):
-    count = len(refs) // 2
-    for source, target in zip(refs[:count], refs[count:]):
-        step = source.shape[1] // 8
-
-        @pl.loop(0, 8)
+    target = refs[-1]
+    steps = 8
+    for number, source in enumerate(refs[:-1]):
+        step, width = source.shape[1] // steps, source.shape[2]
+
+        @pl.loop(0, steps)
         def _(index):
+            rows = pl.ds(pl.multiple_of(index * step, step), step)
+            target[0, rows, number * width : (number + 1) * width] = source[0, rows]
+
+
+def _(index):
             part = pl.ds(pl.multiple_of(index * step, step), step)
             target[0, part] = source[0, part]
 
@@ -258,10 +265,7 @@
     up_ref[0] = total[:, hidden_w:]
 
 
-def finish_kernel(ids_hbm, done_ref, *refs):
-    *refs, ids_ref, ids_sem = refs
-    ids_copy = pltpu.make_async_copy(ids_hbm, ids_ref, ids_sem)
-    ids_copy.start()
+def finish_kernel(ids_ref, done_ref, *refs):
     token_ref, comb_ref = refs[-2:]
     rows, feature_dim = token_ref.shape
     total = refs[0][...].astype(jnp.float32)
@@ -272,7 +276,6 @@
     turned = lax.dot_general(
         one_hot_rows(LANES), comb, NT, preferred_element_type=jnp.float32
     )
-    ids_copy.wait()
     ids = ids_ref[...]
     out = jnp.zeros(ids.shape, jnp.float32)
     for expert in range(ids.shape[0]):
@@ -309,16 +312,19 @@
     place = jnp.stack([lax.axis_index(("expert", "seq")), lax.axis_index("replica")])
     place = place.astype(jnp.int32)
     ids_turned = expert_ids.T
-    own = call(
+    own, ids_held = call(
         message_kernel,
-        jax.ShapeDtypeStruct((rows, 2 * feature_dim + LANES), bf16),
+        [
+            jax.ShapeDtypeStruct((rows, 2 * feature_dim + LANES), bf16),
+            jax.ShapeDtypeStruct(ids_turned.shape, jnp.int32),
+        ],
         tokens,
         cotangent,
         ids_turned,
         combine_int.T,
         in_specs=[HBM] * 4,
-        out_specs=VMEM,
-        scratch=[pltpu.VMEM(ids_turned.shape, jnp.int32)] * 2 + [pltpu.SemaphoreType.DMA] * 4,
+        out_specs=[VMEM] * 2,
+        scratch=[pltpu.VMEM(ids_turned.shape, jnp.int32)] + [pltpu.SemaphoreType.DMA] * 4,
         moved=8 * rows * feature_dim,
         limit=VMEM_MOST,
     )
@@ -333,15 +339,15 @@
     def hold(after_block, *weights):
         return call(
             hold_kernel,
-            [jax.ShapeDtypeStruct(w.shape, bf16) for w in weights],
+            jax.ShapeDtypeStruct((*weights[0].shape[:2], len(weights) * weights[0].shape[2]), bf16),
             after_block,
             *weights,
             in_specs=[VMEM] * (1 + len(weights)),
-            out_specs=[VMEM] * len(weights),
+            out_specs=VMEM,
             moved=4 * len(weights) * feature_dim * hidden_w,
         )
 
-    held = hold(x0, w_gate, w_up) + hold(z3, w_down)
+    held = (hold(x0, w_gate, w_up), hold(z3, w_down))
     part = jax.ShapeDtypeStruct((rows, feature_dim + LANES), bf16)
     pair = jax.ShapeDtypeStruct((2 * rows, feature_dim + LANES), bf16)
 
@@ -357,24 +363,25 @@
             jax.ShapeDtypeStruct((blocks * rows, half), bf16),
         ]
 
-    f2, f3, g2, g3, *far = call(
+    f2, f3, g2, g3, far_grad = call(
         far_kernel,
-        [part] * 4 + exchanged(4),
+        [part] * 4 + [jax.ShapeDtypeStruct((4 * rows, 2 * hidden_w), bf16)],
         place,
         *(z2, z3, x2, x3),
         *held,
-        in_specs=[SMEM] + [VMEM] * 7,
-        out_specs=[VMEM] * 6,
+        in_specs=[SMEM] + [VMEM] * 6,
+        out_specs=[VMEM] * 5,
         **work(4),
     )
     f0, fg1, g0, swap, keep = call(
         near_kernel,
         [part, pair, part] + exchanged(8),
         place,
-        *far,
+        far_grad,
         *(own, z1, x1, x0),
         *held,
-        in_specs=[SMEM] + [VMEM] * 9,
+        *(z2, z3, x2, x3),
+        in_specs=[SMEM] + [VMEM] * 11,
         out_specs=[VMEM] * 5,
         **work(4),
     )
@@ -400,12 +407,11 @@
     token_grad, comb_turned = call(
         finish_kernel,
         (jax.ShapeDtypeStruct((rows, feature_dim), bf16), jax.ShapeDtypeStruct(ids_turned.shape, f32)),
-        ids_turned,
+        ids_held,
         weights_done,
         *(f0, r1[:rows], r0, r2, r3),
-        in_specs=[HBM] + [VMEM] * 6,
+        in_specs=[VMEM] * 7,
         out_specs=[pl.BlockSpec(tokens.shape), pl.BlockSpec(ids_turned.shape)],
-        scratch=[pltpu.VMEM(ids_turned.shape, jnp.int32), pltpu.SemaphoreType.DMA],
         moved=12 * rows * feature_dim,
     )
     return (token_grad, comb_turned.T, grad_gate, grad_up)

time: 37.8 us -> 37.7 us (level)
  no operation moved by 1% of the time
where the time goes in v7:
time: 37.7 us; the launch traced here: 37.4 us
  starting transfers between devices  21.4 us (57%)
  Pallas kernels  7.89 us (21%)
  waiting for transfers between devices  4.86 us (13%)
  local copies, waits for them, and re-layouts  2.43 us (6%)
  between operations  0.74 us (2%)
    ppermute x13, starting transfers between devices, across(): lax.ppermute(block, peers, [(i, i ^ mask) for i in range(lax.axis_size(pe...  21.4 us
    pallas_call x7, Pallas kernels, call(): pl.pallas_call(kernel, out_shape=out_shape, in_specs=in_specs, out_specs=...  7.89 us
    ppermute x13, waiting for transfers between devices, across(): lax.ppermute(block, peers, [(i, i ^ mask) for i in range(lax.axis_size(pe...  4.86 us
    unnamed x10, local copies, waits for them, and re-layouts  2.43 us
  transfers between devices with their start and end apart: 14, of which 5 were waited for; matrix products, arithmetic and copies ran while one was open for 0% of the time, Pallas kernels for 15%

profile of v7, /device:TPU:0, one launch (start us, length us, event | category | flops | bytes accessed | tf_op | source)
XLA Modules:
  0.0 37.4 jit_solution(4541586299894976961)
XLA Ops:
  0.6 1.6 %shard_map.102 = (bf16[32,2176]{1,0:T(8,128)(2,1)}, s32[8,32]{1,0:T(8,128)}) custom-call(bf16[32,1024]{1,0:T(8,128)(2,1)} %x_ref.1, bf16[32,1024]{1,0:T(8,128)(2,1)} %y_ref.1, s32[8,32]{1,0:T(8,128)} %bitcast.5, s32[8,32]{1,0:T(8,128)} %bitcast.6), custom_call_target="tpu_custom_call" | custom-call | bytes 262144 | tf_op jit(solution)/shard_map/pallas_call | solution.py:134
  2.3 5.1 %collective-permute-start = (bf16[32,2176]{1,0:T(8,128)(2,1)}, bf16[32,2176]{1,0:T(8,128)(2,1)S(1)}, u32[]{:S(2)}, u32[]{:S(2)}) collective-permute-start(bf16[32,2176]{1,0:T(8,128)(2,1)} %get-tuple-element.23.refs_0_), channel_id=1, source_target_pairs={{0,12},{2,14},{4,8},{6,10},{8,4},{10,6},{12,0},{14,2},{1,13},{3,15... | collective-permute-start | bytes 417800 | tf_op jit(solution)/shard_map/ppermute | solution.py:288
  7.4 0.0 collective-permute-start.5
  7.4 1.5 %collective-permute-start.4 = (bf16[32,2176]{1,0:T(8,128)(2,1)}, bf16[32,2176]{1,0:T(8,128)(2,1)S(1)}, u32[]{:S(2)}, u32[]{:S(2)}) collective-permute-start(bf16[32,2176]{1,0:T(8,128)(2,1)} %get-tuple-element.23.refs_0_), channel_id=1, source_target_pairs={{0,2},{2,0},{4,6},{6,4},{8,10},{10,8},{12,14},{14,12},{1,3},{3,1},... | collective-permute-start | bytes 417800 | tf_op jit(solution)/shard_map/ppermute | solution.py:288
  8.9 0.6 %collective-permute-start.2 = (bf16[32,2176]{1,0:T(8,128)(2,1)}, bf16[32,2176]{1,0:T(8,128)(2,1)S(1)}, u32[]{:S(2)}, u32[]{:S(2)}) collective-permute-start(bf16[32,2176]{1,0:T(8,128)(2,1)} %get-tuple-element.23.refs_0_), channel_id=1, source_target_pairs={{0,10},{2,8},{4,14},{6,12},{8,2},{10,0},{12,6},{14,4},{1,11},{3,9}... | collective-permute-start | bytes 417800 | tf_op jit(solution)/shard_map/ppermute | solution.py:288
  9.5 2.7 %collective-permute-done.after_ref.refs_1_.refs_7_ = bf16[32,2176]{1,0:T(8,128)(2,1)S(1)} collective-permute-done((bf16[32,2176]{1,0:T(8,128)(2,1)}, bf16[32,2176]{1,0:T(8,128)(2,1)S(1)}, u32[]{:S(2)}, u32[]{:S(2)}) %collective-permute-start) | collective-permute-done | bytes 139296 | tf_op jit(solution)/shard_map/ppermute | solution.py:288
  12.2 1.7 %collective-permute-start.3 = (bf16[32,2176]{1,0:T(8,128)(2,1)S(1)}, bf16[32,2176]{1,0:T(8,128)(2,1)S(1)}, u32[]{:S(2)}, u32[]{:S(2)}) collective-permute-start(bf16[32,2176]{1,0:T(8,128)(2,1)S(1)} %collective-permute-done.after_ref.refs_1_.refs_7_), channel_id=1, source_target_pairs={{0,2},{2,0},{4,6},{6,4},{8,10},{10,8},{12,14},{14,12},{1,3},{3,1},... | collective-permute-start | bytes 417800 | tf_op jit(solution)/shard_map/ppermute | solution.py:288
  13.9 3.6 %collective-permute-start.1 = (bf16[32,2176]{1,0:T(8,128)(2,1)S(1)}, bf16[32,2176]{1,0:T(8,128)(2,1)S(1)}, u32[]{:S(2)}, u32[]{:S(2)}) collective-permute-start(bf16[32,2176]{1,0:T(8,128)(2,1)S(1)} %collective-permute-done.after_ref.refs_1_.refs_7_), channel_id=1, source_target_pairs={{0,4},{2,6},{4,0},{6,2},{8,12},{10,14},{12,8},{14,10},{1,5},{3,7},... | collective-permute-start | bytes 417800 | tf_op jit(solution)/shard_map/ppermute | solution.py:288
  17.5 0.0 collective-permute-done.5.refs_1_
  17.5 0.3 collective-permute-start.6
  17.8 0.1 pad_add_fusion.place_ref
  17.9 1.1 %copy-done = bf16[1,384,1024]{2,1,0:T(8,128)(2,1)S(1)} copy-done((bf16[1,384,1024]{2,1,0:T(8,128)(2,1)S(1)}, bf16[1,384,1024]{2,1,0:T(8,128)(2,1)}, u32[]{:S(2)}) %copy-start) | copy-done | bytes 786456
  19.0 0.1 shard_map.104.refs_5_
  19.1 1.0 %copy-done.1 = bf16[1,1024,384]{2,1,0:T(8,128)(2,1)S(1)} copy-done((bf16[1,1024,384]{2,1,0:T(8,128)(2,1)S(1)}, bf16[1,1024,384]{2,1,0:T(8,128)(2,1)}, u32[]{:S(2)}) %copy-start.1) | copy-done | bytes 786456
  20.2 0.2 copy-done.2
  20.4 0.2 shard_map.103.refs_4_
  20.6 0.0 copy-start.3
  20.7 0.2 collective-permute-done.1.refs_0_.refs_6_
  20.9 1.7 %shard_map.105 = (bf16[32,1152]{1,0:T(8,128)(2,1)S(1)}, bf16[32,1152]{1,0:T(8,128)(2,1)S(1)}, bf16[32,1152]{1,0:T(8,128)(2,1)S(1)}, bf16[32,1152]{1,0:T(8,128)(2,1)S(1)}, bf16[128,768]{1,0:T(8,128)(2,1)S(1)}) custom-call(s32[2]{0:T(128)S(1)} %pad_add_fusion.place_ref, bf16[32,2176]{1,0:T(8,128)(2,1)S(1)} %collective-permute-done.1.refs_0_.refs_6_, ...), custom_call_target="tpu_custom_call" | custom-call | flops 503316480 | bytes 3407872 | tf_op jit(solution)/shard_map/pallas_call | solution.py:134
  22.6 1.6 %collective-permute-start.7 = (bf16[32,1152]{1,0:T(8,128)(2,1)S(1)}, bf16[32,1152]{1,0:T(8,128)(2,1)S(1)}, u32[]{:S(2)}, u32[]{:S(2)}) collective-permute-start(bf16[32,1152]{1,0:T(8,128)(2,1)S(1)} %get-tuple-element.28), channel_id=1, source_target_pairs={{0,2},{2,0},{4,6},{6,4},{8,10},{10,8},{12,14},{14,12},{1,3},{3,1},... | collective-permute-start | bytes 221192 | tf_op jit(solution)/shard_map/ppermute | solution.py:288
  24.2 0.5 %collective-permute-start.12 = (bf16[32,1152]{1,0:T(8,128)(2,1)S(1)}, bf16[32,1152]{1,0:T(8,128)(2,1)S(1)}, u32[]{:S(2)}, u32[]{:S(2)}) collective-permute-start(bf16[32,1152]{1,0:T(8,128)(2,1)S(1)} %get-tuple-element.35), channel_id=1, source_target_pairs={{0,2},{2,0},{4,6},{6,4},{8,10},{10,8},{12,14},{14,12},{1,3},{3,1},... | collective-permute-start | bytes 221192 | tf_op jit(solution)/shard_map/ppermute | solution.py:288
  24.7 1.7 %shard_map.106 = (bf16[32,1152]{1,0:T(8,128)(2,1)S(1)}, bf16[64,1152]{1,0:T(8,128)(2,1)S(1)}, bf16[32,1152]{1,0:T(8,128)(2,1)S(1)}, bf16[256,1280]{1,0:T(8,128)(2,1)S(1)}, bf16[256,512]{1,0:T(8,128)(2,1)S(1)}) custom-call(s32[2]{0:T(128)S(1)} %pad_add_fusion.place_ref, bf16[128,768]{1,0:T(8,128)(2,1)S(1)} %get-tuple-element.24.far_grad_ref, ...), custom_call_target="tpu_custom_call" | custom-call | flops 503316480 | bytes 3407872 | tf_op jit(solution)/shard_map/pallas_call | solution.py:134
  26.4 0.0 copy-start.4
  26.5 1.8 %collective-permute-start.9 = (bf16[64,1152]{1,0:T(8,128)(2,1)S(1)}, bf16[64,1152]{1,0:T(8,128)(2,1)S(1)}, u32[]{:S(2)}, u32[]{:S(2)}) collective-permute-start(bf16[64,1152]{1,0:T(8,128)(2,1)S(1)} %get-tuple-element.32), channel_id=1, source_target_pairs={{0,4},{2,6},{4,0},{6,2},{8,12},{10,14},{12,8},{14,10},{1,5},{3,7},... | collective-permute-start | bytes 442376 | tf_op jit(solution)/shard_map/ppermute | solution.py:288
  28.3 1.5 %collective-permute-start.11 = (bf16[32,1152]{1,0:T(8,128)(2,1)S(1)}, bf16[32,1152]{1,0:T(8,128)(2,1)S(1)}, u32[]{:S(2)}, u32[]{:S(2)}) collective-permute-start(bf16[32,1152]{1,0:T(8,128)(2,1)S(1)} %add_convert_fusion.2), channel_id=1, source_target_pairs={{0,8},{2,10},{4,12},{6,14},{8,0},{10,2},{12,4},{14,6},{1,9},{3,11}... | collective-permute-start | bytes 221192 | tf_op jit(solution)/shard_map/ppermute | solution.py:288
  29.9 1.5 %collective-permute-start.13 = (bf16[32,1152]{1,0:T(8,128)(2,1)S(1)}, bf16[32,1152]{1,0:T(8,128)(2,1)S(1)}, u32[]{:S(2)}, u32[]{:S(2)}) collective-permute-start(bf16[32,1152]{1,0:T(8,128)(2,1)S(1)} %add_convert_fusion), channel_id=1, source_target_pairs={{0,12},{2,14},{4,8},{6,10},{8,4},{10,6},{12,0},{14,2},{1,13},{3,15... | collective-permute-start | bytes 221192 | tf_op jit(solution)/shard_map/ppermute | solution.py:288
  31.3 0.9 %collective-permute-done.9 = bf16[64,1152]{1,0:T(8,128)(2,1)S(1)} collective-permute-done((bf16[64,1152]{1,0:T(8,128)(2,1)S(1)}, bf16[64,1152]{1,0:T(8,128)(2,1)S(1)}, u32[]{:S(2)}, u32[]{:S(2)}) %collective-permute-start.9) | collective-permute-done | bytes 147488 | tf_op jit(solution)/shard_map/ppermute | solution.py:288
  32.3 1.6 %collective-permute-start.10 = (bf16[32,1152]{1,0:T(8,128)(2,1)S(1)}, bf16[32,1152]{1,0:T(8,128)(2,1)S(1)}, u32[]{:S(2)}, u32[]{:S(2)}) collective-permute-start(bf16[32,1152]{1,0:T(8,128)(2,1)S(1)} %add_convert_fusion.1), channel_id=1, source_target_pairs={{0,2},{2,0},{4,6},{6,4},{8,10},{10,8},{12,14},{14,12},{1,3},{3,1},... | collective-permute-start | bytes 221192 | tf_op jit(solution)/shard_map/ppermute | solution.py:288
  33.9 1.8 %shard_map.107 = (f32[1,512,384]{2,1,0:T(8,128)}, f32[1,512,384]{2,1,0:T(8,128)}, f32[8,128]{1,0:T(8,128)S(1)}) custom-call(bf16[256,512]{1,0:T(8,128)(2,1)S(1)} %get-tuple-element.25.keep_ref, bf16[256,1280]{1,0:T(8,128)(2,1)S(1)} %get-tuple-element.29.own_ref, bf16[256,1280]{1,0:T(8,128)(2,1)S(1)} %collective-permute-done.8.other_ref), custom_call_target="tpu_custom_call" | custom-call | flops 402653184 | bytes 2228224 | tf_op jit(solution)/shard_map/pallas_call | solution.py:134
  35.7 0.8 %collective-permute-done.13.refs_4_ = bf16[32,1152]{1,0:T(8,128)(2,1)S(1)} collective-permute-done((bf16[32,1152]{1,0:T(8,128)(2,1)S(1)}, bf16[32,1152]{1,0:T(8,128)(2,1)S(1)}, u32[]{:S(2)}, u32[]{:S(2)}) %collective-permute-start.13) | collective-permute-done | bytes 73760 | tf_op jit(solution)/shard_map/ppermute | solution.py:288
  36.5 0.2 collective-permute-done.10.refs_2_
  36.7 0.7 %shard_map.108 = (bf16[32,1024]{1,0:T(8,128)(2,1)}, f32[8,32]{1,0:T(8,128)}) custom-call(s32[8,32]{1,0:T(8,128)S(1)} %copy-done.4, f32[8,128]{1,0:T(8,128)S(1)} %get-tuple-element.30.done_ref, bf16[32,1152]{1,0:T(8,128)(2,1)S(1)} %get-tuple-element.31.refs_0_, bf16[32,1152]{1,0:T(8,128)(2,1)S(1)} %slice.8.refs_1_, ...), custom_call_target="tpu_custom_call" | custom-call | bytes 393216 | tf_op jit(solution)/shard_map/pallas_call | solution.py:134
  (18 shorter events, 0.1 us)
Async XLA Ops:
  2.3 9.9 %collective-permute-start = (bf16[32,2176]{1,0:T(8,128)(2,1)}, bf16[32,2176]{1,0:T(8,128)(2,1)S(1)}, u32[]{:S(2)}, u32[]{:S(2)}) collective-permute-start(bf16[32,2176]{1,0:T(8,128)(2,1)} %get-tuple-element.23.refs_0_), channel_id=1, source_target_pairs={{0,12},{2,14},{4,8},{6,10},{8,4},{10,6},{12,0},{14,2},{1,13},{3,15... | collective-permute-start | bytes 417800 | tf_op jit(solution)/shard_map/ppermute | solution.py:288
  7.4 10.1 %collective-permute-start.5 = (bf16[32,2176]{1,0:T(8,128)(2,1)}, bf16[32,2176]{1,0:T(8,128)(2,1)S(1)}, u32[]{:S(2)}, u32[]{:S(2)}) collective-permute-start(bf16[32,2176]{1,0:T(8,128)(2,1)} %get-tuple-element.23.refs_0_), channel_id=1, source_target_pairs={{0,4},{2,6},{4,0},{6,2},{8,12},{10,14},{12,8},{14,10},{1,5},{3,7},... | collective-permute-start | bytes 417800 | tf_op jit(solution)/shard_map/ppermute | solution.py:288
  7.4 11.7 %collective-permute-start.4 = (bf16[32,2176]{1,0:T(8,128)(2,1)}, bf16[32,2176]{1,0:T(8,128)(2,1)S(1)}, u32[]{:S(2)}, u32[]{:S(2)}) collective-permute-start(bf16[32,2176]{1,0:T(8,128)(2,1)} %get-tuple-element.23.refs_0_), channel_id=1, source_target_pairs={{0,2},{2,0},{4,6},{6,4},{8,10},{10,8},{12,14},{14,12},{1,3},{3,1},... | collective-permute-start | bytes 417800 | tf_op jit(solution)/shard_map/ppermute | solution.py:288
  8.9 11.7 %collective-permute-start.2 = (bf16[32,2176]{1,0:T(8,128)(2,1)}, bf16[32,2176]{1,0:T(8,128)(2,1)S(1)}, u32[]{:S(2)}, u32[]{:S(2)}) collective-permute-start(bf16[32,2176]{1,0:T(8,128)(2,1)} %get-tuple-element.23.refs_0_), channel_id=1, source_target_pairs={{0,10},{2,8},{4,14},{6,12},{8,2},{10,0},{12,6},{14,4},{1,11},{3,9}... | collective-permute-start | bytes 417800 | tf_op jit(solution)/shard_map/ppermute | solution.py:288
  12.2 8.5 %collective-permute-start.3 = (bf16[32,2176]{1,0:T(8,128)(2,1)S(1)}, bf16[32,2176]{1,0:T(8,128)(2,1)S(1)}, u32[]{:S(2)}, u32[]{:S(2)}) collective-permute-start(bf16[32,2176]{1,0:T(8,128)(2,1)S(1)} %collective-permute-done.after_ref.refs_1_.refs_7_), channel_id=1, source_target_pairs={{0,2},{2,0},{4,6},{6,4},{8,10},{10,8},{12,14},{14,12},{1,3},{3,1},... | collective-permute-start | bytes 417800 | tf_op jit(solution)/shard_map/ppermute | solution.py:288
  13.9 7.0 %collective-permute-start.1 = (bf16[32,2176]{1,0:T(8,128)(2,1)S(1)}, bf16[32,2176]{1,0:T(8,128)(2,1)S(1)}, u32[]{:S(2)}, u32[]{:S(2)}) collective-permute-start(bf16[32,2176]{1,0:T(8,128)(2,1)S(1)} %collective-permute-done.after_ref.refs_1_.refs_7_), channel_id=1, source_target_pairs={{0,4},{2,6},{4,0},{6,2},{8,12},{10,14},{12,8},{14,10},{1,5},{3,7},... | collective-permute-start | bytes 417800 | tf_op jit(solution)/shard_map/ppermute | solution.py:288
  17.5 7.2 %collective-permute-start.6 = (bf16[32,2176]{1,0:T(8,128)(2,1)S(1)}, bf16[32,2176]{1,0:T(8,128)(2,1)S(1)}, u32[]{:S(2)}, u32[]{:S(2)}) collective-permute-start(bf16[32,2176]{1,0:T(8,128)(2,1)S(1)} %collective-permute-done.5.refs_1_), channel_id=1, source_target_pairs={{0,2},{2,0},{4,6},{6,4},{8,10},{10,8},{12,14},{14,12},{1,3},{3,1},... | collective-permute-start | bytes 417800 | tf_op jit(solution)/shard_map/ppermute | solution.py:288
  17.9 1.1 %copy-start = (bf16[1,384,1024]{2,1,0:T(8,128)(2,1)S(1)}, bf16[1,384,1024]{2,1,0:T(8,128)(2,1)}, u32[]{:S(2)}) copy-start(bf16[1,384,1024]{2,1,0:T(8,128)(2,1)} %refs_0_.3) | copy-start | bytes 2359300
  19.0 1.1 %copy-start.1 = (bf16[1,1024,384]{2,1,0:T(8,128)(2,1)S(1)}, bf16[1,1024,384]{2,1,0:T(8,128)(2,1)}, u32[]{:S(2)}) copy-start(bf16[1,1024,384]{2,1,0:T(8,128)(2,1)} %refs_0_.2) | copy-start | bytes 2359300
  19.0 1.4 %copy-start.2 = (bf16[1,1024,384]{2,1,0:T(8,128)(2,1)S(1)}, bf16[1,1024,384]{2,1,0:T(8,128)(2,1)}, u32[]{:S(2)}) copy-start(bf16[1,1024,384]{2,1,0:T(8,128)(2,1)} %refs_1_.1) | copy-start | bytes 2359300
  20.6 4.1 %copy-start.3 = (bf16[32,2176]{1,0:T(8,128)(2,1)S(1)}, bf16[32,2176]{1,0:T(8,128)(2,1)}, u32[]{:S(2)}) copy-start(bf16[32,2176]{1,0:T(8,128)(2,1)} %get-tuple-element.23.refs_0_) | copy-start | bytes 417796
  22.6 5.7 %collective-permute-start.7 = (bf16[32,1152]{1,0:T(8,128)(2,1)S(1)}, bf16[32,1152]{1,0:T(8,128)(2,1)S(1)}, u32[]{:S(2)}, u32[]{:S(2)}) collective-permute-start(bf16[32,1152]{1,0:T(8,128)(2,1)S(1)} %get-tuple-element.28), channel_id=1, source_target_pairs={{0,2},{2,0},{4,6},{6,4},{8,10},{10,8},{12,14},{14,12},{1,3},{3,1},... | collective-permute-start | bytes 221192 | tf_op jit(solution)/shard_map/ppermute | solution.py:288
  24.2 5.7 %collective-permute-start.12 = (bf16[32,1152]{1,0:T(8,128)(2,1)S(1)}, bf16[32,1152]{1,0:T(8,128)(2,1)S(1)}, u32[]{:S(2)}, u32[]{:S(2)}) collective-permute-start(bf16[32,1152]{1,0:T(8,128)(2,1)S(1)} %get-tuple-element.35), channel_id=1, source_target_pairs={{0,2},{2,0},{4,6},{6,4},{8,10},{10,8},{12,14},{14,12},{1,3},{3,1},... | collective-permute-start | bytes 221192 | tf_op jit(solution)/shard_map/ppermute | solution.py:288
  26.4 10.3 %copy-start.4 = (s32[8,32]{1,0:T(8,128)S(1)}, s32[8,32]{1,0:T(8,128)}, u32[]{:S(2)}) copy-start(s32[8,32]{1,0:T(8,128)} %get-tuple-element.22.ids_ref) | copy-start | bytes 3076
  26.5 5.8 %collective-permute-start.9 = (bf16[64,1152]{1,0:T(8,128)(2,1)S(1)}, bf16[64,1152]{1,0:T(8,128)(2,1)S(1)}, u32[]{:S(2)}, u32[]{:S(2)}) collective-permute-start(bf16[64,1152]{1,0:T(8,128)(2,1)S(1)} %get-tuple-element.32), channel_id=1, source_target_pairs={{0,4},{2,6},{4,0},{6,2},{8,12},{10,14},{12,8},{14,10},{1,5},{3,7},... | collective-permute-start | bytes 442376 | tf_op jit(solution)/shard_map/ppermute | solution.py:288
  28.3 7.4 %collective-permute-start.11 = (bf16[32,1152]{1,0:T(8,128)(2,1)S(1)}, bf16[32,1152]{1,0:T(8,128)(2,1)S(1)}, u32[]{:S(2)}, u32[]{:S(2)}) collective-permute-start(bf16[32,1152]{1,0:T(8,128)(2,1)S(1)} %add_convert_fusion.2), channel_id=1, source_target_pairs={{0,8},{2,10},{4,12},{6,14},{8,0},{10,2},{12,4},{14,6},{1,9},{3,11}... | collective-permute-start | bytes 221192 | tf_op jit(solution)/shard_map/ppermute | solution.py:288
  29.8 4.1 %collective-permute-start.8 = (bf16[256,1280]{1,0:T(8,128)(2,1)S(1)}, bf16[256,1280]{1,0:T(8,128)(2,1)S(1)}, u32[]{:S(2)}, u32[]{:S(2)}) collective-permute-start(bf16[256,1280]{1,0:T(8,128)(2,1)S(1)} %get-tuple-element.29.own_ref), channel_id=1, source_target_pairs={{0,1},{1,0},{2,3},{3,2},{4,5},{5,4},{6,7},{7,6},{8,9},{9,8},{10,11... | collective-permute-start | bytes 1966088 | tf_op jit(solution)/shard_map/ppermute | solution.py:292
  29.9 6.6 %collective-permute-start.13 = (bf16[32,1152]{1,0:T(8,128)(2,1)S(1)}, bf16[32,1152]{1,0:T(8,128)(2,1)S(1)}, u32[]{:S(2)}, u32[]{:S(2)}) collective-permute-start(bf16[32,1152]{1,0:T(8,128)(2,1)S(1)} %add_convert_fusion), channel_id=1, source_target_pairs={{0,12},{2,14},{4,8},{6,10},{8,4},{10,6},{12,0},{14,2},{1,13},{3,15... | collective-permute-start | bytes 221192 | tf_op jit(solution)/shard_map/ppermute | solution.py:288
  32.3 4.4 %collective-permute-start.10 = (bf16[32,1152]{1,0:T(8,128)(2,1)S(1)}, bf16[32,1152]{1,0:T(8,128)(2,1)S(1)}, u32[]{:S(2)}, u32[]{:S(2)}) collective-permute-start(bf16[32,1152]{1,0:T(8,128)(2,1)S(1)} %add_convert_fusion.1), channel_id=1, source_target_pairs={{0,2},{2,0},{4,6},{6,4},{8,10},{10,8},{12,14},{14,12},{1,3},{3,1},... | collective-permute-start | bytes 221192 | tf_op jit(solution)/shard_map/ppermute | solution.py:288
